TPU v7x, 256 devices: a whole 4x4x8 slice. The times are simulated.
256 devices in a mesh: district: 16 (over x, z_hi), tile: 16 (over z_lo, y, core).
Axes of the slice: x: 4, y: 4, z: 8 (z_hi: 4, z_lo: 2; z = z_hi * 2 + z_lo), core: 2. Of those that a mesh axis runs over, the one named last changes fastest.
Arguments:
- parent_state: float32 [3, 256, 2048], P(None, 'district', 'tile'), may hold values from -6 to 6
- parent_depth: float32 [256, 2048], P('district', 'tile'), may hold values from 0.25 to 1
- child_state: float32 [3, 1024, 2048], P(None, 'district', 'tile'), may hold values from -6 to 6
- child_depth: float32 [1024, 2048], P('district', 'tile'), may hold values from 0.1 to 1
- child_wet: int32 [4, 1024, 2048], P(None, 'district', 'tile'), may hold values 0 or 1
- interior_state: float32 [3, 16384, 128], P(None, ('district', 'tile')), may hold values from -6 to 6
- interior_wet: int32 [4, 16384, 128], P(None, ('district', 'tile')), may hold values 0 or 1
- parent_anchor: int32 [16, 16, 2], P('district'), may hold values from 0 to 2044, as said below
- open_row: int32 [16384], P(('district', 'tile')), may hold values from 0 to 63
- open_col: int32 [16384], P(('district', 'tile')), may hold values from 0 to 96
- open_owner: int32 [16384, 1], P(('district', 'tile')), may hold values from 0 to 15; in each aligned block of 64 rows (0 to 63, 64 to 127, ...) at most 8 rows name the same one
- open_valid: int32 [16384], P(('district', 'tile')), may hold values 0 or 1
- open_conduct: float32 [16384], P(('district', 'tile')), may hold values from 0.1 to 0.5
- door_rows: int32 [256, 128], P(('district', 'tile')), may hold values from 0 to 63
Outputs:
- parent_final: float32 [3, 256, 2048], P(None, 'district', 'tile')
- child_final: float32 [3, 1024, 2048], P(None, 'district', 'tile')
- interior_final: float32 [3, 16384, 128], P(None, ('district', 'tile'))
Inputs may be any that keep to these rules, and one draw needn't show every extreme that they name: `open_owner`: tile indices within the opening's own district group; among the rows of one device no owner is named by more than 8 rows, padded ones included. `parent_anchor`: entry 0 is the same for all tiles of a district and leaves room for 2 rows within the district's 16 parent rows; entry 1 rises by 4 from one tile to the next and every window lies within the parent grid's columns; district 0's windows start at column 0 and the last district's end at the grid's last column.
All inputs are finite; a program needn't handle non-finite values. No bound on the sum of `child_wet` or of `interior_wet` or of `open_valid` on one device may be relied on, other than what follows from the above.
Results may differ from a plain program's by a relative error of at most 0.0003.
Values sent between devices are 32-bit elements; how exact they have to be, the bound alone decides.
No kernel may reach another device: no remote copies, remote signals or barrier semaphores. Data moves between devices by JAX's collectives and lax.ppermute only.
A program may use at most 64 MiB of HBM per device.

v0:
```python
import jax
import jax.numpy as jnp
from jax import lax
from jax.sharding import PartitionSpec as P

CX = 64
CY = 128
IY = 128
R = 32
STEPS = 4
CAP = 8
SEG = 32
WX = 2
WY = 4


courant = 0.3
nudging = 0.25
area_ratio = 0.0625


def padded_2(cells, sides, width):
    for axis, dim in sides:
        count = lax.axis_size(axis)
        ends = count - 1
        head = lax.slice_in_dim(cells, 0, width, axis=dim)
        tail = lax.slice_in_dim(cells, cells.shape[dim] - width, cells.shape[dim], axis=dim)
        cells = jnp.concatenate(
            [
                lax.ppermute(tail, axis, [(i, (i + 1) % count) for i in range(ends)]),
                cells,
                lax.ppermute(head, axis, [((i + 1) % count, i) for i in range(ends)]),
            ],
            axis=dim,
        )
    return cells


def advance(padded, wet_cells):
    surface = padded[0]
    east_flow = padded[1]
    north_flow = padded[2]
    wet_depth = padded[3]
    new_east = east_flow[1:-1, 2:-2] - courant * (surface[2:, 2:-2] - surface[:-2, 2:-2])
    new_north = north_flow[2:-2, 1:-1] - courant * (surface[2:-2, 2:] - surface[2:-2, :-2])
    flux_east = wet_depth[1:-1, 2:-2] * new_east
    flux_north = wet_depth[2:-2, 1:-1] * new_north
    new_surface = surface[2:-2, 2:-2] - courant * (
        flux_east[2:] - flux_east[:-2] + flux_north[:, 2:] - flux_north[:, :-2]
    )
    return (new_surface, wet_cells * new_east[1:-1], wet_cells * new_north[:, 1:-1])


def room_step(state, wet_cells):
    padded = jnp.pad(jnp.concatenate([state, wet_cells[None]], 0), ((0, 0), (2, 2), (2, 2)))
    return jnp.stack(advance(padded, wet_cells))


def ranks(owners, tile_count):
    matches = (owners[:, None] == jnp.arange(tile_count, dtype=jnp.int32)[None, :]).astype(
        jnp.int32
    )
    return jnp.sum(jnp.cumsum(matches, 0) * matches, 1) - 1


def place_rows(values, owners, slot_of, tile_count):
    empty = jnp.zeros((tile_count, CAP) + values.shape[1:], values.dtype)
    return empty.at[owners, slot_of].set(values)


def opening_flow(street, weights, face_rows):
    inflow = weights[..., None] * (jnp.repeat(street, 4, axis=-1) - face_rows)
    grouped = inflow.reshape(inflow.shape[:-1] + (inflow.shape[-1] // 4, 4))
    return (inflow, jnp.sum(grouped, -1) * area_ratio)


def absorb(surface, room_rows, street, weights):
    face_rows = surface[room_rows].reshape(weights.shape + (IY,))
    inflow, flux_back = opening_flow(street, weights, face_rows)
    return (surface.at[room_rows].add(inflow.reshape(-1, IY)), flux_back)


def body(
    parent_state,
    parent_depth,
    child_state,
    child_depth,
    child_wet,
    interior_state,
    interior_wet,
    parent_anchor,
    open_row,
    open_col,
    open_owner,
    open_valid,
    open_conduct,
    door_rows,
):
    tile_count = lax.axis_size("tile")
    my_tile = lax.axis_index("tile")
    requests = parent_anchor[0]
    anchor = requests[my_tile]
    owners = open_owner[:, 0]
    slot_of = ranks(owners, tile_count)
    cell_ids = (open_row * CY + open_col)[:, None] + jnp.arange(SEG, dtype=jnp.int32)[None, :]
    weights = place_rows(open_conduct * open_valid.astype(jnp.float32), owners, slot_of, tile_count)
    room_rows = door_rows[0]
    parent_now = parent_state
    child_now = child_state
    rooms_now = interior_state
    for section_index in range(STEPS):
        parent_stack = jnp.concatenate([parent_now, parent_depth[None]], 0)
        padded = padded_2(parent_stack, (("district", 1), ("tile", 2)), 2)
        surface, east_flow, north_flow = advance(padded, 1.0)
        parent_now = jnp.stack([surface, east_flow, north_flow])
        district_rows = lax.all_gather(surface, "tile", axis=1, tiled=True)
        window = lax.dynamic_slice(district_rows, (anchor[0], anchor[1]), (WX, WY))
        target = jnp.broadcast_to(window[:, None, :, None], (WX, R, WY, R)).reshape(CX, CY)
        wet_now = child_wet[section_index].astype(jnp.float32)
        child_stack = jnp.concatenate([child_now, (child_depth * wet_now)[None]], 0)
        padded = padded_2(child_stack, (("district", 1), ("tile", 2)), 2)
        surface, east_flow, north_flow = advance(padded, wet_now)
        surface = surface + nudging * (target - surface)
        rooms_now = room_step(rooms_now, interior_wet[section_index].astype(jnp.float32))
        flat_level = surface.reshape(-1)
        street = place_rows(flat_level[cell_ids], owners, slot_of, tile_count)
        inbound, inweights = (
            lax.all_to_all(
                street.reshape(tile_count, CAP * SEG),
                "tile",
                split_axis=0,
                concat_axis=0,
                tiled=True,
            ),
            lax.all_to_all(weights, "tile", split_axis=0, concat_axis=0, tiled=True),
        )
        inbound = inbound.reshape(tile_count, CAP, SEG)
        room_surface, flux_back = absorb(rooms_now[0], room_rows, inbound, inweights)
        returned = lax.all_to_all(
            flux_back.reshape(tile_count, CAP * SEG),
            "tile",
            split_axis=0,
            concat_axis=0,
            tiled=True,
        )
        returned = returned.reshape(tile_count, CAP, SEG)
        rooms_now = rooms_now.at[0].set(room_surface)
        flat_level = flat_level.at[cell_ids].add(-returned[owners, slot_of])
        child_now = jnp.stack([flat_level.reshape(CX, CY), east_flow, north_flow])
    return (parent_now, child_now, rooms_now)


def solution(mesh):
    return jax.shard_map(
        body,
        mesh=mesh,
        in_specs=(
            P(None, "district", "tile"),
            P("district", "tile"),
            P(None, "district", "tile"),
            P("district", "tile"),
            P(None, "district", "tile"),
            P(None, ("district", "tile"), None),
            P(None, ("district", "tile"), None),
            P("district", None, None),
            P(("district", "tile")),
            P(("district", "tile")),
            P(("district", "tile"), None),
            P(("district", "tile")),
            P(("district", "tile")),
            P(("district", "tile"), None),
        ),
        out_specs=(
            P(None, "district", "tile"),
            P(None, "district", "tile"),
            P(None, ("district", "tile"), None),
        ),
        check_vma=False,
    )
```

profile of v0, /device:TPU:1, one launch (start us, length us, event | category | flops | bytes accessed | tf_op | source)
XLA Modules:
  0.0 467.0 jit_solution(14156101166894164927)
XLA Ops:
  1.4 5.7 %collective-permute-start = (f32[4,2,128]{2,1,0:T(2,128)S(1)}, f32[4,2,128]{2,1,0:T(2,128)S(1)}, u32[]{:S(2)}, u32[]{:S(2)}) collective-permute-start(f32[4,2,128]{2,1,0:T(2,128)S(1)} %get-tuple-element.203), channel_id=1, source_target_pairs={{0,16},{16,32},{32,48},{48,64},{64,80},{80,96},{96,112},{112,128},... | collective-permute-start | bytes 12296 | tf_op jit(solution)/shard_map/ppermute | solution.py:30
  9.4 6.7 %collective-permute-start.16 = (f32[4,2,128]{2,1,0:T(2,128)S(1)}, f32[4,2,128]{2,1,0:T(2,128)S(1)}, u32[]{:S(2)}, u32[]{:S(2)}) collective-permute-start(f32[4,2,128]{2,1,0:T(2,128)S(1)} %get-tuple-element.171), channel_id=1, source_target_pairs={{0,16},{16,32},{32,48},{48,64},{64,80},{80,96},{96,112},{112,128},... | collective-permute-start | bytes 12296 | tf_op jit(solution)/shard_map/ppermute | solution.py:30
  22.7 6.2 %all-to-all-start = ((f32[16,1,8]{2,1,0:T(1,128)}), f32[16,1,8]{2,1,0:T(1,128)S(1)}, u32[]{:S(2)}, u32[]{:S(2)}) async-start(f32[16,1,8]{2,1,0:T(1,128)} %copy.81), calls=%async_computation | async-start | bytes 16384 | tf_op jit(solution)/shard_map/all_to_all | solution.py:135
  44.6 3.6 collective-permute-start.18
  50.7 20.3 %all_gather.12 = f32[16,2048]{1,0:T(8,128)S(1)} all-gather(f32[16,128]{1,0:T(8,128)S(1)} %fusion.135), channel_id=1, replica_groups=mesh['district'=16,'tile'=16] {'tile'}, dimensions={1}, use_global_device_ids=true | all-gather | bytes 139264 | tf_op jit(solution)/shard_map/all_gather | solution.py:116
  71.3 6.4 %collective-permute-start.4 = (f32[4,2,128]{2,1,0:T(2,128)S(1)}, f32[4,2,128]{2,1,0:T(2,128)S(1)}, u32[]{:S(2)}, u32[]{:S(2)}) collective-permute-start(f32[4,2,128]{2,1,0:T(2,128)S(1)} %get-tuple-element.201), channel_id=1, source_target_pairs={{0,16},{16,32},{32,48},{48,64},{64,80},{80,96},{96,112},{112,128},... | collective-permute-start | bytes 12296 | tf_op jit(solution)/shard_map/ppermute | solution.py:30
  79.4 5.1 %collective-permute-done.5 = f32[4,2,128]{2,1,0:T(2,128)S(1)} collective-permute-done((f32[4,2,128]{2,1,0:T(2,128)S(1)}, f32[4,2,128]{2,1,0:T(2,128)S(1)}, u32[]{:S(2)}, u32[]{:S(2)}) %collective-permute-start.5) | collective-permute-done | bytes 4128 | tf_op jit(solution)/shard_map/ppermute | solution.py:32
  93.2 5.7 %collective-permute-start.8 = (f32[4,2,128]{2,1,0:T(2,128)S(1)}, f32[4,2,128]{2,1,0:T(2,128)S(1)}, u32[]{:S(2)}, u32[]{:S(2)}) collective-permute-start(f32[4,2,128]{2,1,0:T(2,128)S(1)} %get-tuple-element.199), channel_id=1, source_target_pairs={{0,16},{16,32},{32,48},{48,64},{64,80},{80,96},{96,112},{112,128},... | collective-permute-start | bytes 12296 | tf_op jit(solution)/shard_map/ppermute | solution.py:30
  100.4 11.8 %gather_fusion = f32[2048]{0:T(1024)S(1)} fusion(f32[8192]{0:T(1024)S(1)} %add_bitcast_fusion.3, s32[2048]{0:T(1024)S(1)} %broadcast_clamp_fusion), kind=kCustom, calls=%fused_computation | custom fusion | bytes 24576 | tf_op jit(solution)/shard_map/gather | solution.py:126
  112.2 3.6 scatter_fusion.1
  116.5 8.8 %all-to-all-start.1 = ((f32[16,1,256]{2,1,0:T(1,128)}), f32[16,1,256]{2,1,0:T(1,128)S(1)}, u32[]{:S(2)}, u32[]{:S(2)}) async-start(f32[16,1,256]{2,1,0:T(1,128)} %all_to_all.51), calls=%async_computation.1 | async-start | bytes 32768 | tf_op jit(solution)/shard_map/all_to_all | solution.py:128
  125.5 3.5 collective-permute-start.10
  134.9 4.9 %collective-permute-start.12 = (f32[4,2,128]{2,1,0:T(2,128)S(1)}, f32[4,2,128]{2,1,0:T(2,128)S(1)}, u32[]{:S(2)}, u32[]{:S(2)}) collective-permute-start(f32[4,2,128]{2,1,0:T(2,128)S(1)} %get-tuple-element.197), channel_id=1, source_target_pairs={{0,16},{16,32},{32,48},{48,64},{64,80},{80,96},{96,112},{112,128},... | collective-permute-start | bytes 12296 | tf_op jit(solution)/shard_map/ppermute | solution.py:30
  141.1 18.9 %all_gather.13 = f32[16,2048]{1,0:T(8,128)S(1)} all-gather(f32[16,128]{1,0:T(8,128)S(1)} %fusion.133), channel_id=1, replica_groups=mesh['district'=16,'tile'=16] {'tile'}, dimensions={1}, use_global_device_ids=true | all-gather | bytes 139264 | tf_op jit(solution)/shard_map/all_gather | solution.py:116
  164.7 17.7 %all_gather.14 = f32[16,2048]{1,0:T(8,128)S(1)} all-gather(f32[16,128]{1,0:T(8,128)S(1)} %fusion.131), channel_id=1, replica_groups=mesh['district'=16,'tile'=16] {'tile'}, dimensions={1}, use_global_device_ids=true | all-gather | bytes 139264 | tf_op jit(solution)/shard_map/all_gather | solution.py:116
  183.9 18.6 %all_gather.15 = f32[16,2048]{1,0:T(8,128)S(1)} all-gather(f32[16,128]{1,0:T(8,128)S(1)} %fusion.129), channel_id=1, replica_groups=mesh['district'=16,'tile'=16] {'tile'}, dimensions={1}, use_global_device_ids=true | all-gather | bytes 139264 | tf_op jit(solution)/shard_map/all_gather | solution.py:116
  210.3 5.7 %all-to-all-done.2 = f32[16,1,256]{2,1,0:T(1,128)S(1)} async-done(((f32[16,1,256]{2,1,0:T(1,128)}), f32[16,1,256]{2,1,0:T(1,128)S(1)}, u32[]{:S(2)}, u32[]{:S(2)}) %all-to-all-start.2) | async-done | bytes 16416 | tf_op jit(solution)/shard_map/all_to_all | solution.py:139
  216.9 14.7 %scatter_fusion.2 = f32[8192]{0:T(1024)S(1)} fusion(f32[8192]{0:T(1024)S(1)} %add_bitcast_fusion.3, s32[2048]{0:T(1024)S(1)} %reshape.550, f32[2048]{0:T(1024)S(1)} %reshape.552), kind=kCustom, calls=%fused_computation.14 | custom fusion | flops 2048 | bytes 32768 | tf_op jit(solution)/shard_map/scatter-add | solution.py:148
  231.7 5.2 %collective-permute-start.20 = (f32[4,2,128]{2,1,0:T(2,128)S(1)}, f32[4,2,128]{2,1,0:T(2,128)S(1)}, u32[]{:S(2)}, u32[]{:S(2)}) collective-permute-start(f32[4,2,128]{2,1,0:T(2,128)S(1)} %get-tuple-element.167), channel_id=1, source_target_pairs={{0,16},{16,32},{32,48},{48,64},{64,80},{80,96},{96,112},{112,128},... | collective-permute-start | bytes 12296 | tf_op jit(solution)/shard_map/ppermute | solution.py:30
  238.3 4.0 collective-permute-done.21
  242.4 3.8 collective-permute-start.22
  253.2 11.8 %gather_fusion.3 = f32[2048]{0:T(1024)S(1)} fusion(f32[8192]{0:T(1024)S(1)} %add_bitcast_fusion.2, s32[2048]{0:T(1024)S(1)} %broadcast_clamp_fusion), kind=kCustom, calls=%fused_computation.3 | custom fusion | bytes 24576 | tf_op jit(solution)/shard_map/gather | solution.py:126
  265.1 3.6 scatter_fusion.3
  269.4 6.2 %all-to-all-start.3 = ((f32[16,1,256]{2,1,0:T(1,128)}), f32[16,1,256]{2,1,0:T(1,128)S(1)}, u32[]{:S(2)}, u32[]{:S(2)}) async-start(f32[16,1,256]{2,1,0:T(1,128)} %all_to_all.54), calls=%async_computation.3 | async-start | bytes 32768 | tf_op jit(solution)/shard_map/all_to_all | solution.py:128
  275.6 5.7 %all-to-all-done.3 = f32[16,1,256]{2,1,0:T(1,128)S(1)} async-done(((f32[16,1,256]{2,1,0:T(1,128)}), f32[16,1,256]{2,1,0:T(1,128)S(1)}, u32[]{:S(2)}, u32[]{:S(2)}) %all-to-all-start.3) | async-done | bytes 16416 | tf_op jit(solution)/shard_map/all_to_all | solution.py:128
  285.2 3.7 all-to-all-start.4
  288.9 5.8 %all-to-all-done.4 = f32[16,1,256]{2,1,0:T(1,128)S(1)} async-done(((f32[16,1,256]{2,1,0:T(1,128)}), f32[16,1,256]{2,1,0:T(1,128)S(1)}, u32[]{:S(2)}, u32[]{:S(2)}) %all-to-all-start.4) | async-done | bytes 16416 | tf_op jit(solution)/shard_map/all_to_all | solution.py:139
  295.7 14.5 %scatter_fusion.4 = f32[8192]{0:T(1024)S(1)} fusion(f32[8192]{0:T(1024)S(1)} %add_bitcast_fusion.2, s32[2048]{0:T(1024)S(1)} %reshape.550, f32[2048]{0:T(1024)S(1)} %reshape.574), kind=kCustom, calls=%fused_computation.17 | custom fusion | flops 2048 | bytes 32768 | tf_op jit(solution)/shard_map/scatter-add | solution.py:148
  310.2 5.6 %collective-permute-start.24 = (f32[4,2,128]{2,1,0:T(2,128)S(1)}, f32[4,2,128]{2,1,0:T(2,128)S(1)}, u32[]{:S(2)}, u32[]{:S(2)}) collective-permute-start(f32[4,2,128]{2,1,0:T(2,128)S(1)} %get-tuple-element.161), channel_id=1, source_target_pairs={{0,16},{16,32},{32,48},{48,64},{64,80},{80,96},{96,112},{112,128},... | collective-permute-start | bytes 12296 | tf_op jit(solution)/shard_map/ppermute | solution.py:30
  317.3 3.9 collective-permute-done.25
  321.3 3.9 collective-permute-start.26
  332.2 11.8 %gather_fusion.6 = f32[2048]{0:T(1024)S(1)} fusion(f32[8192]{0:T(1024)S(1)} %add_bitcast_fusion.1, s32[2048]{0:T(1024)S(1)} %broadcast_clamp_fusion), kind=kCustom, calls=%fused_computation.6 | custom fusion | bytes 24576 | tf_op jit(solution)/shard_map/gather | solution.py:126
  344.1 3.6 scatter_fusion.5
  348.4 6.2 %all-to-all-start.5 = ((f32[16,1,256]{2,1,0:T(1,128)}), f32[16,1,256]{2,1,0:T(1,128)S(1)}, u32[]{:S(2)}, u32[]{:S(2)}) async-start(f32[16,1,256]{2,1,0:T(1,128)} %all_to_all.57), calls=%async_computation.5 | async-start | bytes 32768 | tf_op jit(solution)/shard_map/all_to_all | solution.py:128
  354.6 5.7 %all-to-all-done.5 = f32[16,1,256]{2,1,0:T(1,128)S(1)} async-done(((f32[16,1,256]{2,1,0:T(1,128)}), f32[16,1,256]{2,1,0:T(1,128)S(1)}, u32[]{:S(2)}, u32[]{:S(2)}) %all-to-all-start.5) | async-done | bytes 16416 | tf_op jit(solution)/shard_map/all_to_all | solution.py:128
  364.2 3.7 all-to-all-start.6
  367.9 5.8 %all-to-all-done.6 = f32[16,1,256]{2,1,0:T(1,128)S(1)} async-done(((f32[16,1,256]{2,1,0:T(1,128)}), f32[16,1,256]{2,1,0:T(1,128)S(1)}, u32[]{:S(2)}, u32[]{:S(2)}) %all-to-all-start.6) | async-done | bytes 16416 | tf_op jit(solution)/shard_map/all_to_all | solution.py:139
  374.7 14.5 %scatter_fusion.6 = f32[8192]{0:T(1024)S(1)} fusion(f32[8192]{0:T(1024)S(1)} %add_bitcast_fusion.1, s32[2048]{0:T(1024)S(1)} %reshape.550, f32[2048]{0:T(1024)S(1)} %reshape.596), kind=kCustom, calls=%fused_computation.20 | custom fusion | flops 2048 | bytes 32768 | tf_op jit(solution)/shard_map/scatter-add | solution.py:148
  389.2 5.5 %collective-permute-start.28 = (f32[4,2,128]{2,1,0:T(2,128)S(1)}, f32[4,2,128]{2,1,0:T(2,128)S(1)}, u32[]{:S(2)}, u32[]{:S(2)}) collective-permute-start(f32[4,2,128]{2,1,0:T(2,128)S(1)} %get-tuple-element.155), channel_id=1, source_target_pairs={{0,16},{16,32},{32,48},{48,64},{64,80},{80,96},{96,112},{112,128},... | collective-permute-start | bytes 12296 | tf_op jit(solution)/shard_map/ppermute | solution.py:30
  396.2 4.1 collective-permute-done.29
  400.4 3.7 collective-permute-start.30
  411.1 11.8 %gather_fusion.9 = f32[2048]{0:T(1024)S(1)} fusion(f32[8192]{0:T(1024)S(1)} %add_bitcast_fusion, s32[2048]{0:T(1024)S(1)} %broadcast_clamp_fusion), kind=kCustom, calls=%fused_computation.9 | custom fusion | bytes 24576 | tf_op jit(solution)/shard_map/gather | solution.py:126
  423.0 3.6 scatter_fusion.7
  427.3 6.2 %all-to-all-start.7 = ((f32[16,1,256]{2,1,0:T(1,128)}), f32[16,1,256]{2,1,0:T(1,128)S(1)}, u32[]{:S(2)}, u32[]{:S(2)}) async-start(f32[16,1,256]{2,1,0:T(1,128)} %all_to_all.60), calls=%async_computation.7 | async-start | bytes 32768 | tf_op jit(solution)/shard_map/all_to_all | solution.py:128
  433.5 5.7 %all-to-all-done.7 = f32[16,1,256]{2,1,0:T(1,128)S(1)} async-done(((f32[16,1,256]{2,1,0:T(1,128)}), f32[16,1,256]{2,1,0:T(1,128)S(1)}, u32[]{:S(2)}, u32[]{:S(2)}) %all-to-all-start.7) | async-done | bytes 16416 | tf_op jit(solution)/shard_map/all_to_all | solution.py:128
  441.3 3.7 all-to-all-start.8
  446.3 4.5 all-to-all-done.8
  451.8 14.5 %scatter_fusion.8 = f32[8192]{0:T(1024)S(1)} fusion(f32[8192]{0:T(1024)S(1)} %add_bitcast_fusion, s32[2048]{0:T(1024)S(1)} %reshape.550, f32[2048]{0:T(1024)S(1)} %reshape.618), kind=kCustom, calls=%fused_computation.23 | custom fusion | flops 2048 | bytes 32768 | tf_op jit(solution)/shard_map/scatter-add | solution.py:148
  (313 shorter events, 100.6 us)
Async XLA Ops:
  0.6 28.3 %copy-start = (s32[1,16,2]{1,2,0:T(2,128)S(1)}, s32[1,16,2]{1,2,0:T(2,128)}, u32[]{:S(2)}) copy-start(s32[1,16,2]{1,2,0:T(2,128)} %param.29) | copy-start | bytes 388
  0.6 7.9 %copy-start.8 = (f32[64,128]{1,0:T(8,128)S(1)}, f32[64,128]{1,0:T(8,128)}, u32[]{:S(2)}) copy-start(f32[64,128]{1,0:T(8,128)} %param.25) | copy-start | bytes 98308
  1.4 36.9 %collective-permute-start = (f32[4,2,128]{2,1,0:T(2,128)S(1)}, f32[4,2,128]{2,1,0:T(2,128)S(1)}, u32[]{:S(2)}, u32[]{:S(2)}) collective-permute-start(f32[4,2,128]{2,1,0:T(2,128)S(1)} %get-tuple-element.203), channel_id=1, source_target_pairs={{0,16},{16,32},{32,48},{48,64},{64,80},{80,96},{96,112},{112,128},... | collective-permute-start | bytes 12296 | tf_op jit(solution)/shard_map/ppermute | solution.py:30
  7.1 31.1 %collective-permute-start.1 = (f32[4,2,128]{2,1,0:T(2,128)S(1)}, f32[4,2,128]{2,1,0:T(2,128)S(1)}, u32[]{:S(2)}, u32[]{:S(2)}) collective-permute-start(f32[4,2,128]{2,1,0:T(2,128)S(1)} %get-tuple-element.204), channel_id=1, source_target_pairs={{16,0},{32,16},{48,32},{64,48},{80,64},{96,80},{112,96},{128,112},... | collective-permute-start | bytes 12296 | tf_op jit(solution)/shard_map/ppermute | solution.py:32
  9.4 35.0 %collective-permute-start.16 = (f32[4,2,128]{2,1,0:T(2,128)S(1)}, f32[4,2,128]{2,1,0:T(2,128)S(1)}, u32[]{:S(2)}, u32[]{:S(2)}) collective-permute-start(f32[4,2,128]{2,1,0:T(2,128)S(1)} %get-tuple-element.171), channel_id=1, source_target_pairs={{0,16},{16,32},{32,48},{48,64},{64,80},{80,96},{96,112},{112,128},... | collective-permute-start | bytes 12296 | tf_op jit(solution)/shard_map/ppermute | solution.py:30
  16.2 28.2 %collective-permute-start.17 = (f32[4,2,128]{2,1,0:T(2,128)S(1)}, f32[4,2,128]{2,1,0:T(2,128)S(1)}, u32[]{:S(2)}, u32[]{:S(2)}) collective-permute-start(f32[4,2,128]{2,1,0:T(2,128)S(1)} %get-tuple-element.172), channel_id=1, source_target_pairs={{16,0},{32,16},{48,32},{64,48},{80,64},{96,80},{112,96},{128,112},... | collective-permute-start | bytes 12296 | tf_op jit(solution)/shard_map/ppermute | solution.py:32
  18.5 11.0 %copy-start.12 = (s32[64]{0:T(128)S(1)}, s32[64]{0:T(128)}, u32[]{:S(2)}) copy-start(s32[64]{0:T(128)} %param.31) | copy-start | bytes 772
  18.5 11.0 %copy-start.13 = (s32[64]{0:T(128)S(1)}, s32[64]{0:T(128)}, u32[]{:S(2)}) copy-start(s32[64]{0:T(128)} %param.30) | copy-start | bytes 772
  22.0 7.6 %copy-start.3 = (s32[4,64,128]{2,1,0:T(8,128)S(1)}, s32[4,64,128]{2,1,0:T(8,128)}, u32[]{:S(2)}) copy-start(s32[4,64,128]{2,1,0:T(8,128)} %param.28) | copy-start | bytes 393220
  22.7 14.2 %all-to-all-start = ((f32[16,1,8]{2,1,0:T(1,128)}), f32[16,1,8]{2,1,0:T(1,128)S(1)}, u32[]{:S(2)}, u32[]{:S(2)}) async-start(f32[16,1,8]{2,1,0:T(1,128)} %copy.81), calls=%async_computation | async-start | bytes 16384 | tf_op jit(solution)/shard_map/all_to_all | solution.py:135
  39.0 11.2 %collective-permute-start.2 = (f32[4,20,2]{2,1,0:T(8,128)S(1)}, f32[4,20,2]{2,1,0:T(8,128)S(1)}, u32[]{:S(2)}, u32[]{:S(2)}) collective-permute-start(f32[4,20,2]{2,1,0:T(8,128)S(1)} %get-tuple-element.195), channel_id=1, source_target_pairs={{0,1},{1,2},{2,3},{3,4},{4,5},{5,6},{6,7},{7,8},{8,9},{9,10},{10,1... | collective-permute-start | bytes 1928 | tf_op jit(solution)/shard_map/ppermute | solution.py:30
  42.5 7.7 %collective-permute-start.3 = (f32[4,20,2]{2,1,0:T(8,128)S(1)}, f32[4,20,2]{2,1,0:T(8,128)S(1)}, u32[]{:S(2)}, u32[]{:S(2)}) collective-permute-start(f32[4,20,2]{2,1,0:T(8,128)S(1)} %get-tuple-element.196), channel_id=1, source_target_pairs={{1,0},{2,1},{3,2},{4,3},{5,4},{6,5},{7,6},{8,7},{9,8},{10,9},{11,1... | collective-permute-start | bytes 1928 | tf_op jit(solution)/shard_map/ppermute | solution.py:32
  44.6 34.4 %collective-permute-start.18 = (f32[4,68,2]{2,1,0:T(8,128)S(1)}, f32[4,68,2]{2,1,0:T(8,128)S(1)}, u32[]{:S(2)}, u32[]{:S(2)}) collective-permute-start(f32[4,68,2]{2,1,0:T(8,128)S(1)} %get-tuple-element.143), channel_id=1, source_target_pairs={{0,1},{1,2},{2,3},{3,4},{4,5},{5,6},{6,7},{7,8},{8,9},{9,10},{10,1... | collective-permute-start | bytes 6536 | tf_op jit(solution)/shard_map/ppermute | solution.py:30
  48.2 30.8 %collective-permute-start.19 = (f32[4,68,2]{2,1,0:T(8,128)S(1)}, f32[4,68,2]{2,1,0:T(8,128)S(1)}, u32[]{:S(2)}, u32[]{:S(2)}) collective-permute-start(f32[4,68,2]{2,1,0:T(8,128)S(1)} %get-tuple-element.144), channel_id=1, source_target_pairs={{1,0},{2,1},{3,2},{4,3},{5,4},{6,5},{7,6},{8,7},{9,8},{10,9},{11,1... | collective-permute-start | bytes 6536 | tf_op jit(solution)/shard_map/ppermute | solution.py:32
  71.3 8.1 %collective-permute-start.4 = (f32[4,2,128]{2,1,0:T(2,128)S(1)}, f32[4,2,128]{2,1,0:T(2,128)S(1)}, u32[]{:S(2)}, u32[]{:S(2)}) collective-permute-start(f32[4,2,128]{2,1,0:T(2,128)S(1)} %get-tuple-element.201), channel_id=1, source_target_pairs={{0,16},{16,32},{32,48},{48,64},{64,80},{80,96},{96,112},{112,128},... | collective-permute-start | bytes 12296 | tf_op jit(solution)/shard_map/ppermute | solution.py:30
  77.7 6.7 %collective-permute-start.5 = (f32[4,2,128]{2,1,0:T(2,128)S(1)}, f32[4,2,128]{2,1,0:T(2,128)S(1)}, u32[]{:S(2)}, u32[]{:S(2)}) collective-permute-start(f32[4,2,128]{2,1,0:T(2,128)S(1)} %get-tuple-element.202), channel_id=1, source_target_pairs={{16,0},{32,16},{48,32},{64,48},{80,64},{96,80},{112,96},{128,112},... | collective-permute-start | bytes 12296 | tf_op jit(solution)/shard_map/ppermute | solution.py:32
  84.5 4.8 %collective-permute-start.6 = (f32[4,20,2]{2,1,0:T(8,128)S(1)}, f32[4,20,2]{2,1,0:T(8,128)S(1)}, u32[]{:S(2)}, u32[]{:S(2)}) collective-permute-start(f32[4,20,2]{2,1,0:T(8,128)S(1)} %get-tuple-element.193), channel_id=1, source_target_pairs={{0,1},{1,2},{2,3},{3,4},{4,5},{5,6},{6,7},{7,8},{8,9},{9,10},{10,1... | collective-permute-start | bytes 1928 | tf_op jit(solution)/shard_map/ppermute | solution.py:30
  87.3 5.4 %collective-permute-start.7 = (f32[4,20,2]{2,1,0:T(8,128)S(1)}, f32[4,20,2]{2,1,0:T(8,128)S(1)}, u32[]{:S(2)}, u32[]{:S(2)}) collective-permute-start(f32[4,20,2]{2,1,0:T(8,128)S(1)} %get-tuple-element.194), channel_id=1, source_target_pairs={{1,0},{2,1},{3,2},{4,3},{5,4},{6,5},{7,6},{8,7},{9,8},{10,9},{11,1... | collective-permute-start | bytes 1928 | tf_op jit(solution)/shard_map/ppermute | solution.py:32
  93.2 32.1 %collective-permute-start.8 = (f32[4,2,128]{2,1,0:T(2,128)S(1)}, f32[4,2,128]{2,1,0:T(2,128)S(1)}, u32[]{:S(2)}, u32[]{:S(2)}) collective-permute-start(f32[4,2,128]{2,1,0:T(2,128)S(1)} %get-tuple-element.199), channel_id=1, source_target_pairs={{0,16},{16,32},{32,48},{48,64},{64,80},{80,96},{96,112},{112,128},... | collective-permute-start | bytes 12296 | tf_op jit(solution)/shard_map/ppermute | solution.py:30
  99.0 26.4 %collective-permute-start.9 = (f32[4,2,128]{2,1,0:T(2,128)S(1)}, f32[4,2,128]{2,1,0:T(2,128)S(1)}, u32[]{:S(2)}, u32[]{:S(2)}) collective-permute-start(f32[4,2,128]{2,1,0:T(2,128)S(1)} %get-tuple-element.200), channel_id=1, source_target_pairs={{16,0},{32,16},{48,32},{64,48},{80,64},{96,80},{112,96},{128,112},... | collective-permute-start | bytes 12296 | tf_op jit(solution)/shard_map/ppermute | solution.py:32
  116.5 86.3 %all-to-all-start.1 = ((f32[16,1,256]{2,1,0:T(1,128)}), f32[16,1,256]{2,1,0:T(1,128)S(1)}, u32[]{:S(2)}, u32[]{:S(2)}) async-start(f32[16,1,256]{2,1,0:T(1,128)} %all_to_all.51), calls=%async_computation.1 | async-start | bytes 32768 | tf_op jit(solution)/shard_map/all_to_all | solution.py:128
  125.3 5.6 %copy-start.4 = (s32[4,64,128]{2,1,0:T(8,128)S(1)}, s32[4,64,128]{2,1,0:T(8,128)}, u32[]{:S(2)}) copy-start(s32[4,64,128]{2,1,0:T(8,128)} %param.26) | copy-start | bytes 393220
  125.5 5.6 %collective-permute-start.10 = (f32[4,20,2]{2,1,0:T(8,128)S(1)}, f32[4,20,2]{2,1,0:T(8,128)S(1)}, u32[]{:S(2)}, u32[]{:S(2)}) collective-permute-start(f32[4,20,2]{2,1,0:T(8,128)S(1)} %get-tuple-element.191), channel_id=1, source_target_pairs={{0,1},{1,2},{2,3},{3,4},{4,5},{5,6},{6,7},{7,8},{8,9},{9,10},{10,1... | collective-permute-start | bytes 1928 | tf_op jit(solution)/shard_map/ppermute | solution.py:30
  129.0 5.4 %collective-permute-start.11 = (f32[4,20,2]{2,1,0:T(8,128)S(1)}, f32[4,20,2]{2,1,0:T(8,128)S(1)}, u32[]{:S(2)}, u32[]{:S(2)}) collective-permute-start(f32[4,20,2]{2,1,0:T(8,128)S(1)} %get-tuple-element.192), channel_id=1, source_target_pairs={{1,0},{2,1},{3,2},{4,3},{5,4},{6,5},{7,6},{8,7},{9,8},{10,9},{11,1... | collective-permute-start | bytes 1928 | tf_op jit(solution)/shard_map/ppermute | solution.py:32
  134.9 25.4 %collective-permute-start.12 = (f32[4,2,128]{2,1,0:T(2,128)S(1)}, f32[4,2,128]{2,1,0:T(2,128)S(1)}, u32[]{:S(2)}, u32[]{:S(2)}) collective-permute-start(f32[4,2,128]{2,1,0:T(2,128)S(1)} %get-tuple-element.197), channel_id=1, source_target_pairs={{0,16},{16,32},{32,48},{48,64},{64,80},{80,96},{96,112},{112,128},... | collective-permute-start | bytes 12296 | tf_op jit(solution)/shard_map/ppermute | solution.py:30
  139.8 20.5 %collective-permute-start.13 = (f32[4,2,128]{2,1,0:T(2,128)S(1)}, f32[4,2,128]{2,1,0:T(2,128)S(1)}, u32[]{:S(2)}, u32[]{:S(2)}) collective-permute-start(f32[4,2,128]{2,1,0:T(2,128)S(1)} %get-tuple-element.198), channel_id=1, source_target_pairs={{16,0},{32,16},{48,32},{64,48},{80,64},{96,80},{112,96},{128,112},... | collective-permute-start | bytes 12296 | tf_op jit(solution)/shard_map/ppermute | solution.py:32
  160.4 22.4 %collective-permute-start.14 = (f32[4,20,2]{2,1,0:T(8,128)S(1)}, f32[4,20,2]{2,1,0:T(8,128)S(1)}, u32[]{:S(2)}, u32[]{:S(2)}) collective-permute-start(f32[4,20,2]{2,1,0:T(8,128)S(1)} %get-tuple-element.189), channel_id=1, source_target_pairs={{0,1},{1,2},{2,3},{3,4},{4,5},{5,6},{6,7},{7,8},{8,9},{9,10},{10,1... | collective-permute-start | bytes 1928 | tf_op jit(solution)/shard_map/ppermute | solution.py:30
  162.3 20.5 %collective-permute-start.15 = (f32[4,20,2]{2,1,0:T(8,128)S(1)}, f32[4,20,2]{2,1,0:T(8,128)S(1)}, u32[]{:S(2)}, u32[]{:S(2)}) collective-permute-start(f32[4,20,2]{2,1,0:T(8,128)S(1)} %get-tuple-element.190), channel_id=1, source_target_pairs={{1,0},{2,1},{3,2},{4,3},{5,4},{6,5},{7,6},{8,7},{9,8},{10,9},{11,1... | collective-permute-start | bytes 1928 | tf_op jit(solution)/shard_map/ppermute | solution.py:32
  206.7 9.3 %all-to-all-start.2 = ((f32[16,1,256]{2,1,0:T(1,128)}), f32[16,1,256]{2,1,0:T(1,128)S(1)}, u32[]{:S(2)}, u32[]{:S(2)}) async-start(f32[16,1,256]{2,1,0:T(1,128)} %mul.476), calls=%async_computation.2 | async-start | bytes 32768 | tf_op jit(solution)/shard_map/all_to_all | solution.py:139
  231.7 6.6 %collective-permute-start.20 = (f32[4,2,128]{2,1,0:T(2,128)S(1)}, f32[4,2,128]{2,1,0:T(2,128)S(1)}, u32[]{:S(2)}, u32[]{:S(2)}) collective-permute-start(f32[4,2,128]{2,1,0:T(2,128)S(1)} %get-tuple-element.167), channel_id=1, source_target_pairs={{0,16},{16,32},{32,48},{48,64},{64,80},{80,96},{96,112},{112,128},... | collective-permute-start | bytes 12296 | tf_op jit(solution)/shard_map/ppermute | solution.py:30
  236.9 5.4 %collective-permute-start.21 = (f32[4,2,128]{2,1,0:T(2,128)S(1)}, f32[4,2,128]{2,1,0:T(2,128)S(1)}, u32[]{:S(2)}, u32[]{:S(2)}) collective-permute-start(f32[4,2,128]{2,1,0:T(2,128)S(1)} %get-tuple-element.168), channel_id=1, source_target_pairs={{16,0},{32,16},{48,32},{64,48},{80,64},{96,80},{112,96},{128,112},... | collective-permute-start | bytes 12296 | tf_op jit(solution)/shard_map/ppermute | solution.py:32
  242.4 7.1 %collective-permute-start.22 = (f32[4,68,2]{2,1,0:T(8,128)S(1)}, f32[4,68,2]{2,1,0:T(8,128)S(1)}, u32[]{:S(2)}, u32[]{:S(2)}) collective-permute-start(f32[4,68,2]{2,1,0:T(8,128)S(1)} %get-tuple-element.141), channel_id=1, source_target_pairs={{0,1},{1,2},{2,3},{3,4},{4,5},{5,6},{6,7},{7,8},{8,9},{9,10},{10,1... | collective-permute-start | bytes 6536 | tf_op jit(solution)/shard_map/ppermute | solution.py:30
  246.2 6.5 %collective-permute-start.23 = (f32[4,68,2]{2,1,0:T(8,128)S(1)}, f32[4,68,2]{2,1,0:T(8,128)S(1)}, u32[]{:S(2)}, u32[]{:S(2)}) collective-permute-start(f32[4,68,2]{2,1,0:T(8,128)S(1)} %get-tuple-element.142), channel_id=1, source_target_pairs={{1,0},{2,1},{3,2},{4,3},{5,4},{6,5},{7,6},{8,7},{9,8},{10,9},{11,1... | collective-permute-start | bytes 6536 | tf_op jit(solution)/shard_map/ppermute | solution.py:32
  269.4 11.9 %all-to-all-start.3 = ((f32[16,1,256]{2,1,0:T(1,128)}), f32[16,1,256]{2,1,0:T(1,128)S(1)}, u32[]{:S(2)}, u32[]{:S(2)}) async-start(f32[16,1,256]{2,1,0:T(1,128)} %all_to_all.54), calls=%async_computation.3 | async-start | bytes 32768 | tf_op jit(solution)/shard_map/all_to_all | solution.py:128
  285.2 9.5 %all-to-all-start.4 = ((f32[16,1,256]{2,1,0:T(1,128)}), f32[16,1,256]{2,1,0:T(1,128)S(1)}, u32[]{:S(2)}, u32[]{:S(2)}) async-start(f32[16,1,256]{2,1,0:T(1,128)} %mul.477), calls=%async_computation.4 | async-start | bytes 32768 | tf_op jit(solution)/shard_map/all_to_all | solution.py:139
  310.2 7.0 %collective-permute-start.24 = (f32[4,2,128]{2,1,0:T(2,128)S(1)}, f32[4,2,128]{2,1,0:T(2,128)S(1)}, u32[]{:S(2)}, u32[]{:S(2)}) collective-permute-start(f32[4,2,128]{2,1,0:T(2,128)S(1)} %get-tuple-element.161), channel_id=1, source_target_pairs={{0,16},{16,32},{32,48},{48,64},{64,80},{80,96},{96,112},{112,128},... | collective-permute-start | bytes 12296 | tf_op jit(solution)/shard_map/ppermute | solution.py:30
  315.9 5.3 %collective-permute-start.25 = (f32[4,2,128]{2,1,0:T(2,128)S(1)}, f32[4,2,128]{2,1,0:T(2,128)S(1)}, u32[]{:S(2)}, u32[]{:S(2)}) collective-permute-start(f32[4,2,128]{2,1,0:T(2,128)S(1)} %get-tuple-element.162), channel_id=1, source_target_pairs={{16,0},{32,16},{48,32},{64,48},{80,64},{96,80},{112,96},{128,112},... | collective-permute-start | bytes 12296 | tf_op jit(solution)/shard_map/ppermute | solution.py:32
  321.3 7.2 %collective-permute-start.26 = (f32[4,68,2]{2,1,0:T(8,128)S(1)}, f32[4,68,2]{2,1,0:T(8,128)S(1)}, u32[]{:S(2)}, u32[]{:S(2)}) collective-permute-start(f32[4,68,2]{2,1,0:T(8,128)S(1)} %get-tuple-element.139), channel_id=1, source_target_pairs={{0,1},{1,2},{2,3},{3,4},{4,5},{5,6},{6,7},{7,8},{8,9},{9,10},{10,1... | collective-permute-start | bytes 6536 | tf_op jit(solution)/shard_map/ppermute | solution.py:30
  325.2 6.5 %collective-permute-start.27 = (f32[4,68,2]{2,1,0:T(8,128)S(1)}, f32[4,68,2]{2,1,0:T(8,128)S(1)}, u32[]{:S(2)}, u32[]{:S(2)}) collective-permute-start(f32[4,68,2]{2,1,0:T(8,128)S(1)} %get-tuple-element.140), channel_id=1, source_target_pairs={{1,0},{2,1},{3,2},{4,3},{5,4},{6,5},{7,6},{8,7},{9,8},{10,9},{11,1... | collective-permute-start | bytes 6536 | tf_op jit(solution)/shard_map/ppermute | solution.py:32
  348.4 11.9 %all-to-all-start.5 = ((f32[16,1,256]{2,1,0:T(1,128)}), f32[16,1,256]{2,1,0:T(1,128)S(1)}, u32[]{:S(2)}, u32[]{:S(2)}) async-start(f32[16,1,256]{2,1,0:T(1,128)} %all_to_all.57), calls=%async_computation.5 | async-start | bytes 32768 | tf_op jit(solution)/shard_map/all_to_all | solution.py:128
  364.2 9.5 %all-to-all-start.6 = ((f32[16,1,256]{2,1,0:T(1,128)}), f32[16,1,256]{2,1,0:T(1,128)S(1)}, u32[]{:S(2)}, u32[]{:S(2)}) async-start(f32[16,1,256]{2,1,0:T(1,128)} %mul.478), calls=%async_computation.6 | async-start | bytes 32768 | tf_op jit(solution)/shard_map/all_to_all | solution.py:139
  389.2 6.9 %collective-permute-start.28 = (f32[4,2,128]{2,1,0:T(2,128)S(1)}, f32[4,2,128]{2,1,0:T(2,128)S(1)}, u32[]{:S(2)}, u32[]{:S(2)}) collective-permute-start(f32[4,2,128]{2,1,0:T(2,128)S(1)} %get-tuple-element.155), channel_id=1, source_target_pairs={{0,16},{16,32},{32,48},{48,64},{64,80},{80,96},{96,112},{112,128},... | collective-permute-start | bytes 12296 | tf_op jit(solution)/shard_map/ppermute | solution.py:30
  394.8 5.5 %collective-permute-start.29 = (f32[4,2,128]{2,1,0:T(2,128)S(1)}, f32[4,2,128]{2,1,0:T(2,128)S(1)}, u32[]{:S(2)}, u32[]{:S(2)}) collective-permute-start(f32[4,2,128]{2,1,0:T(2,128)S(1)} %get-tuple-element.156), channel_id=1, source_target_pairs={{16,0},{32,16},{48,32},{64,48},{80,64},{96,80},{112,96},{128,112},... | collective-permute-start | bytes 12296 | tf_op jit(solution)/shard_map/ppermute | solution.py:32
  400.4 6.9 %collective-permute-start.30 = (f32[4,68,2]{2,1,0:T(8,128)S(1)}, f32[4,68,2]{2,1,0:T(8,128)S(1)}, u32[]{:S(2)}, u32[]{:S(2)}) collective-permute-start(f32[4,68,2]{2,1,0:T(8,128)S(1)} %get-tuple-element.137), channel_id=1, source_target_pairs={{0,1},{1,2},{2,3},{3,4},{4,5},{5,6},{6,7},{7,8},{8,9},{9,10},{10,1... | collective-permute-start | bytes 6536 | tf_op jit(solution)/shard_map/ppermute | solution.py:30
  404.1 6.5 %collective-permute-start.31 = (f32[4,68,2]{2,1,0:T(8,128)S(1)}, f32[4,68,2]{2,1,0:T(8,128)S(1)}, u32[]{:S(2)}, u32[]{:S(2)}) collective-permute-start(f32[4,68,2]{2,1,0:T(8,128)S(1)} %get-tuple-element.138), channel_id=1, source_target_pairs={{1,0},{2,1},{3,2},{4,3},{5,4},{6,5},{7,6},{8,7},{9,8},{10,9},{11,1... | collective-permute-start | bytes 6536 | tf_op jit(solution)/shard_map/ppermute | solution.py:32
  427.3 12.0 %all-to-all-start.7 = ((f32[16,1,256]{2,1,0:T(1,128)}), f32[16,1,256]{2,1,0:T(1,128)S(1)}, u32[]{:S(2)}, u32[]{:S(2)}) async-start(f32[16,1,256]{2,1,0:T(1,128)} %all_to_all.60), calls=%async_computation.7 | async-start | bytes 32768 | tf_op jit(solution)/shard_map/all_to_all | solution.py:128
  441.3 9.5 %all-to-all-start.8 = ((f32[16,1,256]{2,1,0:T(1,128)}), f32[16,1,256]{2,1,0:T(1,128)S(1)}, u32[]{:S(2)}, u32[]{:S(2)}) async-start(f32[16,1,256]{2,1,0:T(1,128)} %mul.479), calls=%async_computation.8 | async-start | bytes 32768 | tf_op jit(solution)/shard_map/all_to_all | solution.py:139
  446.3 5.4 %copy-start.6 = (f32[3,64,128]{2,1,0:T(8,128)}, f32[3,64,128]{2,1,0:T(8,128)S(1)}, u32[]{:S(2)}) copy-start(f32[3,64,128]{2,1,0:T(8,128)S(1)} %bitcast_dynamic-update-slice_fusion) | copy-start | bytes 294916
  (8 other events, 10.4 us)
where the time goes:
time: 469 us; the launch traced here: 467 us
  starting transfers between devices  147 us (31%)
  local copies, waits for them, and re-layouts  91 us (19%)
  blocking collectives  75.6 us (16%)
  other arithmetic  75 us (16%)
  waiting for transfers between devices  72.2 us (15%)
  between operations  6.22 us (1%)
    all_gather x4, blocking collectives, body(): district_rows = lax.all_gather(surface, 'tile', axis=1, tiled=True)  75.6 us
    ppermute x16, starting transfers between devices, padded_2(): lax.ppermute(tail, axis, [(i, (i + 1) % count) for i in range(ends)])  72.6 us
    scatter-add x4, other arithmetic, body(): flat_level = flat_level.at[cell_ids].add(-returned[owners, slot_of])  58.4 us
    gather x8, local copies, waits for them, and re-layouts, body(): street = place_rows(flat_level[cell_ids], owners, slot_of, tile_count)  47.4 us
    ppermute x16, waiting for transfers between devices, padded_2(): lax.ppermute(head, axis, [((i + 1) % count, i) for i in range(ends)])  33.3 us
    all_to_all x4, starting transfers between devices, body(): lax.all_to_all(street.reshape(tile_count, CAP * SEG), 'tile', split_axis=...  27.3 us
    ppermute x16, starting transfers between devices, padded_2(): lax.ppermute(head, axis, [((i + 1) % count, i) for i in range(ends)])  26.3 us
    all_to_all x4, waiting for transfers between devices, body(): lax.all_to_all(flux_back.reshape(tile_count, CAP * SEG), 'tile', split_ax...  21.7 us
  transfers between devices with their start and end apart: 41, of which 16 were waited for; matrix products, arithmetic and copies ran while one was open for 7% of the time, Pallas kernels for 0%

commit v1 on v0

v1 whole, which is shorter than its diff:
```python
import jax
import jax.numpy as jnp
from jax import lax
from jax.experimental import pallas as pl
from jax.experimental.pallas import tpu as pltpu
from jax.sharding import PartitionSpec as P

f32 = jnp.float32
bf16 = jnp.bfloat16
i32 = jnp.int32

CX = 64
PX = 16
LANES = 128
R = 32
STEPS = 4
CAP = 8
TILES = 16
SLOTS = TILES * CAP

courant = 0.3
nudging = 0.25
area_ratio = 0.0625

L_ROOM = 32
L_NEAR = 64
L_FIX = 68
L_PCOL = 72
L_WIN = 80
L_CCOL = 96


def lane(shape):
    return lax.broadcasted_iota(i32, shape, 1)


def sub(shape):
    return lax.broadcasted_iota(i32, shape, 0)


def roll(cells, by):
    return pltpu.roll(cells, by % LANES, 1)


def along(cells, index):
    return jnp.take_along_axis(cells, index, axis=1, mode="promise_in_bounds")


def halves(cells):
    high = cells.astype(bf16)
    low = (cells - high.astype(f32)).astype(bf16)
    return jnp.concatenate([high, low], 0)


def pick(selector, cells):
    return jnp.dot(selector, halves(cells), preferred_element_type=f32)


def pack4(packed, cells, at):
    at_lane = lane(packed.shape)
    for g in range(cells.shape[0] // 8):
        first = at + 4 * g
        moved = roll(cells[8 * g : 8 * g + 8], first + 2)
        packed = jnp.where((at_lane >= first) & (at_lane < first + 4), moved, packed)
    return packed


def pack2(packed, cells, at):
    at_lane = lane(packed.shape)
    for g in range(cells.shape[0] // 8):
        first = at + 2 * g
        moved = roll(cells[8 * g : 8 * g + 8], first + 1)
        packed = jnp.where((at_lane >= first) & (at_lane < first + 2), moved, packed)
    return packed


def unpack4(left, right, at, groups):
    chosen = jnp.where(lane(left.shape) % 4 >= 2, right, left)
    return jnp.concatenate([roll(chosen, -(at + 4 * g + 2)) for g in range(groups)], 0)


def unpack2(left, right, at, groups):
    chosen = jnp.where(lane(left.shape) % 2 == 1, right, left)
    return jnp.concatenate([roll(chosen, -(at + 2 * g + 1)) for g in range(groups)], 0)


def advance(eta_x, u_x, v, v_h, eta_h, q, q_up, q_dn, q_h, flux_x, rows):
    top, end = 8, 8 + rows
    at_lane = lane((rows, LANES))
    first, last = at_lane == 0, at_lane == LANES - 1
    eta = eta_x[top:end]
    u_new = u_x[top:end] - courant * (eta_x[top + 1 : end + 1] - eta_x[top - 1 : end - 1])
    u_up = u_x[top - 1 : top] - courant * (eta_x[top : top + 1] - eta_x[top - 2 : top - 1])
    u_dn = u_x[end : end + 1] - courant * (eta_x[end + 1 : end + 2] - eta_x[end - 1 : end])
    after = roll(jnp.where(first, eta_h, eta), -1)
    before = roll(jnp.where(last, eta_h, eta), 1)
    v_new = v - courant * (after - before)
    after = roll(jnp.where(first, eta, eta_h), -1)
    before = roll(jnp.where(last, eta, eta_h), 1)
    v_edge = v_h - courant * (after - before)
    flux_x[top:end] = q * u_new
    flux_x[top - 1 : top] = q_up * u_up
    flux_x[end : end + 1] = q_dn * u_dn
    flux = q * v_new
    flux_h = q_h * v_edge
    after = roll(jnp.where(first, flux_h, flux), -1)
    before = roll(jnp.where(last, flux_h, flux), 1)
    eta_new = eta - courant * (
        flux_x[top + 1 : end + 1] - flux_x[top - 1 : end - 1] + after - before
    )
    return eta_new, u_new, u_up, u_dn, v_new, v_edge


def wet_of(q):
    return jnp.where(q > 0, 1.0, 0.0).astype(f32)


def room_advance(eta, u, v, wet, eta_x, flux_x):
    at_lane = lane((CX, LANES))
    first, last = at_lane == 0, at_lane == LANES - 1
    blank = jnp.zeros((8, LANES), f32)
    for ref in (eta_x, flux_x):
        ref[0:8] = blank
        ref[8 + CX : 16 + CX] = blank
    eta_x[8 : 8 + CX] = eta
    u_new = u - courant * (eta_x[9 : 9 + CX] - eta_x[7 : 7 + CX])
    v_new = v - courant * (
        jnp.where(last, 0.0, roll(eta, -1)) - jnp.where(first, 0.0, roll(eta, 1))
    )
    flux_x[8 : 8 + CX] = wet * u_new
    flux = wet * v_new
    eta_new = eta - courant * (
        flux_x[9 : 9 + CX]
        - flux_x[7 : 7 + CX]
        + jnp.where(last, 0.0, roll(flux, -1))
        - jnp.where(first, 0.0, roll(flux, 1))
    )
    return eta_new, wet * u_new, wet * v_new


def room_reply(eta, door2, fixed):
    sums = eta + roll(eta, -1)
    sums = sums + roll(sums, -2)
    at_lane = lane((CX, LANES))
    sums = along(sums, (4 * (at_lane - L_ROOM)) & (LANES - 1))
    both = pick(door2, jnp.concatenate([eta, sums], 1))
    rows, sums = both[:, :LANES], both[:, LANES:]
    ahead = roll(jnp.concatenate([sums[8:], sums[:8]], 0), L_NEAR - L_ROOM)
    behind = roll(jnp.concatenate([sums[-8:], sums[:-8]], 0), L_NEAR + 2 - (L_ROOM + 30))
    at_lane = lane(sums.shape)
    reply = jnp.where(
        at_lane < L_NEAR,
        sums,
        jnp.where(at_lane < L_NEAR + 2, ahead, jnp.where(at_lane < L_FIX, behind, fixed)),
    )
    return rows, reply


def slots_of(side):
    shape = (SLOTS, LANES)
    held = sub(shape).astype(f32) == side[8:9]

    def take(values):
        return jnp.sum(jnp.where(held, values, 0.0), axis=1, keepdims=True)

    row = take(side[9:10] + 1.0) - 1.0
    return row.astype(i32), take(side[10:11]).astype(i32), take(side[11:12])


def edges_kernel(
    parent, parent_depth, child, child_depth, child_wet, row, col, owner, owner_t, valid, conduct, up, dn, side
):
    up[...] = jnp.zeros((16, LANES), f32)
    dn[...] = jnp.zeros((16, LANES), f32)
    side[...] = jnp.zeros((16, LANES), f32)
    eta = child[0]
    packed = pack4(jnp.zeros((8, LANES), f32), eta, 0)
    packed = pack2(packed, child[2], 32)
    up[0:2] = eta[0:2]
    dn[0:2] = eta[CX - 2 : CX]
    up[2:3] = child[1, 0:1]
    dn[2:3] = child[1, CX - 1 : CX]
    for s in range(STEPS):
        q = child_depth[...] * child_wet[s].astype(f32)
        up[3 + s : 4 + s] = q[0:1]
        dn[3 + s : 4 + s] = q[CX - 1 : CX]
        packed = pack2(packed, q, 48 + 16 * s)
    eta = parent[0]
    up[7:9] = eta[0:2]
    dn[7:9] = eta[PX - 2 : PX]
    up[9:10] = parent[1, 0:1]
    dn[9:10] = parent[1, PX - 1 : PX]
    up[10:11] = parent_depth[0:1]
    dn[10:11] = parent_depth[PX - 1 : PX]
    packed = pack4(packed, eta, 112)
    packed = pack2(packed, parent[2], 120)
    packed = pack2(packed, parent_depth[...], 124)
    side[0:8] = packed
    count = owner.shape[1]
    earlier = (owner_t[...] == owner[...]) & (sub((count, count)) < lane((count, count)))
    rank = jnp.sum(jnp.where(earlier, 1.0, 0.0), axis=0, keepdims=True)
    side[8:9] = jnp.full((1, LANES), -1.0, f32)
    side[8:9, 0:count] = owner[...].astype(f32) * CAP + rank
    side[9:10, 0:count] = row[...].astype(f32)
    side[10:11, 0:count] = col[...].astype(f32)
    side[11:12, 0:count] = conduct[...] * valid[...].astype(f32)


def setup_kernel(
    side, door, room, room_wet, row2, row_t2, index_s, index_a, gain, lower, fixed, door2, door_t2, room_new, face, reply, eta_x, flux_x
):
    shape = (SLOTS, LANES)
    at_lane = lane(shape)
    row, col, weight = slots_of(side[...])
    chosen = jnp.where(at_lane == row, 1.0, 0.0)
    row2[...] = (chosen + roll(chosen, CX)).astype(bf16)
    turned = jnp.transpose(chosen)[0:CX].astype(bf16)
    row_t2[...] = jnp.concatenate([turned, turned], 1)
    index_s[...] = (at_lane + col) & (LANES - 1)
    index_a[...] = (at_lane - col + L_ROOM) & (LANES - 1)
    inside = (at_lane >= col) & (at_lane < col + R)
    gain[...] = jnp.where(inside, area_ratio * weight, 0.0)
    half = jnp.where(row >= R, 1.0, 0.0)
    lower[...] = jnp.broadcast_to(half, shape)
    fixed_now = jnp.where(
        at_lane == L_FIX,
        weight,
        jnp.where(at_lane == L_FIX + 1, col.astype(f32), jnp.where(at_lane == L_FIX + 2, half, 0.0)),
    )
    fixed[...] = fixed_now
    chosen_t = jnp.where(sub(shape) == door[...], 1.0, 0.0)
    turned = chosen_t[0:CX].astype(bf16)
    door_t2[...] = jnp.concatenate([turned, turned], 1)
    chosen = jnp.transpose(chosen_t)
    both = (chosen + roll(chosen, CX)).astype(bf16)
    door2[...] = both
    eta, u, v = room_advance(room[0], room[1], room[2], room_wet[0].astype(f32), eta_x, flux_x)
    room_new[0] = eta
    room_new[1] = u
    room_new[2] = v
    face[...], reply[...] = room_reply(eta, both, fixed_now)


def near_kernel(left, right, row2, row_t2, index, gain):
    shape = (SLOTS, LANES)
    at_lane = lane(shape)
    turned = []
    for part, side in enumerate((right, left)):
        rows = slice(part * SLOTS, (part + 1) * SLOTS)
        row, col, weight = slots_of(side[...])
        chosen = jnp.where(at_lane == row, 1.0, 0.0)
        row2[rows] = (chosen + roll(chosen, CX)).astype(bf16)
        turned.append(jnp.transpose(chosen)[0:CX].astype(bf16))
        if part == 0:
            touched = (at_lane < 2) & (at_lane >= col)
            index[rows] = (at_lane - col + L_NEAR) & (LANES - 1)
        else:
            touched = (at_lane >= LANES - 2) & (at_lane < col + R)
            index[rows] = (at_lane - col + (L_NEAR + 2 - 30)) & (LANES - 1)
        gain[rows] = jnp.where(touched, area_ratio * weight, 0.0)
    row_t2[...] = jnp.concatenate(turned + turned, 1)


def send_kernel(step, *refs):
    if step == 0:
        (
            scal, parent, parent_depth, child, child_depth, child_wet, above0, below0, left0, right0, reply, row2, index_s,
            eta_o, u_o, v_o, vh_o, peta_o, pu_o, pv_o, pvh_o, street_o, out, eta_x, flux_x, u_x, peta_x, pflux_x, pu_x,
        ) = refs
        u_x[8 : 8 + CX] = child[1]
        u_x[7:8] = above0[2:3]
        u_x[8 + CX : 9 + CX] = below0[2:3]
        pu_x[8 : 8 + PX] = parent[1]
        pu_x[7:8] = above0[9:10]
        pu_x[8 + PX : 9 + PX] = below0[9:10]
        eta_x[8 : 8 + CX] = child[0]
        peta_x[8 : 8 + PX] = parent[0]
        eta_x[6:8] = above0[0:2]
        eta_x[8 + CX : 10 + CX] = below0[0:2]
        peta_x[6:8] = above0[7:9]
        peta_x[8 + PX : 10 + PX] = below0[7:9]
        left, right = left0[0:8], right0[0:8]
        v, v_h = child[2], unpack2(left, right, 32, 8)
        eta_h = unpack4(left, right, 0, 8)
        pv, pv_h = parent[2], unpack2(left, right, 120, 2)
        peta_h = unpack4(left, right, 112, 2)
    else:
        (
            scal, parent_depth, child_depth, child_wet, above0, below0, left0, right0, reply, row2, index_s,
            above, below, eta_i, u_x, v_i, vh_i, etah_i, peta_i, pu_x, pv_i, pvh_i, petah_i,
            eta_o, u_o, v_o, vh_o, peta_o, pu_o, pv_o, pvh_o, street_o, out, eta_x, flux_x, peta_x, pflux_x,
        ) = refs
        eta_x[8 : 8 + CX] = eta_i[...]
        peta_x[8 : 8 + PX] = peta_i[...]
        eta_x[6:8] = above[0:2]
        eta_x[8 + CX : 10 + CX] = below[0:2]
        peta_x[6:8] = above[2:4]
        peta_x[8 + PX : 10 + PX] = below[2:4]
        left, right = left0[0:8], right0[0:8]
        v, v_h, eta_h = v_i[...], vh_i[...], etah_i[...]
        pv, pv_h, peta_h = pv_i[...], pvh_i[...], petah_i[...]
    wet = child_wet[step].astype(f32)
    q = child_depth[...] * wet
    q_up, q_dn = above0[3 + step : 4 + step], below0[3 + step : 4 + step]
    q_h = unpack2(left, right, 48 + 16 * step, 8)
    eta, u, u_up, u_dn, v, v_h = advance(eta_x, u_x, v, v_h, eta_h, q, q_up, q_dn, q_h, flux_x, CX)
    street = pick(row2[...], eta)
    peta, pu, pu_up, pu_dn, pv, pv_h = advance(
        peta_x, pu_x, pv, pv_h, peta_h, parent_depth[...], above0[10:11], below0[10:11], unpack2(left, right, 124, 2), pflux_x, PX
    )
    eta_o[...] = eta
    u_o[8 : 8 + CX] = wet * u
    u_o[7:8] = wet_of(q_up) * u_up
    u_o[8 + CX : 9 + CX] = wet_of(q_dn) * u_dn
    v_o[...] = wet * v
    vh_o[...] = wet_of(q_h) * v_h
    peta_o[...] = peta
    pu_o[8 : 8 + PX] = pu
    pu_o[7:8] = pu_up
    pu_o[8 + PX : 9 + PX] = pu_dn
    pv_o[...] = pv
    pvh_o[...] = pv_h
    street_o[...] = street
    tile, first_row, first_col = scal[0], scal[1], scal[2]
    shape = (8, LANES)
    at_lane = lane(shape)
    common = pack4(jnp.zeros(shape, f32), eta, L_CCOL)
    common = pack4(common, peta, L_PCOL)
    line0 = peta_o[pl.ds(first_row, 1)]
    line1 = peta_o[pl.ds(first_row + 1, 1)]
    lines = jnp.where(sub(shape) < 4, line0, line1)
    index = first_col - LANES * tile + 4 * (at_lane - L_WIN) + (sub(shape) & 3)
    window = along(lines, index & (LANES - 1))
    window = jnp.where((index >= 0) & (index < LANES), window, 0.0)
    common = jnp.where((at_lane >= L_WIN) & (at_lane < L_CCOL), window, common)
    street = along(street, index_s[...])
    for t in range(TILES):
        rows = slice(t * CAP, (t + 1) * CAP)
        out[rows] = jnp.where(at_lane < R, street[rows], jnp.where(at_lane < L_PCOL, reply[rows], common))


def windows_sum(inbox):
    parts = [inbox[8 * t : 8 * t + 8] for t in range(TILES)]
    while len(parts) > 1:
        parts = [parts[i] + parts[i + 1] for i in range(0, len(parts), 2)]
    return parts[0]


def nudge(eta, target):
    return eta + nudging * (target - eta)


def street_update(scal, inbox, eta, street, row_t2, index_a, gain, lower):
    shape = (8, LANES)
    windows = windows_sum(inbox)
    mine = along(windows, jnp.full(shape, L_WIN, i32) + scal[0])
    mine = jnp.where((sub(shape) & 3) == lane(shape) // R, mine, 0.0)
    target0 = jnp.sum(mine[0:4], axis=0, keepdims=True)
    target1 = jnp.sum(mine[4:8], axis=0, keepdims=True)
    eta = jnp.concatenate([nudge(eta[0:R], target0), nudge(eta[R:CX], target1)], 0)
    levels = nudge(street, jnp.where(lower > 0, target1, target0))
    flow = gain * (4.0 * levels - along(inbox, index_a))
    return eta - pick(row_t2, flow), windows


def room_flow(inbox, windows, face):
    shape = (SLOTS, LANES)
    at_lane = lane(shape)
    holder = jnp.where(at_lane == L_WIN + sub(shape) // CAP, 1.0, 0.0).astype(bf16)
    high = windows.astype(bf16)
    low = (windows - high.astype(f32)).astype(bf16)
    per_slot = lax.dot_general(
        jnp.concatenate([holder, holder], 1),
        jnp.concatenate([jnp.concatenate([high, low], 1), jnp.zeros((LANES - 8, 2 * LANES), bf16)], 0),
        (((1,), (1,)), ((), ())),
        preferred_element_type=f32,
    )
    weight = inbox[:, L_FIX : L_FIX + 1]
    col = inbox[:, L_FIX + 1 : L_FIX + 2].astype(i32)
    half = inbox[:, L_FIX + 2 : L_FIX + 3].astype(i32)
    cell = at_lane // 4
    target = along(per_slot, 4 * half + ((col + cell) // R & 3))
    levels = nudge(along(inbox, cell), target)
    return weight * (levels - face)


def street_kernel(scal, inbox, eta, street, row_t2, index_a, gain, lower, peta, eta_o, up, dn, windows_o):
    eta, windows_o[...] = street_update(
        scal, inbox[...], eta[...], street[...], row_t2[...], index_a[...], gain[...], lower[...]
    )
    eta_o[...] = eta
    blank = jnp.zeros((4, LANES), f32)
    up[0:2] = eta[0:2]
    up[2:4] = peta[0:2]
    up[4:8] = blank
    dn[0:2] = eta[CX - 2 : CX]
    dn[2:4] = peta[PX - 2 : PX]
    dn[4:8] = blank


def room_kernel(
    step, scal, inbox, windows, room, room_wet, face, door2, door_t2, fixed, near2, near_t2, near_index, near_gain,
    room_new, face_o, reply, etah_o, petah_o, eta_x, flux_x,
):
    received = inbox[...]
    flow = room_flow(received, windows[...], face[...])
    eta = room[0] + pick(door_t2[...], flow)
    eta, u, v = room_advance(eta, room[1], room[2], room_wet[step].astype(f32), eta_x, flux_x)
    room_new[0] = eta
    room_new[1] = u
    room_new[2] = v
    face_o[...], reply[...] = room_reply(eta, door2[...], fixed[...])
    tile = scal[0]
    left = inbox[pl.ds(pl.multiple_of(8 * lax.rem(tile + TILES - 1, TILES), 8), 8)]
    right = inbox[pl.ds(pl.multiple_of(8 * lax.rem(tile + 1, TILES), 8), 8)]
    at_lane = lane((8, LANES))

    def kept(cells):
        return jnp.where(jnp.where(lane(cells.shape) < R, TILES - 1 - tile, tile) > 0, cells, 0.0)

    petah_o[...] = kept(unpack4(left, right, L_PCOL, 2))
    eta_h = unpack4(left, right, L_CCOL, 8)
    spread = along(windows[...], L_WIN + ((jnp.where(at_lane < R, tile + 1, tile - 1)) & (TILES - 1)))
    target0 = jnp.where(at_lane < R, spread[0:1], spread[3:4])
    target1 = jnp.where(at_lane < R, spread[4:5], spread[7:8])
    eta_h = nudge(eta_h, jnp.concatenate([target0] * 4 + [target1] * 4, 0))
    levels = pick(near2[...], eta_h)
    sums = along(jnp.concatenate([received, received], 0), near_index[...])
    eta_h = eta_h - pick(near_t2[...], near_gain[...] * (4.0 * levels - sums))
    etah_o[...] = kept(eta_h)


def final_kernel(
    scal, inbox, eta, street, row_t2, index_a, gain, lower, u_x, v, peta, pu_x, pv, room, face, door_t2,
    parent_o, child_o, room_o,
):
    received = inbox[...]
    eta, windows = street_update(scal, received, eta[...], street[...], row_t2[...], index_a[...], gain[...], lower[...])
    child_o[0] = eta
    child_o[1] = u_x[8 : 8 + CX]
    child_o[2] = v[...]
    parent_o[0] = peta[...]
    parent_o[1] = pu_x[8 : 8 + PX]
    parent_o[2] = pv[...]
    room_o[0] = room[0] + pick(door_t2[...], room_flow(received, windows, face[...]))
    room_o[1] = room[1]
    room_o[2] = room[2]


def sds(*shape, dtype=f32):
    return jax.ShapeDtypeStruct(shape, dtype)


def call(name, kernel, outs, args, scalars=0, scratch=(), us=1):
    spec = pl.BlockSpec(memory_space=pltpu.VMEM)
    return pl.pallas_call(
        kernel,
        out_shape=outs,
        in_specs=[pl.BlockSpec(memory_space=pltpu.SMEM)] * scalars + [spec] * (len(args) - scalars),
        out_specs=jax.tree.map(lambda _: spec, outs),
        scratch_shapes=[pltpu.VMEM((rows, LANES), f32) for rows in scratch],
        compiler_params=pltpu.CompilerParams(vmem_limit_bytes=16 * 2**20),
        cost_estimate=pl.CostEstimate(flops=1000000 * us, bytes_accessed=1000000 * us, transcendentals=0),
        name=name,
    )(*args)


def shifts(up, dn, axis):
    count = lax.axis_size(axis)
    before = lax.ppermute(dn, axis, [(i, i + 1) for i in range(count - 1)])
    after = lax.ppermute(up, axis, [(i + 1, i) for i in range(count - 1)])
    return before, after


def body(
    parent_state,
    parent_depth,
    child_state,
    child_depth,
    child_wet,
    interior_state,
    interior_wet,
    parent_anchor,
    open_row,
    open_col,
    open_owner,
    open_valid,
    open_conduct,
    door_rows,
):
    block, tall = sds(CX, LANES), sds(CX + 16, LANES)
    pblock, ptall = sds(PX, LANES), sds(PX + 16, LANES)
    grid, tile8, tile16 = sds(SLOTS, LANES), sds(8, LANES), sds(16, LANES)
    rooms = sds(3, CX, LANES)
    my_tile = lax.axis_index("tile").astype(i32)
    scal = jnp.stack([my_tile, parent_anchor[0, 0, 0], parent_anchor[0, 0, 1], my_tile])

    def flat(values):
        return values.reshape(1, -1)

    up, dn, side = call(
        "edges",
        edges_kernel,
        [tile16] * 3,
        [
            parent_state, parent_depth, child_state, child_depth, child_wet, flat(open_row), flat(open_col),
            flat(open_owner), open_owner, flat(open_valid), flat(open_conduct),
        ],
    )
    above0, below0 = shifts(up, dn, "district")
    left0, right0 = shifts(side, side, "tile")
    row2, row_t2, index_s, index_a, gain, lower, fixed, door2, door_t2, room, face, reply = call(
        "setup",
        setup_kernel,
        [
            sds(SLOTS, LANES, dtype=bf16), sds(CX, 2 * SLOTS, dtype=bf16), sds(SLOTS, LANES, dtype=i32),
            sds(SLOTS, LANES, dtype=i32), grid, grid, grid, sds(SLOTS, LANES, dtype=bf16),
            sds(CX, 2 * SLOTS, dtype=bf16), rooms, grid, grid,
        ],
        [side, door_rows, interior_state, interior_wet],
        scratch=(CX + 16, CX + 16),
        us=4,
    )
    near = call(
        "near",
        near_kernel,
        [
            sds(2 * SLOTS, LANES, dtype=bf16), sds(CX, 4 * SLOTS, dtype=bf16), sds(2 * SLOTS, LANES, dtype=i32),
            sds(2 * SLOTS, LANES),
        ],
        [left0, right0],
        us=3,
    )
    outs = [block, tall, block, block, pblock, ptall, pblock, pblock, grid, grid]
    for step in range(STEPS):
        with_step = lambda *refs, step=step: send_kernel(step, *refs)
        if step == 0:
            args = [
                scal, parent_state, parent_depth, child_state, child_depth, child_wet, above0, below0, left0, right0,
                reply, row2, index_s,
            ]
            scratch = (CX + 16,) * 3 + (PX + 16,) * 3
        else:
            args = [
                scal, parent_depth, child_depth, child_wet, above0, below0, left0, right0, reply, row2, index_s,
                above, below, eta, u, v, v_h, eta_h, peta, pu, pv, pv_h, peta_h,
            ]
            scratch = (CX + 16,) * 2 + (PX + 16,) * 2
        eta, u, v, v_h, peta, pu, pv, pv_h, street, outbox = call(
            f"send{step}", with_step, outs, args, scalars=1, scratch=scratch
        )
        inbox = lax.all_to_all(outbox, "tile", split_axis=0, concat_axis=0, tiled=True)
        shared = [scal, inbox, eta, street, row_t2, index_a, gain, lower]
        if step == STEPS - 1:
            return tuple(
                call(
                    "final",
                    final_kernel,
                    [sds(3, PX, LANES), rooms, rooms],
                    shared + [u, v, peta, pu, pv, room, face, door_t2],
                    scalars=1,
                )
            )
        eta, up, dn, windows = call(
            f"street{step}", street_kernel, [block, tile8, tile8, tile8], shared + [peta], scalars=1
        )
        above, below = shifts(up, dn, "district")
        with_step = lambda *refs, step=step: room_kernel(step + 1, *refs)
        room, face, reply, eta_h, peta_h = call(
            f"room{step}",
            with_step,
            [rooms, grid, grid, block, pblock],
            [scal, inbox, windows, room, interior_wet, face, door2, door_t2, fixed, *near],
            scalars=1,
            scratch=(CX + 16, CX + 16),
            us=3,
        )


def solution(mesh):
    return jax.shard_map(
        body,
        mesh=mesh,
        in_specs=(
            P(None, "district", "tile"),
            P("district", "tile"),
            P(None, "district", "tile"),
            P("district", "tile"),
            P(None, "district", "tile"),
            P(None, ("district", "tile"), None),
            P(None, ("district", "tile"), None),
            P("district", None, None),
            P(("district", "tile")),
            P(("district", "tile")),
            P(("district", "tile"), None),
            P(("district", "tile")),
            P(("district", "tile")),
            P(("district", "tile"), None),
        ),
        out_specs=(
            P(None, "district", "tile"),
            P(None, "district", "tile"),
            P(None, ("district", "tile"), None),
        ),
        check_vma=False,
    )
```

time: 469 us -> 106 us (0.23)
  starting transfers between devices: 147 us -> 30.8 us
  local copies, waits for them, and re-layouts: 91 us -> 6.47 us
  other arithmetic: 75 us -> 1.37 us
  waiting for transfers between devices: 72.2 us -> 9.63 us
  blocking collectives: 75.6 us -> 42.4 us
  Pallas kernels: 0 us -> 14 us
  between operations: 6.22 us -> 0.91 us
    all_gather x4 -> x0, blocking collectives: 75.6 us -> none  [body(): district_rows = lax.all_gather(surface, 'tile', axis=1, tiled=True)]
    ppermute x32 -> x10, starting transfers between devices: 98.9 us -> 30.8 us  [the longest x5 20.5 us: shifts(): before = lax.ppermute(dn, axis, [(i, i + 1) for i in range(count - 1)])]
    scatter-add x8 -> x0, other arithmetic: 63.8 us -> none  [the longest x4 58.4 us: body(): flat_level = flat_level.at[cell_ids].add(-returned[owners, slot_of])]
    gather x20 -> x0, local copies, waits for them, and re-layouts: 53.4 us -> none  [the longest x8 47.4 us: body(): street = place_rows(flat_level[cell_ids], owners, slot_of, tile_count)]
    all_to_all x9 -> x0, starting transfers between devices: 48 us -> none  [the longest x4 27.3 us: body(): lax.all_to_all(street.reshape(tile_count, CAP * SEG), 'tile', split_axis=...]
    all_to_all x0 -> x4, blocking collectives: none -> 42.4 us  [body(): lax.all_to_all(outbox, 'tile', split_axis=0, concat_axis=0, tiled=True)]
    all_to_all x9 -> x0, waiting for transfers between devices: 38.8 us -> none  [the longest x4 21.7 us: body(): lax.all_to_all(flux_back.reshape(tile_count, CAP * SEG), 'tile', split_ax...]
    ppermute x32 -> x10, waiting for transfers between devices: 33.4 us -> 9.63 us  [the longest x5 9.61 us: shifts(): after = lax.ppermute(up, axis, [(i + 1, i) for i in range(count - 1)])]
  transfers between devices with their start and end apart: 41 -> 10, of which waited for: 16 -> 4; matrix products, arithmetic and copies ran while one was open for 7% -> 2% of each run, Pallas kernels for 0% -> 5%
where the time goes in v1:
time: 106 us
  blocking collectives  42.4 us (40%)
  starting transfers between devices  30.8 us (29%)
  Pallas kernels  14 us (13%)
  waiting for transfers between devices  9.63 us (9%)
  local copies, waits for them, and re-layouts  6.47 us (6%)
  other arithmetic  1.37 us (1%)
    all_to_all x4, blocking collectives, body(): lax.all_to_all(outbox, 'tile', split_axis=0, concat_axis=0, tiled=True)  42.4 us
    ppermute x5, starting transfers between devices, shifts(): before = lax.ppermute(dn, axis, [(i, i + 1) for i in range(count - 1)])  20.5 us
    pallas_call x14, Pallas kernels, call(): pl.pallas_call(kernel, out_shape=outs, in_specs=[pl.BlockSpec(memory_spac...  14 us
    ppermute x5, starting transfers between devices, shifts(): after = lax.ppermute(up, axis, [(i + 1, i) for i in range(count - 1)])  10.3 us
    ppermute x5, waiting for transfers between devices, shifts(): after = lax.ppermute(up, axis, [(i + 1, i) for i in range(count - 1)])  9.61 us
    unnamed x35, local copies, waits for them, and re-layouts  5.95 us
  transfers between devices with their start and end apart: 10, of which 4 were waited for; matrix products, arithmetic and copies ran while one was open for 2% of the time, Pallas kernels for 5%

profile of v1, /device:TPU:1, one launch (start us, length us, event | category | flops | bytes accessed | tf_op | source)
XLA Modules:
  0.0 105.5 jit_solution(4182983493427118853)
XLA Ops:
  0.7 0.8 copy.17.owner_t
  1.4 0.0 copy-start.11
  1.5 0.7 copy-done.6
  2.1 0.9 copy-done
  3.0 0.9 copy-done.4
  3.9 0.7 copy-done.7
  4.6 0.7 copy-done.13
  5.3 0.7 copy-done.14
  6.0 0.1 edges.1
  6.1 5.1 %collective-permute-start.3 = (f32[16,128]{1,0:T(8,128)S(1)}, f32[16,128]{1,0:T(8,128)S(1)}, u32[]{:S(2)}, u32[]{:S(2)}) collective-permute-start(f32[16,128]{1,0:T(8,128)S(1)} %get-tuple-element.89.side), channel_id=1, source_target_pairs={{1,0},{2,1},{3,2},{4,3},{5,4},{6,5},{7,6},{8,7},{9,8},{10,9},{11,1... | collective-permute-start | bytes 24584 | tf_op jit(solution)/shard_map/ppermute | solution.py:471
  11.3 1.9 %collective-permute-start.2 = (f32[16,128]{1,0:T(8,128)S(1)}, f32[16,128]{1,0:T(8,128)S(1)}, u32[]{:S(2)}, u32[]{:S(2)}) collective-permute-start(f32[16,128]{1,0:T(8,128)S(1)} %get-tuple-element.89.side), channel_id=1, source_target_pairs={{0,1},{1,2},{2,3},{3,4},{4,5},{5,6},{6,7},{7,8},{8,9},{9,10},{10,1... | collective-permute-start | bytes 24584 | tf_op jit(solution)/shard_map/ppermute | solution.py:470
  13.2 4.3 %collective-permute-start = (f32[16,128]{1,0:T(8,128)S(1)}, f32[16,128]{1,0:T(8,128)S(1)}, u32[]{:S(2)}, u32[]{:S(2)}) collective-permute-start(f32[16,128]{1,0:T(8,128)S(1)} %get-tuple-element.87), channel_id=1, source_target_pairs={{0,16},{16,32},{32,48},{48,64},{64,80},{80,96},{96,112},{112,128},... | collective-permute-start | bytes 24584 | tf_op jit(solution)/shard_map/ppermute | solution.py:470
  17.5 1.3 %collective-permute-start.1 = (f32[16,128]{1,0:T(8,128)S(1)}, f32[16,128]{1,0:T(8,128)S(1)}, u32[]{:S(2)}, u32[]{:S(2)}) collective-permute-start(f32[16,128]{1,0:T(8,128)S(1)} %get-tuple-element.88), channel_id=1, source_target_pairs={{16,0},{32,16},{48,32},{64,48},{80,64},{96,80},{112,96},{128,112},... | collective-permute-start | bytes 24584 | tf_op jit(solution)/shard_map/ppermute | solution.py:471
  18.8 0.0 copy-start.16
  18.8 0.0 copy-start.15
  18.9 0.0 copy-start.1
  18.9 0.6 copy-done.16
  19.5 0.5 fusion
  20.0 1.4 %pad_add_fusion.refs_0_.scal = s32[4]{0:T(128)S(1)} fusion(s32[1]{0:T(128)} %bitcast, s32[1]{0:T(128)} %bitcast.2, s32[1]{0:T(128)} %bitcast.1), kind=kLoop, calls=%fused_computation | loop fusion | flops 12 | bytes 28 | tf_op jit(solution)/shard_map/stack | solution.py:496
  21.4 0.0 copy-start.5
  21.4 0.0 copy-start.8
  21.4 0.7 setup.1
  22.1 2.6 %collective-permute-done.1.refs_7_.refs_5_ = f32[16,128]{1,0:T(8,128)S(1)} collective-permute-done((f32[16,128]{1,0:T(8,128)S(1)}, f32[16,128]{1,0:T(8,128)S(1)}, u32[]{:S(2)}, u32[]{:S(2)}) %collective-permute-start.1) | collective-permute-done | bytes 8224 | tf_op jit(solution)/shard_map/ppermute | solution.py:471
  24.8 1.1 %send0.1 = (f32[64,128]{1,0:T(8,128)S(1)}, f32[80,128]{1,0:T(8,128)S(1)}, f32[64,128]{1,0:T(8,128)S(1)}, f32[64,128]{1,0:T(8,128)S(1)}, f32[16,128]{1,0:T(8,128)...) custom-call(s32[4]{0:T(128)S(1)} %pad_add_fusion.refs_0_.scal, ...), custom_call_target="tpu_custom_call" | custom-call | flops 1000000 | bytes 1000000 | tf_op jit(solution)/shard_map/send0/pallas_call | solution.py:456
  25.9 12.0 %all_to_all.44 = f32[16,8,128]{2,1,0:T(8,128)S(1)} all-to-all(f32[16,8,128]{2,1,0:T(8,128)S(1)} %bitcast.26), channel_id=1, replica_groups=mesh['district'=16,'tile'=16] {'tile'}, dimensions={0} | all-to-all | bytes 131072 | tf_op jit(solution)/shard_map/all_to_all | solution.py:552
  37.8 0.8 street0.1
  38.6 5.5 %collective-permute-start.4 = (f32[8,128]{1,0:T(8,128)S(1)}, f32[8,128]{1,0:T(8,128)S(1)}, u32[]{:S(2)}, u32[]{:S(2)}) collective-permute-start(f32[8,128]{1,0:T(8,128)S(1)} %get-tuple-element.112), channel_id=1, source_target_pairs={{0,16},{16,32},{32,48},{48,64},{64,80},{80,96},{96,112},{112,128},... | collective-permute-start | bytes 12296 | tf_op jit(solution)/shard_map/ppermute | solution.py:470
  44.1 1.3 %collective-permute-start.5 = (f32[8,128]{1,0:T(8,128)S(1)}, f32[8,128]{1,0:T(8,128)S(1)}, u32[]{:S(2)}, u32[]{:S(2)}) collective-permute-start(f32[8,128]{1,0:T(8,128)S(1)} %get-tuple-element.113), channel_id=1, source_target_pairs={{16,0},{32,16},{48,32},{64,48},{80,64},{96,80},{112,96},{128,112},... | collective-permute-start | bytes 12296 | tf_op jit(solution)/shard_map/ppermute | solution.py:471
  45.4 0.4 near.1
  45.7 1.5 %room0.1 = (f32[3,64,128]{2,1,0:T(8,128)S(1)}, f32[128,128]{1,0:T(8,128)S(1)}, f32[128,128]{1,0:T(8,128)S(1)}, f32[64,128]{1,0:T(8,128)S(1)}, f32[16,128]{1,0:T(8,128)S(1)}) custom-call(s32[4]{0:T(128)S(1)} %pad_add_fusion.refs_0_.scal, f32[128,128]{1,0:T(8,128)S(1)} %bitcast.17, f32[8,128]{1,0:T(8,128)S(1)} %get-tuple-element.101.refs_2_, ...), custom_call_target="tpu_custom_call" | custom-call | flops 3000000 | bytes 3000000 | tf_op jit(solution)/shard_map/room0/pallas_call | solution.py:456
  47.2 2.1 %collective-permute-done.5.refs_12_ = f32[8,128]{1,0:T(8,128)S(1)} collective-permute-done((f32[8,128]{1,0:T(8,128)S(1)}, f32[8,128]{1,0:T(8,128)S(1)}, u32[]{:S(2)}, u32[]{:S(2)}) %collective-permute-start.5) | collective-permute-done | bytes 4128 | tf_op jit(solution)/shard_map/ppermute | solution.py:471
  49.4 1.0 send1.1
  50.3 10.1 %all_to_all.45 = f32[16,8,128]{2,1,0:T(8,128)S(1)} all-to-all(f32[16,8,128]{2,1,0:T(8,128)S(1)} %bitcast.24), channel_id=1, replica_groups=mesh['district'=16,'tile'=16] {'tile'}, dimensions={0} | all-to-all | bytes 131072 | tf_op jit(solution)/shard_map/all_to_all | solution.py:552
  60.4 0.8 street1.1
  61.2 5.5 %collective-permute-start.6 = (f32[8,128]{1,0:T(8,128)S(1)}, f32[8,128]{1,0:T(8,128)S(1)}, u32[]{:S(2)}, u32[]{:S(2)}) collective-permute-start(f32[8,128]{1,0:T(8,128)S(1)} %get-tuple-element.131), channel_id=1, source_target_pairs={{0,16},{16,32},{32,48},{48,64},{64,80},{80,96},{96,112},{112,128},... | collective-permute-start | bytes 12296 | tf_op jit(solution)/shard_map/ppermute | solution.py:470
  66.8 1.3 %collective-permute-start.7 = (f32[8,128]{1,0:T(8,128)S(1)}, f32[8,128]{1,0:T(8,128)S(1)}, u32[]{:S(2)}, u32[]{:S(2)}) collective-permute-start(f32[8,128]{1,0:T(8,128)S(1)} %get-tuple-element.132), channel_id=1, source_target_pairs={{16,0},{32,16},{48,32},{64,48},{80,64},{96,80},{112,96},{128,112},... | collective-permute-start | bytes 12296 | tf_op jit(solution)/shard_map/ppermute | solution.py:471
  68.1 1.5 %room1.1 = (f32[3,64,128]{2,1,0:T(8,128)S(1)}, f32[128,128]{1,0:T(8,128)S(1)}, f32[128,128]{1,0:T(8,128)S(1)}, f32[64,128]{1,0:T(8,128)S(1)}, f32[16,128]{1,0:T(8,128)S(1)}) custom-call(s32[4]{0:T(128)S(1)} %pad_add_fusion.refs_0_.scal, f32[128,128]{1,0:T(8,128)S(1)} %bitcast.21, f32[8,128]{1,0:T(8,128)S(1)} %get-tuple-element.127.refs_2_, ...), custom_call_target="tpu_custom_call" | custom-call | flops 3000000 | bytes 3000000 | tf_op jit(solution)/shard_map/room1/pallas_call | solution.py:456
  69.6 2.4 %collective-permute-done.7.refs_12_ = f32[8,128]{1,0:T(8,128)S(1)} collective-permute-done((f32[8,128]{1,0:T(8,128)S(1)}, f32[8,128]{1,0:T(8,128)S(1)}, u32[]{:S(2)}, u32[]{:S(2)}) %collective-permute-start.7) | collective-permute-done | bytes 4128 | tf_op jit(solution)/shard_map/ppermute | solution.py:471
  72.0 1.0 send2.1
  73.0 10.2 %all_to_all.46 = f32[16,8,128]{2,1,0:T(8,128)S(1)} all-to-all(f32[16,8,128]{2,1,0:T(8,128)S(1)} %bitcast.25), channel_id=1, replica_groups=mesh['district'=16,'tile'=16] {'tile'}, dimensions={0} | all-to-all | bytes 131072 | tf_op jit(solution)/shard_map/all_to_all | solution.py:552
  83.2 0.8 street2.1
  83.9 3.2 %collective-permute-start.8 = (f32[8,128]{1,0:T(8,128)S(1)}, f32[8,128]{1,0:T(8,128)S(1)}, u32[]{:S(2)}, u32[]{:S(2)}) collective-permute-start(f32[8,128]{1,0:T(8,128)S(1)} %get-tuple-element.150), channel_id=1, source_target_pairs={{0,16},{16,32},{32,48},{48,64},{64,80},{80,96},{96,112},{112,128},... | collective-permute-start | bytes 12296 | tf_op jit(solution)/shard_map/ppermute | solution.py:470
  87.2 1.3 %collective-permute-start.9 = (f32[8,128]{1,0:T(8,128)S(1)}, f32[8,128]{1,0:T(8,128)S(1)}, u32[]{:S(2)}, u32[]{:S(2)}) collective-permute-start(f32[8,128]{1,0:T(8,128)S(1)} %get-tuple-element.151), channel_id=1, source_target_pairs={{16,0},{32,16},{48,32},{64,48},{80,64},{96,80},{112,96},{128,112},... | collective-permute-start | bytes 12296 | tf_op jit(solution)/shard_map/ppermute | solution.py:471
  88.5 1.5 %room2.1 = (f32[3,64,128]{2,1,0:T(8,128)S(1)}, f32[128,128]{1,0:T(8,128)S(1)}, f32[128,128]{1,0:T(8,128)S(1)}, f32[64,128]{1,0:T(8,128)S(1)}, f32[16,128]{1,0:T(8,128)S(1)}) custom-call(s32[4]{0:T(128)S(1)} %pad_add_fusion.refs_0_.scal, f32[128,128]{1,0:T(8,128)S(1)} %bitcast.19, f32[8,128]{1,0:T(8,128)S(1)} %get-tuple-element.146.refs_2_, ...), custom_call_target="tpu_custom_call" | custom-call | flops 3000000 | bytes 3000000 | tf_op jit(solution)/shard_map/room2/pallas_call | solution.py:456
  90.0 2.4 %collective-permute-done.9.refs_12_ = f32[8,128]{1,0:T(8,128)S(1)} collective-permute-done((f32[8,128]{1,0:T(8,128)S(1)}, f32[8,128]{1,0:T(8,128)S(1)}, u32[]{:S(2)}, u32[]{:S(2)}) %collective-permute-start.9) | collective-permute-done | bytes 4128 | tf_op jit(solution)/shard_map/ppermute | solution.py:471
  92.4 1.3 %send3.1 = (f32[64,128]{1,0:T(8,128)S(1)}, f32[80,128]{1,0:T(8,128)S(1)}, f32[64,128]{1,0:T(8,128)S(1)}, f32[64,128]{1,0:T(8,128)}, f32[16,128]{1,0:T(8,128)S(1)...) custom-call(s32[4]{0:T(128)S(1)} %pad_add_fusion.refs_0_.scal, ...), custom_call_target="tpu_custom_call" | custom-call | flops 1000000 | bytes 1000000 | tf_op jit(solution)/shard_map/send3/pallas_call | solution.py:456
  93.8 10.2 %all_to_all.47 = f32[16,8,128]{2,1,0:T(8,128)S(1)} all-to-all(f32[16,8,128]{2,1,0:T(8,128)S(1)} %bitcast.23), channel_id=1, replica_groups=mesh['district'=16,'tile'=16] {'tile'}, dimensions={0} | all-to-all | bytes 131072 | tf_op jit(solution)/shard_map/all_to_all | solution.py:552
  104.0 1.6 %final.1 = (f32[3,16,128]{2,1,0:T(8,128)}, f32[3,64,128]{2,1,0:T(8,128)}, f32[3,64,128]{2,1,0:T(8,128)}) custom-call(s32[4]{0:T(128)S(1)} %pad_add_fusion.refs_0_.scal, f32[128,128]{1,0:T(8,128)S(1)} %bitcast.22, f32[64,128]{1,0:T(8,128)S(1)} %get-tuple-element.162.eta, f32[128,128]{1,0:T(8,128)S(1)} %get-tuple-element.163.street, ...), custom_call_target="tpu_custom_call" | custom-call | flops 1000000 | bytes 1000000 | tf_op jit(solution)/shard_map/final/pallas_call | solution.py:456
  (27 shorter events, 0.1 us)
Async XLA Ops:
  0.6 0.8 copy-start.3
  0.6 0.8 copy-start.12
  1.4 0.7 copy-start.6
  1.4 0.7 copy-start.10
  1.4 0.7 copy-start.11
  2.1 0.9 copy-start
  3.0 0.9 copy-start.4
  3.9 0.7 copy-start.7
  4.6 0.7 copy-start.13
  5.3 0.7 copy-start.14
  6.0 15.4 %copy-start.2 = (s32[4,64,128]{2,1,0:T(8,128)S(1)}, s32[4,64,128]{2,1,0:T(8,128)}, u32[]{:S(2)}) copy-start(s32[4,64,128]{2,1,0:T(8,128)} %refs_4_.7) | copy-start | bytes 393220
  6.0 15.4 %copy-start.9 = (f32[3,64,128]{2,1,0:T(8,128)S(1)}, f32[3,64,128]{2,1,0:T(8,128)}, u32[]{:S(2)}) copy-start(f32[3,64,128]{2,1,0:T(8,128)} %room.1) | copy-start | bytes 294916
  6.1 18.7 %collective-permute-start.3 = (f32[16,128]{1,0:T(8,128)S(1)}, f32[16,128]{1,0:T(8,128)S(1)}, u32[]{:S(2)}, u32[]{:S(2)}) collective-permute-start(f32[16,128]{1,0:T(8,128)S(1)} %get-tuple-element.89.side), channel_id=1, source_target_pairs={{1,0},{2,1},{3,2},{4,3},{5,4},{6,5},{7,6},{8,7},{9,8},{10,9},{11,1... | collective-permute-start | bytes 24584 | tf_op jit(solution)/shard_map/ppermute | solution.py:471
  11.3 13.5 %collective-permute-start.2 = (f32[16,128]{1,0:T(8,128)S(1)}, f32[16,128]{1,0:T(8,128)S(1)}, u32[]{:S(2)}, u32[]{:S(2)}) collective-permute-start(f32[16,128]{1,0:T(8,128)S(1)} %get-tuple-element.89.side), channel_id=1, source_target_pairs={{0,1},{1,2},{2,3},{3,4},{4,5},{5,6},{6,7},{7,8},{8,9},{9,10},{10,1... | collective-permute-start | bytes 24584 | tf_op jit(solution)/shard_map/ppermute | solution.py:470
  13.2 8.9 %collective-permute-start = (f32[16,128]{1,0:T(8,128)S(1)}, f32[16,128]{1,0:T(8,128)S(1)}, u32[]{:S(2)}, u32[]{:S(2)}) collective-permute-start(f32[16,128]{1,0:T(8,128)S(1)} %get-tuple-element.87), channel_id=1, source_target_pairs={{0,16},{16,32},{32,48},{48,64},{64,80},{80,96},{96,112},{112,128},... | collective-permute-start | bytes 24584 | tf_op jit(solution)/shard_map/ppermute | solution.py:470
  17.5 7.2 %collective-permute-start.1 = (f32[16,128]{1,0:T(8,128)S(1)}, f32[16,128]{1,0:T(8,128)S(1)}, u32[]{:S(2)}, u32[]{:S(2)}) collective-permute-start(f32[16,128]{1,0:T(8,128)S(1)} %get-tuple-element.88), channel_id=1, source_target_pairs={{16,0},{32,16},{48,32},{64,48},{80,64},{96,80},{112,96},{128,112},... | collective-permute-start | bytes 24584 | tf_op jit(solution)/shard_map/ppermute | solution.py:471
  18.8 0.7 copy-start.16
  18.8 2.6 %copy-start.15 = (s32[1,128]{1,0:T(1,128)S(1)}, s32[1,128]{1,0:T(1,128)}, u32[]{:S(2)}) copy-start(s32[1,128]{1,0:T(1,128)} %door.1) | copy-start | bytes 1540
  18.9 5.9 %copy-start.1 = (s32[4,64,128]{2,1,0:T(8,128)S(1)}, s32[4,64,128]{2,1,0:T(8,128)}, u32[]{:S(2)}) copy-start(s32[4,64,128]{2,1,0:T(8,128)} %refs_3_.7) | copy-start | bytes 393220
  21.4 3.4 %copy-start.5 = (f32[3,64,128]{2,1,0:T(8,128)S(1)}, f32[3,64,128]{2,1,0:T(8,128)}, u32[]{:S(2)}) copy-start(f32[3,64,128]{2,1,0:T(8,128)} %refs_3_.4) | copy-start | bytes 294916
  21.4 3.3 %copy-start.8 = (f32[3,16,128]{2,1,0:T(8,128)S(1)}, f32[3,16,128]{2,1,0:T(8,128)}, u32[]{:S(2)}) copy-start(f32[3,16,128]{2,1,0:T(8,128)} %refs_1_.4) | copy-start | bytes 73732
  38.6 8.7 %collective-permute-start.4 = (f32[8,128]{1,0:T(8,128)S(1)}, f32[8,128]{1,0:T(8,128)S(1)}, u32[]{:S(2)}, u32[]{:S(2)}) collective-permute-start(f32[8,128]{1,0:T(8,128)S(1)} %get-tuple-element.112), channel_id=1, source_target_pairs={{0,16},{16,32},{32,48},{48,64},{64,80},{80,96},{96,112},{112,128},... | collective-permute-start | bytes 12296 | tf_op jit(solution)/shard_map/ppermute | solution.py:470
  44.1 5.3 %collective-permute-start.5 = (f32[8,128]{1,0:T(8,128)S(1)}, f32[8,128]{1,0:T(8,128)S(1)}, u32[]{:S(2)}, u32[]{:S(2)}) collective-permute-start(f32[8,128]{1,0:T(8,128)S(1)} %get-tuple-element.113), channel_id=1, source_target_pairs={{16,0},{32,16},{48,32},{64,48},{80,64},{96,80},{112,96},{128,112},... | collective-permute-start | bytes 12296 | tf_op jit(solution)/shard_map/ppermute | solution.py:471
  61.2 8.4 %collective-permute-start.6 = (f32[8,128]{1,0:T(8,128)S(1)}, f32[8,128]{1,0:T(8,128)S(1)}, u32[]{:S(2)}, u32[]{:S(2)}) collective-permute-start(f32[8,128]{1,0:T(8,128)S(1)} %get-tuple-element.131), channel_id=1, source_target_pairs={{0,16},{16,32},{32,48},{48,64},{64,80},{80,96},{96,112},{112,128},... | collective-permute-start | bytes 12296 | tf_op jit(solution)/shard_map/ppermute | solution.py:470
  66.8 5.3 %collective-permute-start.7 = (f32[8,128]{1,0:T(8,128)S(1)}, f32[8,128]{1,0:T(8,128)S(1)}, u32[]{:S(2)}, u32[]{:S(2)}) collective-permute-start(f32[8,128]{1,0:T(8,128)S(1)} %get-tuple-element.132), channel_id=1, source_target_pairs={{16,0},{32,16},{48,32},{64,48},{80,64},{96,80},{112,96},{128,112},... | collective-permute-start | bytes 12296 | tf_op jit(solution)/shard_map/ppermute | solution.py:471
  83.9 6.1 %collective-permute-start.8 = (f32[8,128]{1,0:T(8,128)S(1)}, f32[8,128]{1,0:T(8,128)S(1)}, u32[]{:S(2)}, u32[]{:S(2)}) collective-permute-start(f32[8,128]{1,0:T(8,128)S(1)} %get-tuple-element.150), channel_id=1, source_target_pairs={{0,16},{16,32},{32,48},{48,64},{64,80},{80,96},{96,112},{112,128},... | collective-permute-start | bytes 12296 | tf_op jit(solution)/shard_map/ppermute | solution.py:470
  87.2 5.3 %collective-permute-start.9 = (f32[8,128]{1,0:T(8,128)S(1)}, f32[8,128]{1,0:T(8,128)S(1)}, u32[]{:S(2)}, u32[]{:S(2)}) collective-permute-start(f32[8,128]{1,0:T(8,128)S(1)} %get-tuple-element.151), channel_id=1, source_target_pairs={{16,0},{32,16},{48,32},{64,48},{80,64},{96,80},{112,96},{128,112},... | collective-permute-start | bytes 12296 | tf_op jit(solution)/shard_map/ppermute | solution.py:471

commit v2 on v1

--- a/solution.py
+++ b/solution.py
@@ -158,7 +158,10 @@
 
 def slots_of(side):
     shape = (SLOTS, LANES)
-    held = sub(shape).astype(f32) == side[8:9]
+    owner = jnp.broadcast_to(side[8:9], shape)
+    earlier = (jnp.transpose(owner) == owner) & (sub(shape) < lane(shape))
+    rank = jnp.sum(jnp.where(earlier, 1.0, 0.0), axis=0, keepdims=True)
+    held = sub(shape).astype(f32) == jnp.where(side[8:9] >= 0, side[8:9] * CAP + rank, -1.0)
 
     def take(values):
         return jnp.sum(jnp.where(held, values, 0.0), axis=1, keepdims=True)
@@ -168,11 +171,21 @@
 
 
 def edges_kernel(
-    parent, parent_depth, child, child_depth, child_wet, row, col, owner, owner_t, valid, conduct, up, dn, side
+    parent_i, parent_depth_i, child_i, child_depth_i, child_wet_i, row_i, col_i, owner_i, valid_i, conduct_i, up, dn, side,
+    parent, parent_depth, child, child_depth, child_wet, row, col, owner, valid, conduct, done,
 ):
+    pairs = [
+        (child_i, child), (child_depth_i, child_depth), (child_wet_i, child_wet), (parent_i, parent),
+        (parent_depth_i, parent_depth), (row_i, row), (col_i, col), (owner_i, owner), (valid_i, valid), (conduct_i, conduct),
+    ]
+    copies = [pltpu.make_async_copy(src, dst, done.at[k]) for k, (src, dst) in enumerate(pairs)]
+    for copy in copies:
+        copy.start()
     up[...] = jnp.zeros((16, LANES), f32)
     dn[...] = jnp.zeros((16, LANES), f32)
     side[...] = jnp.zeros((16, LANES), f32)
+    for copy in copies:
+        copy.wait()
     eta = child[0]
     packed = pack4(jnp.zeros((8, LANES), f32), eta, 0)
     packed = pack2(packed, child[2], 32)
@@ -197,10 +210,8 @@
     packed = pack2(packed, parent_depth[...], 124)
     side[0:8] = packed
     count = owner.shape[1]
-    earlier = (owner_t[...] == owner[...]) & (sub((count, count)) < lane((count, count)))
-    rank = jnp.sum(jnp.where(earlier, 1.0, 0.0), axis=0, keepdims=True)
     side[8:9] = jnp.full((1, LANES), -1.0, f32)
-    side[8:9, 0:count] = owner[...].astype(f32) * CAP + rank
+    side[8:9, 0:count] = owner[...].astype(f32)
     side[9:10, 0:count] = row[...].astype(f32)
     side[10:11, 0:count] = col[...].astype(f32)
     side[11:12, 0:count] = conduct[...] * valid[...].astype(f32)
@@ -261,25 +272,32 @@
     row_t2[...] = jnp.concatenate(turned + turned, 1)
 
 
+def gate(there, cells):
+    return jnp.where(there, cells, 0.0)
+
+
 def send_kernel(step, *refs):
+    scal = refs[0]
+    has_left, has_right = scal[0] > 0, scal[0] < TILES - 1
+    has_above, has_below = scal[3] > 0, scal[3] < scal[4] - 1
     if step == 0:
         (
             scal, parent, parent_depth, child, child_depth, child_wet, above0, below0, left0, right0, reply, row2, index_s,
             eta_o, u_o, v_o, vh_o, peta_o, pu_o, pv_o, pvh_o, street_o, out, eta_x, flux_x, u_x, peta_x, pflux_x, pu_x,
         ) = refs
         u_x[8 : 8 + CX] = child[1]
-        u_x[7:8] = above0[2:3]
-        u_x[8 + CX : 9 + CX] = below0[2:3]
+        u_x[7:8] = gate(has_above, above0[2:3])
+        u_x[8 + CX : 9 + CX] = gate(has_below, below0[2:3])
         pu_x[8 : 8 + PX] = parent[1]
-        pu_x[7:8] = above0[9:10]
-        pu_x[8 + PX : 9 + PX] = below0[9:10]
+        pu_x[7:8] = gate(has_above, above0[9:10])
+        pu_x[8 + PX : 9 + PX] = gate(has_below, below0[9:10])
         eta_x[8 : 8 + CX] = child[0]
         peta_x[8 : 8 + PX] = parent[0]
-        eta_x[6:8] = above0[0:2]
-        eta_x[8 + CX : 10 + CX] = below0[0:2]
-        peta_x[6:8] = above0[7:9]
-        peta_x[8 + PX : 10 + PX] = below0[7:9]
-        left, right = left0[0:8], right0[0:8]
+        eta_x[6:8] = gate(has_above, above0[0:2])
+        eta_x[8 + CX : 10 + CX] = gate(has_below, below0[0:2])
+        peta_x[6:8] = gate(has_above, above0[7:9])
+        peta_x[8 + PX : 10 + PX] = gate(has_below, below0[7:9])
+        left, right = gate(has_left, left0[0:8]), gate(has_right, right0[0:8])
         v, v_h = child[2], unpack2(left, right, 32, 8)
         eta_h = unpack4(left, right, 0, 8)
         pv, pv_h = parent[2], unpack2(left, right, 120, 2)
@@ -292,21 +310,23 @@
         ) = refs
         eta_x[8 : 8 + CX] = eta_i[...]
         peta_x[8 : 8 + PX] = peta_i[...]
-        eta_x[6:8] = above[0:2]
-        eta_x[8 + CX : 10 + CX] = below[0:2]
-        peta_x[6:8] = above[2:4]
-        peta_x[8 + PX : 10 + PX] = below[2:4]
-        left, right = left0[0:8], right0[0:8]
+        eta_x[6:8] = gate(has_above, above[0:2])
+        eta_x[8 + CX : 10 + CX] = gate(has_below, below[0:2])
+        peta_x[6:8] = gate(has_above, above[2:4])
+        peta_x[8 + PX : 10 + PX] = gate(has_below, below[2:4])
+        left, right = gate(has_left, left0[0:8]), gate(has_right, right0[0:8])
         v, v_h, eta_h = v_i[...], vh_i[...], etah_i[...]
         pv, pv_h, peta_h = pv_i[...], pvh_i[...], petah_i[...]
     wet = child_wet[step].astype(f32)
     q = child_depth[...] * wet
-    q_up, q_dn = above0[3 + step : 4 + step], below0[3 + step : 4 + step]
+    q_up = gate(has_above, above0[3 + step : 4 + step])
+    q_dn = gate(has_below, below0[3 + step : 4 + step])
+    pq_up, pq_dn = gate(has_above, above0[10:11]), gate(has_below, below0[10:11])
     q_h = unpack2(left, right, 48 + 16 * step, 8)
     eta, u, u_up, u_dn, v, v_h = advance(eta_x, u_x, v, v_h, eta_h, q, q_up, q_dn, q_h, flux_x, CX)
     street = pick(row2[...], eta)
     peta, pu, pu_up, pu_dn, pv, pv_h = advance(
-        peta_x, pu_x, pv, pv_h, peta_h, parent_depth[...], above0[10:11], below0[10:11], unpack2(left, right, 124, 2), pflux_x, PX
+        peta_x, pu_x, pv, pv_h, peta_h, parent_depth[...], pq_up, pq_dn, unpack2(left, right, 124, 2), pflux_x, PX
     )
     eta_o[...] = eta
     u_o[8 : 8 + CX] = wet * u
@@ -451,15 +471,19 @@
     return jax.ShapeDtypeStruct(shape, dtype)
 
 
-def call(name, kernel, outs, args, scalars=0, scratch=(), us=1):
+def call(name, kernel, outs, args, scalars=0, scratch=(), us=1, own_copies=False):
     spec = pl.BlockSpec(memory_space=pltpu.VMEM)
+    first = pl.BlockSpec(memory_space=pltpu.HBM) if own_copies else spec
+    scratch_shapes = [pltpu.VMEM((rows, LANES), f32) for rows in scratch]
+    if own_copies:
+        scratch_shapes = [pltpu.VMEM(a.shape, a.dtype) for a in args] + [pltpu.SemaphoreType.DMA((len(args),))]
     return pl.pallas_call(
         kernel,
         out_shape=outs,
-        in_specs=[pl.BlockSpec(memory_space=pltpu.SMEM)] * scalars + [spec] * (len(args) - scalars),
+        in_specs=[pl.BlockSpec(memory_space=pltpu.SMEM)] * scalars + [first] * (len(args) - scalars),
         out_specs=jax.tree.map(lambda _: spec, outs),
-        scratch_shapes=[pltpu.VMEM((rows, LANES), f32) for rows in scratch],
-        compiler_params=pltpu.CompilerParams(vmem_limit_bytes=16 * 2**20),
+        scratch_shapes=scratch_shapes,
+        compiler_params=pltpu.CompilerParams(vmem_limit_bytes=(60 if own_copies else 16) * 2**20),
         cost_estimate=pl.CostEstimate(flops=1000000 * us, bytes_accessed=1000000 * us, transcendentals=0),
         name=name,
     )(*args)
@@ -467,8 +491,8 @@
 
 def shifts(up, dn, axis):
     count = lax.axis_size(axis)
-    before = lax.ppermute(dn, axis, [(i, i + 1) for i in range(count - 1)])
-    after = lax.ppermute(up, axis, [(i + 1, i) for i in range(count - 1)])
+    before = lax.ppermute(dn, axis, [(i, (i + 1) % count) for i in range(count)])
+    after = lax.ppermute(up, axis, [((i + 1) % count, i) for i in range(count)])
     return before, after
 
 
@@ -493,7 +517,9 @@
     grid, tile8, tile16 = sds(SLOTS, LANES), sds(8, LANES), sds(16, LANES)
     rooms = sds(3, CX, LANES)
     my_tile = lax.axis_index("tile").astype(i32)
-    scal = jnp.stack([my_tile, parent_anchor[0, 0, 0], parent_anchor[0, 0, 1], my_tile])
+    my_district = lax.axis_index("district").astype(i32)
+    last = jnp.int32(lax.axis_size("district"))
+    scal = jnp.stack([my_tile, parent_anchor[0, 0, 0], parent_anchor[0, 0, 1], my_district, last])
 
     def flat(values):
         return values.reshape(1, -1)
@@ -504,8 +530,9 @@
         [tile16] * 3,
         [
             parent_state, parent_depth, child_state, child_depth, child_wet, flat(open_row), flat(open_col),
-            flat(open_owner), open_owner, flat(open_valid), flat(open_conduct),
+            flat(open_owner), flat(open_valid), flat(open_conduct),
         ],
+        own_copies=True,
     )
     above0, below0 = shifts(up, dn, "district")
     left0, right0 = shifts(side, side, "tile")

time: 106 us -> 88.4 us (0.83)
  waiting for transfers between devices: 9.63 us -> 0.03 us
  local copies, waits for them, and re-layouts: 6.47 us -> 2.56 us
  blocking collectives: 42.4 us -> 40 us
  starting transfers between devices: 30.8 us -> 28.6 us
  Pallas kernels: 14 us -> 16 us
  other arithmetic: 1.37 us -> 0 us
    ppermute x10, waiting for transfers between devices: 9.63 us -> 0.03 us  [the longest x5 0.01 us: shifts(): after = lax.ppermute(up, axis, [((i + 1) % count, i) for i in range(count)])]
    unnamed x35 -> x20, local copies, waits for them, and re-layouts: 5.95 us -> 0.73 us
    all_to_all x4, blocking collectives: 42.4 us -> 40 us  [body(): lax.all_to_all(outbox, 'tile', split_axis=0, concat_axis=0, tiled=True)]
    ppermute x10, starting transfers between devices: 30.8 us -> 28.6 us  [the longest x5 25.3 us: shifts(): after = lax.ppermute(up, axis, [((i + 1) % count, i) for i in range(count)])]
    pallas_call x14, Pallas kernels: 14 us -> 16 us  [call(): pl.pallas_call(kernel, out_shape=outs, in_specs=[pl.BlockSpec(memory_spac...]
    another operation x1 -> x0, other arithmetic: 1.37 us -> none  [body(): jnp.stack([my_tile, parent_anchor[0, 0, 0], parent_anchor[0, 0, 1], my_ti...]
    another operation x0 -> x1, local copies, waits for them, and re-layouts: none -> 1.28 us  [body(): jnp.stack([my_tile, parent_anchor[0, 0, 0], parent_anchor[0, 0, 1], my_di...]
  transfers between devices with their start and end apart: 10 -> 10, of which waited for: 4 -> 0; matrix products, arithmetic and copies ran while one was open for 2% -> 2% of each run, Pallas kernels for 5% -> 7%
where the time goes in v2:
time: 88.4 us; the launch traced here: 88 us
  blocking collectives  40 us (45%)
  starting transfers between devices  28.6 us (32%)
  Pallas kernels  16 us (18%)
  local copies, waits for them, and re-layouts  2.56 us (3%)
    all_to_all x4, blocking collectives, body(): lax.all_to_all(outbox, 'tile', split_axis=0, concat_axis=0, tiled=True)  40 us
    ppermute x5, starting transfers between devices, shifts(): after = lax.ppermute(up, axis, [((i + 1) % count, i) for i in range(count)])  25.3 us
    pallas_call x14, Pallas kernels, call(): pl.pallas_call(kernel, out_shape=outs, in_specs=[pl.BlockSpec(memory_spac...  16 us
    ppermute x5, starting transfers between devices, shifts(): lax.ppermute(dn, axis, [(i, (i + 1) % count) for i in range(count)])  3.29 us
  transfers between devices with their start and end apart: 10, of which 0 were waited for; matrix products, arithmetic and copies ran while one was open for 2% of the time, Pallas kernels for 7%

profile of v2, /device:TPU:1, one launch (start us, length us, event | category | flops | bytes accessed | tf_op | source)
XLA Modules:
  0.0 88.0 jit_solution(3824469951210187607)
XLA Ops:
  0.6 0.0 copy-start.1
  0.6 0.0 copy-start.6
  0.7 0.0 copy-start.5
  0.7 1.8 %edges.1 = (f32[16,128]{1,0:T(8,128)}, f32[16,128]{1,0:T(8,128)}, f32[16,128]{1,0:T(8,128)}) custom-call(f32[3,16,128]{2,1,0:T(8,128)} %refs_1_.4, f32[16,128]{1,0:T(8,128)} %refs_1_.7, f32[3,64,128]{2,1,0:T(8,128)} %refs_3_.4, f32[64,128]{1,0:T(8,128)} %refs_2_.7, s32[4,64,128]{2,1,0:T(8,128)} %refs_3_.7, s32[1,64]{1,0:T(1,128)} %bitcast.28, ...), custom_call_target="tpu_custom_call" | custom-call | flops 1000000 | bytes 1000000 | tf_op jit(solution)/shard_map/edges/pallas_call | solution.py:480
  2.5 3.3 %collective-permute-start.3 = (f32[16,128]{1,0:T(8,128)}, f32[16,128]{1,0:T(8,128)S(1)}, u32[]{:S(2)}, u32[]{:S(2)}) collective-permute-start(f32[16,128]{1,0:T(8,128)} %get-tuple-element.89.side), channel_id=1, source_target_pairs={{1,0},{2,1},{3,2},{4,3},{5,4},{6,5},{7,6},{8,7},{9,8},{10,9},{11,1... | collective-permute-start | bytes 24584 | tf_op jit(solution)/shard_map/ppermute | solution.py:495
  5.8 0.0 collective-permute-start.2
  5.8 2.5 %collective-permute-start = (f32[16,128]{1,0:T(8,128)}, f32[16,128]{1,0:T(8,128)S(1)}, u32[]{:S(2)}, u32[]{:S(2)}) collective-permute-start(f32[16,128]{1,0:T(8,128)} %get-tuple-element.87), channel_id=1, source_target_pairs={{0,16},{16,32},{32,48},{48,64},{64,80},{80,96},{96,112},{112,128},... | collective-permute-start | bytes 24584 | tf_op jit(solution)/shard_map/ppermute | solution.py:494
  8.4 5.2 %collective-permute-start.1 = (f32[16,128]{1,0:T(8,128)}, f32[16,128]{1,0:T(8,128)S(1)}, u32[]{:S(2)}, u32[]{:S(2)}) collective-permute-start(f32[16,128]{1,0:T(8,128)} %get-tuple-element.88), channel_id=1, source_target_pairs={{16,0},{32,16},{48,32},{64,48},{80,64},{96,80},{112,96},{128,112},... | collective-permute-start | bytes 24584 | tf_op jit(solution)/shard_map/ppermute | solution.py:495
  13.6 0.0 copy-done.9
  13.6 0.5 fusion
  14.1 1.3 %stack.11.refs_0_.scal = s32[5]{0:T(128)S(1)} concatenate(s32[1]{0:T(128)} %bitcast, s32[1]{0:T(128)} %bitcast.1, s32[1]{0:T(128)} %bitcast.2, s32[1]{0:T(128)} %bitcast.3, s32[1]{0:T(128)} %constant.8.clone.1), dimensions={0} | concatenate | bytes 40 | tf_op jit(solution)/shard_map/stack | solution.py:522
  15.4 0.0 copy-done.1
  15.4 0.0 copy-done.8
  15.4 0.0 copy-start.7
  15.4 0.7 copy-done.7
  16.1 0.8 setup.1
  17.0 0.0 collective-permute-done.refs_6_.refs_4_
  17.0 0.0 collective-permute-done.1.refs_7_.refs_5_
  17.0 0.0 collective-permute-done.3.refs_9_.right.refs_7_
  17.0 0.0 collective-permute-done.2.refs_8_.left.refs_6_
  17.1 1.1 %send0.1 = (f32[64,128]{1,0:T(8,128)S(1)}, f32[80,128]{1,0:T(8,128)S(1)}, f32[64,128]{1,0:T(8,128)S(1)}, f32[64,128]{1,0:T(8,128)S(1)}, f32[16,128]{1,0:T(8,128)...) custom-call(s32[5]{0:T(128)S(1)} %stack.11.refs_0_.scal, ...), custom_call_target="tpu_custom_call" | custom-call | flops 1000000 | bytes 1000000 | tf_op jit(solution)/shard_map/send0/pallas_call | solution.py:480
  18.1 12.4 %all_to_all.44 = f32[16,8,128]{2,1,0:T(8,128)S(1)} all-to-all(f32[16,8,128]{2,1,0:T(8,128)S(1)} %bitcast.27), channel_id=1, replica_groups=mesh['district'=16,'tile'=16] {'tile'}, dimensions={0} | all-to-all | bytes 131072 | tf_op jit(solution)/shard_map/all_to_all | solution.py:579
  30.5 0.8 street0.1
  31.3 0.4 collective-permute-start.4
  31.7 5.3 %collective-permute-start.5 = (f32[8,128]{1,0:T(8,128)S(1)}, f32[8,128]{1,0:T(8,128)S(1)}, u32[]{:S(2)}, u32[]{:S(2)}) collective-permute-start(f32[8,128]{1,0:T(8,128)S(1)} %get-tuple-element.113), channel_id=1, source_target_pairs={{16,0},{32,16},{48,32},{64,48},{80,64},{96,80},{112,96},{128,112},... | collective-permute-start | bytes 12296 | tf_op jit(solution)/shard_map/ppermute | solution.py:495
  37.0 0.4 near.1
  37.4 1.5 %room0.1 = (f32[3,64,128]{2,1,0:T(8,128)S(1)}, f32[128,128]{1,0:T(8,128)S(1)}, f32[128,128]{1,0:T(8,128)S(1)}, f32[64,128]{1,0:T(8,128)S(1)}, f32[16,128]{1,0:T(8,128)S(1)}) custom-call(s32[5]{0:T(128)S(1)} %stack.11.refs_0_.scal, f32[128,128]{1,0:T(8,128)S(1)} %bitcast.18, f32[8,128]{1,0:T(8,128)S(1)} %get-tuple-element.101.refs_2_, ...), custom_call_target="tpu_custom_call" | custom-call | flops 3000000 | bytes 3000000 | tf_op jit(solution)/shard_map/room0/pallas_call | solution.py:480
  39.0 0.0 collective-permute-done.4.refs_11_
  39.0 0.0 collective-permute-done.5.refs_12_
  39.0 1.0 %send1.1 = (f32[64,128]{1,0:T(8,128)S(1)}, f32[80,128]{1,0:T(8,128)S(1)}, f32[64,128]{1,0:T(8,128)S(1)}, f32[64,128]{1,0:T(8,128)S(1)}, f32[16,128]{1,0:T(8,128)...) custom-call(s32[5]{0:T(128)S(1)} %stack.11.refs_0_.scal, ...), custom_call_target="tpu_custom_call" | custom-call | flops 1000000 | bytes 1000000 | tf_op jit(solution)/shard_map/send1/pallas_call | solution.py:480
  40.0 9.3 %all_to_all.45 = f32[16,8,128]{2,1,0:T(8,128)S(1)} all-to-all(f32[16,8,128]{2,1,0:T(8,128)S(1)} %bitcast.25), channel_id=1, replica_groups=mesh['district'=16,'tile'=16] {'tile'}, dimensions={0} | all-to-all | bytes 131072 | tf_op jit(solution)/shard_map/all_to_all | solution.py:579
  49.3 0.8 street1.1
  50.1 0.3 collective-permute-start.6
  50.4 5.4 %collective-permute-start.7 = (f32[8,128]{1,0:T(8,128)S(1)}, f32[8,128]{1,0:T(8,128)S(1)}, u32[]{:S(2)}, u32[]{:S(2)}) collective-permute-start(f32[8,128]{1,0:T(8,128)S(1)} %get-tuple-element.132), channel_id=1, source_target_pairs={{16,0},{32,16},{48,32},{64,48},{80,64},{96,80},{112,96},{128,112},... | collective-permute-start | bytes 12296 | tf_op jit(solution)/shard_map/ppermute | solution.py:495
  55.8 1.5 %room1.1 = (f32[3,64,128]{2,1,0:T(8,128)S(1)}, f32[128,128]{1,0:T(8,128)S(1)}, f32[128,128]{1,0:T(8,128)S(1)}, f32[64,128]{1,0:T(8,128)S(1)}, f32[16,128]{1,0:T(8,128)S(1)}) custom-call(s32[5]{0:T(128)S(1)} %stack.11.refs_0_.scal, f32[128,128]{1,0:T(8,128)S(1)} %bitcast.22, f32[8,128]{1,0:T(8,128)S(1)} %get-tuple-element.127.refs_2_, ...), custom_call_target="tpu_custom_call" | custom-call | flops 3000000 | bytes 3000000 | tf_op jit(solution)/shard_map/room1/pallas_call | solution.py:480
  57.3 0.0 collective-permute-done.6.refs_11_
  57.3 0.0 collective-permute-done.7.refs_12_
  57.3 1.0 %send2.1 = (f32[64,128]{1,0:T(8,128)S(1)}, f32[80,128]{1,0:T(8,128)S(1)}, f32[64,128]{1,0:T(8,128)S(1)}, f32[64,128]{1,0:T(8,128)S(1)}, f32[16,128]{1,0:T(8,128)...) custom-call(s32[5]{0:T(128)S(1)} %stack.11.refs_0_.scal, ...), custom_call_target="tpu_custom_call" | custom-call | flops 1000000 | bytes 1000000 | tf_op jit(solution)/shard_map/send2/pallas_call | solution.py:480
  58.3 9.3 %all_to_all.46 = f32[16,8,128]{2,1,0:T(8,128)S(1)} all-to-all(f32[16,8,128]{2,1,0:T(8,128)S(1)} %bitcast.26), channel_id=1, replica_groups=mesh['district'=16,'tile'=16] {'tile'}, dimensions={0} | all-to-all | bytes 131072 | tf_op jit(solution)/shard_map/all_to_all | solution.py:579
  67.6 0.8 street2.1
  68.4 0.0 collective-permute-start.8
  68.4 6.1 %collective-permute-start.9 = (f32[8,128]{1,0:T(8,128)S(1)}, f32[8,128]{1,0:T(8,128)S(1)}, u32[]{:S(2)}, u32[]{:S(2)}) collective-permute-start(f32[8,128]{1,0:T(8,128)S(1)} %get-tuple-element.151), channel_id=1, source_target_pairs={{16,0},{32,16},{48,32},{64,48},{80,64},{96,80},{112,96},{128,112},... | collective-permute-start | bytes 12296 | tf_op jit(solution)/shard_map/ppermute | solution.py:495
  74.5 1.5 %room2.1 = (f32[3,64,128]{2,1,0:T(8,128)S(1)}, f32[128,128]{1,0:T(8,128)S(1)}, f32[128,128]{1,0:T(8,128)S(1)}, f32[64,128]{1,0:T(8,128)S(1)}, f32[16,128]{1,0:T(8,128)S(1)}) custom-call(s32[5]{0:T(128)S(1)} %stack.11.refs_0_.scal, f32[128,128]{1,0:T(8,128)S(1)} %bitcast.20, f32[8,128]{1,0:T(8,128)S(1)} %get-tuple-element.146.refs_2_, ...), custom_call_target="tpu_custom_call" | custom-call | flops 3000000 | bytes 3000000 | tf_op jit(solution)/shard_map/room2/pallas_call | solution.py:480
  76.0 0.0 collective-permute-done.8.refs_11_
  76.0 0.0 collective-permute-done.9.refs_12_
  76.0 1.4 %send3.1 = (f32[64,128]{1,0:T(8,128)S(1)}, f32[80,128]{1,0:T(8,128)S(1)}, f32[64,128]{1,0:T(8,128)S(1)}, f32[64,128]{1,0:T(8,128)}, f32[16,128]{1,0:T(8,128)S(1)...) custom-call(s32[5]{0:T(128)S(1)} %stack.11.refs_0_.scal, ...), custom_call_target="tpu_custom_call" | custom-call | flops 1000000 | bytes 1000000 | tf_op jit(solution)/shard_map/send3/pallas_call | solution.py:480
  77.4 9.0 %all_to_all.47 = f32[16,8,128]{2,1,0:T(8,128)S(1)} all-to-all(f32[16,8,128]{2,1,0:T(8,128)S(1)} %bitcast.24), channel_id=1, replica_groups=mesh['district'=16,'tile'=16] {'tile'}, dimensions={0} | all-to-all | bytes 131072 | tf_op jit(solution)/shard_map/all_to_all | solution.py:579
  86.4 1.6 %final.1 = (f32[3,16,128]{2,1,0:T(8,128)}, f32[3,64,128]{2,1,0:T(8,128)}, f32[3,64,128]{2,1,0:T(8,128)}) custom-call(s32[5]{0:T(128)S(1)} %stack.11.refs_0_.scal, f32[128,128]{1,0:T(8,128)S(1)} %bitcast.23, f32[64,128]{1,0:T(8,128)S(1)} %get-tuple-element.162.eta, f32[128,128]{1,0:T(8,128)S(1)} %get-tuple-element.163.street, ...), custom_call_target="tpu_custom_call" | custom-call | flops 1000000 | bytes 1000000 | tf_op jit(solution)/shard_map/final/pallas_call | solution.py:480
  (12 shorter events, 0.0 us)
Async XLA Ops:
  0.6 14.8 %copy-start.1 = (s32[4,64,128]{2,1,0:T(8,128)S(1)}, s32[4,64,128]{2,1,0:T(8,128)}, u32[]{:S(2)}) copy-start(s32[4,64,128]{2,1,0:T(8,128)} %refs_4_.7) | copy-start | bytes 393220
  0.6 14.8 %copy-start.6 = (f32[3,64,128]{2,1,0:T(8,128)S(1)}, f32[3,64,128]{2,1,0:T(8,128)}, u32[]{:S(2)}) copy-start(f32[3,64,128]{2,1,0:T(8,128)} %room.1) | copy-start | bytes 294916
  0.7 16.4 %copy-start.5 = (f32[3,16,128]{2,1,0:T(8,128)S(1)}, f32[3,16,128]{2,1,0:T(8,128)}, u32[]{:S(2)}) copy-start(f32[3,16,128]{2,1,0:T(8,128)} %refs_1_.4) | copy-start | bytes 73732
  2.5 14.5 %collective-permute-start.3 = (f32[16,128]{1,0:T(8,128)}, f32[16,128]{1,0:T(8,128)S(1)}, u32[]{:S(2)}, u32[]{:S(2)}) collective-permute-start(f32[16,128]{1,0:T(8,128)} %get-tuple-element.89.side), channel_id=1, source_target_pairs={{1,0},{2,1},{3,2},{4,3},{5,4},{6,5},{7,6},{8,7},{9,8},{10,9},{11,1... | collective-permute-start | bytes 24584 | tf_op jit(solution)/shard_map/ppermute | solution.py:495
  5.8 11.2 %collective-permute-start.2 = (f32[16,128]{1,0:T(8,128)}, f32[16,128]{1,0:T(8,128)S(1)}, u32[]{:S(2)}, u32[]{:S(2)}) collective-permute-start(f32[16,128]{1,0:T(8,128)} %get-tuple-element.89.side), channel_id=1, source_target_pairs={{0,1},{1,2},{2,3},{3,4},{4,5},{5,6},{6,7},{7,8},{8,9},{9,10},{10,1... | collective-permute-start | bytes 24584 | tf_op jit(solution)/shard_map/ppermute | solution.py:494
  5.8 7.8 %copy-start.9 = (s32[1,16,2]{1,2,0:T(2,128)S(1)}, s32[1,16,2]{1,2,0:T(2,128)}, u32[]{:S(2)}) copy-start(s32[1,16,2]{1,2,0:T(2,128)} %param.21) | copy-start | bytes 388
  5.8 11.1 %collective-permute-start = (f32[16,128]{1,0:T(8,128)}, f32[16,128]{1,0:T(8,128)S(1)}, u32[]{:S(2)}, u32[]{:S(2)}) collective-permute-start(f32[16,128]{1,0:T(8,128)} %get-tuple-element.87), channel_id=1, source_target_pairs={{0,16},{16,32},{32,48},{48,64},{64,80},{80,96},{96,112},{112,128},... | collective-permute-start | bytes 24584 | tf_op jit(solution)/shard_map/ppermute | solution.py:494
  8.4 8.7 %copy-start.4 = (f32[16,128]{1,0:T(8,128)S(1)}, f32[16,128]{1,0:T(8,128)}, u32[]{:S(2)}) copy-start(f32[16,128]{1,0:T(8,128)} %refs_1_.7) | copy-start | bytes 24580
  8.4 8.6 %collective-permute-start.1 = (f32[16,128]{1,0:T(8,128)}, f32[16,128]{1,0:T(8,128)S(1)}, u32[]{:S(2)}, u32[]{:S(2)}) collective-permute-start(f32[16,128]{1,0:T(8,128)} %get-tuple-element.88), channel_id=1, source_target_pairs={{16,0},{32,16},{48,32},{64,48},{80,64},{96,80},{112,96},{128,112},... | collective-permute-start | bytes 24584 | tf_op jit(solution)/shard_map/ppermute | solution.py:495
  14.1 1.3 %copy-start.8 = (s32[1,128]{1,0:T(1,128)S(1)}, s32[1,128]{1,0:T(1,128)}, u32[]{:S(2)}) copy-start(s32[1,128]{1,0:T(1,128)} %door.1) | copy-start | bytes 1540
  14.1 2.9 %copy-start = (s32[4,64,128]{2,1,0:T(8,128)S(1)}, s32[4,64,128]{2,1,0:T(8,128)}, u32[]{:S(2)}) copy-start(s32[4,64,128]{2,1,0:T(8,128)} %refs_3_.7) | copy-start | bytes 393220
  15.4 0.7 copy-start.7
  16.1 0.9 %copy-start.2 = (f32[64,128]{1,0:T(8,128)S(1)}, f32[64,128]{1,0:T(8,128)}, u32[]{:S(2)}) copy-start(f32[64,128]{1,0:T(8,128)} %refs_2_.7) | copy-start | bytes 98308
  16.1 0.9 %copy-start.3 = (f32[3,64,128]{2,1,0:T(8,128)S(1)}, f32[3,64,128]{2,1,0:T(8,128)}, u32[]{:S(2)}) copy-start(f32[3,64,128]{2,1,0:T(8,128)} %refs_3_.4) | copy-start | bytes 294916
  31.3 7.6 %collective-permute-start.4 = (f32[8,128]{1,0:T(8,128)S(1)}, f32[8,128]{1,0:T(8,128)S(1)}, u32[]{:S(2)}, u32[]{:S(2)}) collective-permute-start(f32[8,128]{1,0:T(8,128)S(1)} %get-tuple-element.112), channel_id=1, source_target_pairs={{0,16},{16,32},{32,48},{48,64},{64,80},{80,96},{96,112},{112,128},... | collective-permute-start | bytes 12296 | tf_op jit(solution)/shard_map/ppermute | solution.py:494
  31.7 7.3 %collective-permute-start.5 = (f32[8,128]{1,0:T(8,128)S(1)}, f32[8,128]{1,0:T(8,128)S(1)}, u32[]{:S(2)}, u32[]{:S(2)}) collective-permute-start(f32[8,128]{1,0:T(8,128)S(1)} %get-tuple-element.113), channel_id=1, source_target_pairs={{16,0},{32,16},{48,32},{64,48},{80,64},{96,80},{112,96},{128,112},... | collective-permute-start | bytes 12296 | tf_op jit(solution)/shard_map/ppermute | solution.py:495
  50.1 7.2 %collective-permute-start.6 = (f32[8,128]{1,0:T(8,128)S(1)}, f32[8,128]{1,0:T(8,128)S(1)}, u32[]{:S(2)}, u32[]{:S(2)}) collective-permute-start(f32[8,128]{1,0:T(8,128)S(1)} %get-tuple-element.131), channel_id=1, source_target_pairs={{0,16},{16,32},{32,48},{48,64},{64,80},{80,96},{96,112},{112,128},... | collective-permute-start | bytes 12296 | tf_op jit(solution)/shard_map/ppermute | solution.py:494
  50.4 6.9 %collective-permute-start.7 = (f32[8,128]{1,0:T(8,128)S(1)}, f32[8,128]{1,0:T(8,128)S(1)}, u32[]{:S(2)}, u32[]{:S(2)}) collective-permute-start(f32[8,128]{1,0:T(8,128)S(1)} %get-tuple-element.132), channel_id=1, source_target_pairs={{16,0},{32,16},{48,32},{64,48},{80,64},{96,80},{112,96},{128,112},... | collective-permute-start | bytes 12296 | tf_op jit(solution)/shard_map/ppermute | solution.py:495
  68.4 7.6 %collective-permute-start.8 = (f32[8,128]{1,0:T(8,128)S(1)}, f32[8,128]{1,0:T(8,128)S(1)}, u32[]{:S(2)}, u32[]{:S(2)}) collective-permute-start(f32[8,128]{1,0:T(8,128)S(1)} %get-tuple-element.150), channel_id=1, source_target_pairs={{0,16},{16,32},{32,48},{48,64},{64,80},{80,96},{96,112},{112,128},... | collective-permute-start | bytes 12296 | tf_op jit(solution)/shard_map/ppermute | solution.py:494
  68.4 7.6 %collective-permute-start.9 = (f32[8,128]{1,0:T(8,128)S(1)}, f32[8,128]{1,0:T(8,128)S(1)}, u32[]{:S(2)}, u32[]{:S(2)}) collective-permute-start(f32[8,128]{1,0:T(8,128)S(1)} %get-tuple-element.151), channel_id=1, source_target_pairs={{16,0},{32,16},{48,32},{64,48},{80,64},{96,80},{112,96},{128,112},... | collective-permute-start | bytes 12296 | tf_op jit(solution)/shard_map/ppermute | solution.py:495

commit v3 on v2

--- a/solution.py
+++ b/solution.py
@@ -170,13 +170,26 @@
     return row.astype(i32), take(side[10:11]).astype(i32), take(side[11:12])
 
 
+def list_openings(side, row, col, owner, valid, conduct):
+    count = owner.shape[1]
+    side[8:9] = jnp.full((1, LANES), -1.0, f32)
+    side[8:9, 0:count] = owner[...].astype(f32)
+    side[9:10, 0:count] = row[...].astype(f32)
+    side[10:11, 0:count] = col[...].astype(f32)
+    side[11:12, 0:count] = conduct[...] * valid[...].astype(f32)
+
+
 def edges_kernel(
-    parent_i, parent_depth_i, child_i, child_depth_i, child_wet_i, row_i, col_i, owner_i, valid_i, conduct_i, up, dn, side,
+    parent_i, parent_depth_i, child_i, child_depth_i, child_wet_i, row_i, col_i, owner_i, valid_i, conduct_i,
+    up, dn, side,
     parent, parent_depth, child, child_depth, child_wet, row, col, owner, valid, conduct, done,
 ):
-    pairs = [
-        (child_i, child), (child_depth_i, child_depth), (child_wet_i, child_wet), (parent_i, parent),
-        (parent_depth_i, parent_depth), (row_i, row), (col_i, col), (owner_i, owner), (valid_i, valid), (conduct_i, conduct),
+    pairs = [(child_wet_i.at[s], child_wet.at[s]) for s in range(STEPS)]
+    pairs += [(child_i.at[f], child.at[f]) for f in (0, 2)]
+    pairs += [(child_i.at[1, pl.ds(r, 8)], child.at[1, pl.ds(r, 8)]) for r in (0, CX - 8)]
+    pairs += [
+        (child_depth_i, child_depth), (parent_i, parent), (parent_depth_i, parent_depth),
+        (row_i, row), (col_i, col), (owner_i, owner), (valid_i, valid), (conduct_i, conduct),
     ]
     copies = [pltpu.make_async_copy(src, dst, done.at[k]) for k, (src, dst) in enumerate(pairs)]
     for copy in copies:
@@ -209,17 +222,17 @@
     packed = pack2(packed, parent[2], 120)
     packed = pack2(packed, parent_depth[...], 124)
     side[0:8] = packed
-    count = owner.shape[1]
-    side[8:9] = jnp.full((1, LANES), -1.0, f32)
-    side[8:9, 0:count] = owner[...].astype(f32)
-    side[9:10, 0:count] = row[...].astype(f32)
-    side[10:11, 0:count] = col[...].astype(f32)
-    side[11:12, 0:count] = conduct[...] * valid[...].astype(f32)
+    list_openings(side, row, col, owner, valid, conduct)
 
 
 def setup_kernel(
-    side, door, room, room_wet, row2, row_t2, index_s, index_a, gain, lower, fixed, door2, door_t2, room_new, face, reply, eta_x, flux_x
+    opening_row, opening_col, owner, valid, conduct, anchor, door, room, room_wet, row2, row_t2, index_s, index_a, gain, lower, fixed,
+    door2, door_t2, room_new, face, reply, place, eta_x, flux_x, side,
 ):
+    side[8:16] = jnp.zeros((8, LANES), f32)
+    list_openings(side, opening_row, opening_col, owner, valid, conduct)
+    place[0:8] = jnp.broadcast_to(anchor[0:1, 0:1], (8, LANES))
+    place[8:16] = jnp.broadcast_to(anchor[1:2, 0:1], (8, LANES))
     shape = (SLOTS, LANES)
     at_lane = lane(shape)
     row, col, weight = slots_of(side[...])
@@ -277,13 +290,14 @@
 
 
 def send_kernel(step, *refs):
-    scal = refs[0]
-    has_left, has_right = scal[0] > 0, scal[0] < TILES - 1
-    has_above, has_below = scal[3] > 0, scal[3] < scal[4] - 1
+    tile, district = lax.axis_index("tile"), lax.axis_index("district")
+    has_left, has_right = tile > 0, tile < TILES - 1
+    has_above, has_below = district > 0, district < lax.axis_size("district") - 1
+    last = step == STEPS - 1
     if step == 0:
         (
-            scal, parent, parent_depth, child, child_depth, child_wet, above0, below0, left0, right0, reply, row2, index_s,
-            eta_o, u_o, v_o, vh_o, peta_o, pu_o, pv_o, pvh_o, street_o, out, eta_x, flux_x, u_x, peta_x, pflux_x, pu_x,
+            place, parent, parent_depth, child, child_depth, child_wet, above0, below0, left0, right0, reply, row2, index_s,
+            eta_o, u_o, v_o, peta_o, pu_o, pv_o, street_o, out, *more, eta_x, flux_x, u_x, peta_x, pflux_x, pu_x,
         ) = refs
         u_x[8 : 8 + CX] = child[1]
         u_x[7:8] = gate(has_above, above0[2:3])
@@ -304,9 +318,9 @@
         peta_h = unpack4(left, right, 112, 2)
     else:
         (
-            scal, parent_depth, child_depth, child_wet, above0, below0, left0, right0, reply, row2, index_s,
+            place, parent_depth, child_depth, child_wet, above0, below0, left0, right0, reply, row2, index_s,
             above, below, eta_i, u_x, v_i, vh_i, etah_i, peta_i, pu_x, pv_i, pvh_i, petah_i,
-            eta_o, u_o, v_o, vh_o, peta_o, pu_o, pv_o, pvh_o, street_o, out, eta_x, flux_x, peta_x, pflux_x,
+            eta_o, u_o, v_o, peta_o, pu_o, pv_o, street_o, out, *more, eta_x, flux_x, peta_x, pflux_x,
         ) = refs
         eta_x[8 : 8 + CX] = eta_i[...]
         peta_x[8 : 8 + PX] = peta_i[...]
@@ -330,25 +344,29 @@
     )
     eta_o[...] = eta
     u_o[8 : 8 + CX] = wet * u
-    u_o[7:8] = wet_of(q_up) * u_up
-    u_o[8 + CX : 9 + CX] = wet_of(q_dn) * u_dn
     v_o[...] = wet * v
-    vh_o[...] = wet_of(q_h) * v_h
     peta_o[...] = peta
     pu_o[8 : 8 + PX] = pu
-    pu_o[7:8] = pu_up
-    pu_o[8 + PX : 9 + PX] = pu_dn
     pv_o[...] = pv
-    pvh_o[...] = pv_h
     street_o[...] = street
-    tile, first_row, first_col = scal[0], scal[1], scal[2]
+    if not last:
+        vh_o, pvh_o = more
+        u_o[7:8] = wet_of(q_up) * u_up
+        u_o[8 + CX : 9 + CX] = wet_of(q_dn) * u_dn
+        vh_o[...] = wet_of(q_h) * v_h
+        pu_o[7:8] = pu_up
+        pu_o[8 + PX : 9 + PX] = pu_dn
+        pvh_o[...] = pv_h
     shape = (8, LANES)
     at_lane = lane(shape)
     common = pack4(jnp.zeros(shape, f32), eta, L_CCOL)
     common = pack4(common, peta, L_PCOL)
-    line0 = peta_o[pl.ds(first_row, 1)]
-    line1 = peta_o[pl.ds(first_row + 1, 1)]
-    lines = jnp.where(sub(shape) < 4, line0, line1)
+    first_row, first_col = place[0:8], place[8:16]
+    lines = []
+    for k in range(2):
+        halves_of = [jnp.where(sub(shape) + g == first_row + k, peta[g : g + 8], 0.0) for g in (0, 8)]
+        lines.append(jnp.sum(halves_of[0] + halves_of[1], axis=0, keepdims=True))
+    lines = jnp.where(sub(shape) < 4, lines[0], lines[1])
     index = first_col - LANES * tile + 4 * (at_lane - L_WIN) + (sub(shape) & 3)
     window = along(lines, index & (LANES - 1))
     window = jnp.where((index >= 0) & (index < LANES), window, 0.0)
@@ -370,10 +388,10 @@
     return eta + nudging * (target - eta)
 
 
-def street_update(scal, inbox, eta, street, row_t2, index_a, gain, lower):
+def street_update(inbox, eta, street, row_t2, index_a, gain, lower):
     shape = (8, LANES)
     windows = windows_sum(inbox)
-    mine = along(windows, jnp.full(shape, L_WIN, i32) + scal[0])
+    mine = along(windows, jnp.full(shape, L_WIN, i32) + lax.axis_index("tile"))
     mine = jnp.where((sub(shape) & 3) == lane(shape) // R, mine, 0.0)
     target0 = jnp.sum(mine[0:4], axis=0, keepdims=True)
     target1 = jnp.sum(mine[4:8], axis=0, keepdims=True)
@@ -404,9 +422,9 @@
     return weight * (levels - face)
 
 
-def street_kernel(scal, inbox, eta, street, row_t2, index_a, gain, lower, peta, eta_o, up, dn, windows_o):
+def street_kernel(inbox, eta, street, row_t2, index_a, gain, lower, peta, eta_o, up, dn, windows_o):
     eta, windows_o[...] = street_update(
-        scal, inbox[...], eta[...], street[...], row_t2[...], index_a[...], gain[...], lower[...]
+        inbox[...], eta[...], street[...], row_t2[...], index_a[...], gain[...], lower[...]
     )
     eta_o[...] = eta
     blank = jnp.zeros((4, LANES), f32)
@@ -419,7 +437,7 @@
 
 
 def room_kernel(
-    step, scal, inbox, windows, room, room_wet, face, door2, door_t2, fixed, near2, near_t2, near_index, near_gain,
+    step, inbox, windows, room, room_wet, face, door2, door_t2, fixed, near2, near_t2, near_index, near_gain,
     room_new, face_o, reply, etah_o, petah_o, eta_x, flux_x,
 ):
     received = inbox[...]
@@ -430,7 +448,7 @@
     room_new[1] = u
     room_new[2] = v
     face_o[...], reply[...] = room_reply(eta, door2[...], fixed[...])
-    tile = scal[0]
+    tile = lax.axis_index("tile")
     left = inbox[pl.ds(pl.multiple_of(8 * lax.rem(tile + TILES - 1, TILES), 8), 8)]
     right = inbox[pl.ds(pl.multiple_of(8 * lax.rem(tile + 1, TILES), 8), 8)]
     at_lane = lane((8, LANES))
@@ -451,49 +469,57 @@
 
 
 def final_kernel(
-    scal, inbox, eta, street, row_t2, index_a, gain, lower, u_x, v, peta, pu_x, pv, room, face, door_t2,
-    parent_o, child_o, room_o,
+    inbox, eta, street, row_t2, index_a, gain, lower, u_x, v, peta, pu_x, pv, room, face, door_t2,
+    parent_o, child_o, room_o, child_eta, room_eta, done,
 ):
+    pairs = [
+        (u_x.at[pl.ds(8, CX)], child_o.at[1]), (v, child_o.at[2]), (peta, parent_o.at[0]),
+        (pu_x.at[pl.ds(8, PX)], parent_o.at[1]), (pv, parent_o.at[2]), (room.at[1], room_o.at[1]),
+        (room.at[2], room_o.at[2]), (room_eta, room_o.at[0]), (child_eta, child_o.at[0]),
+    ]
+    copies = [pltpu.make_async_copy(src, dst, done.at[k]) for k, (src, dst) in enumerate(pairs)]
+    for copy in copies[:-2]:
+        copy.start()
     received = inbox[...]
-    eta, windows = street_update(scal, received, eta[...], street[...], row_t2[...], index_a[...], gain[...], lower[...])
-    child_o[0] = eta
-    child_o[1] = u_x[8 : 8 + CX]
-    child_o[2] = v[...]
-    parent_o[0] = peta[...]
-    parent_o[1] = pu_x[8 : 8 + PX]
-    parent_o[2] = pv[...]
-    room_o[0] = room[0] + pick(door_t2[...], room_flow(received, windows, face[...]))
-    room_o[1] = room[1]
-    room_o[2] = room[2]
+    child_eta[...], windows = street_update(
+        received, eta[...], street[...], row_t2[...], index_a[...], gain[...], lower[...]
+    )
+    copies[-1].start()
+    room_eta[...] = room[0] + pick(door_t2[...], room_flow(received, windows, face[...]))
+    copies[-2].start()
+    for copy in copies:
+        copy.wait()
 
 
 def sds(*shape, dtype=f32):
     return jax.ShapeDtypeStruct(shape, dtype)
 
 
-def call(name, kernel, outs, args, scalars=0, scratch=(), us=1, own_copies=False):
-    spec = pl.BlockSpec(memory_space=pltpu.VMEM)
-    first = pl.BlockSpec(memory_space=pltpu.HBM) if own_copies else spec
-    scratch_shapes = [pltpu.VMEM((rows, LANES), f32) for rows in scratch]
-    if own_copies:
-        scratch_shapes = [pltpu.VMEM(a.shape, a.dtype) for a in args] + [pltpu.SemaphoreType.DMA((len(args),))]
+VMEM = pl.BlockSpec(memory_space=pltpu.VMEM)
+HBM = pl.BlockSpec(memory_space=pltpu.HBM)
+
+
+def call(name, kernel, outs, args, scratch=(), us=1, reads=VMEM, writes=VMEM, limit=16):
     return pl.pallas_call(
         kernel,
         out_shape=outs,
-        in_specs=[pl.BlockSpec(memory_space=pltpu.SMEM)] * scalars + [first] * (len(args) - scalars),
-        out_specs=jax.tree.map(lambda _: spec, outs),
-        scratch_shapes=scratch_shapes,
-        compiler_params=pltpu.CompilerParams(vmem_limit_bytes=(60 if own_copies else 16) * 2**20),
+        in_specs=[reads] * len(args),
+        out_specs=[writes] * len(outs),
+        scratch_shapes=[pltpu.VMEM((rows, LANES), f32) if isinstance(rows, int) else rows for rows in scratch],
+        compiler_params=pltpu.CompilerParams(vmem_limit_bytes=limit * 2**20),
         cost_estimate=pl.CostEstimate(flops=1000000 * us, bytes_accessed=1000000 * us, transcendentals=0),
         name=name,
     )(*args)
 
 
-def shifts(up, dn, axis):
+def to_next(cells, axis):
     count = lax.axis_size(axis)
-    before = lax.ppermute(dn, axis, [(i, (i + 1) % count) for i in range(count)])
-    after = lax.ppermute(up, axis, [((i + 1) % count, i) for i in range(count)])
-    return before, after
+    return lax.ppermute(cells, axis, [(i, (i + 1) % count) for i in range(count)])
+
+
+def to_previous(cells, axis):
+    count = lax.axis_size(axis)
+    return lax.ppermute(cells, axis, [((i + 1) % count, i) for i in range(count)])
 
 
 def body(
@@ -516,38 +542,36 @@
     pblock, ptall = sds(PX, LANES), sds(PX + 16, LANES)
     grid, tile8, tile16 = sds(SLOTS, LANES), sds(8, LANES), sds(16, LANES)
     rooms = sds(3, CX, LANES)
-    my_tile = lax.axis_index("tile").astype(i32)
-    my_district = lax.axis_index("district").astype(i32)
-    last = jnp.int32(lax.axis_size("district"))
-    scal = jnp.stack([my_tile, parent_anchor[0, 0, 0], parent_anchor[0, 0, 1], my_district, last])
 
     def flat(values):
         return values.reshape(1, -1)
 
+    openings = [flat(open_row), flat(open_col), flat(open_owner), flat(open_valid), flat(open_conduct)]
+    inputs = [parent_state, parent_depth, child_state, child_depth, child_wet, *openings]
     up, dn, side = call(
         "edges",
         edges_kernel,
         [tile16] * 3,
-        [
-            parent_state, parent_depth, child_state, child_depth, child_wet, flat(open_row), flat(open_col),
-            flat(open_owner), flat(open_valid), flat(open_conduct),
-        ],
-        own_copies=True,
-    )
-    above0, below0 = shifts(up, dn, "district")
-    left0, right0 = shifts(side, side, "tile")
-    row2, row_t2, index_s, index_a, gain, lower, fixed, door2, door_t2, room, face, reply = call(
+        inputs,
+        scratch=[pltpu.VMEM(a.shape, a.dtype) for a in inputs] + [pltpu.SemaphoreType.DMA((16,))],
+        reads=HBM,
+        limit=60,
+    )
+    left0 = to_next(side, "tile")
+    right0 = to_previous(side, "tile")
+    row2, row_t2, index_s, index_a, gain, lower, fixed, door2, door_t2, room, face, reply, place = call(
         "setup",
         setup_kernel,
         [
             sds(SLOTS, LANES, dtype=bf16), sds(CX, 2 * SLOTS, dtype=bf16), sds(SLOTS, LANES, dtype=i32),
             sds(SLOTS, LANES, dtype=i32), grid, grid, grid, sds(SLOTS, LANES, dtype=bf16),
-            sds(CX, 2 * SLOTS, dtype=bf16), rooms, grid, grid,
+            sds(CX, 2 * SLOTS, dtype=bf16), rooms, grid, grid, sds(16, LANES, dtype=i32),
         ],
-        [side, door_rows, interior_state, interior_wet],
-        scratch=(CX + 16, CX + 16),
-        us=4,
-    )
+        [*openings, jnp.transpose(parent_anchor, (0, 2, 1))[0], door_rows, interior_state, interior_wet],
+        scratch=(CX + 16, CX + 16, 16),
+    )
+    above0 = to_next(dn, "district")
+    below0 = to_previous(up, "district")
     near = call(
         "near",
         near_kernel,
@@ -556,28 +580,27 @@
             sds(2 * SLOTS, LANES),
         ],
         [left0, right0],
-        us=3,
-    )
-    outs = [block, tall, block, block, pblock, ptall, pblock, pblock, grid, grid]
+    )
     for step in range(STEPS):
         with_step = lambda *refs, step=step: send_kernel(step, *refs)
         if step == 0:
             args = [
-                scal, parent_state, parent_depth, child_state, child_depth, child_wet, above0, below0, left0, right0,
+                place, parent_state, parent_depth, child_state, child_depth, child_wet, above0, below0, left0, right0,
                 reply, row2, index_s,
             ]
             scratch = (CX + 16,) * 3 + (PX + 16,) * 3
         else:
             args = [
-                scal, parent_depth, child_depth, child_wet, above0, below0, left0, right0, reply, row2, index_s,
+                place, parent_depth, child_depth, child_wet, above0, below0, left0, right0, reply, row2, index_s,
                 above, below, eta, u, v, v_h, eta_h, peta, pu, pv, pv_h, peta_h,
             ]
             scratch = (CX + 16,) * 2 + (PX + 16,) * 2
-        eta, u, v, v_h, peta, pu, pv, pv_h, street, outbox = call(
-            f"send{step}", with_step, outs, args, scalars=1, scratch=scratch
-        )
+        outs = [block, tall, block, pblock, ptall, pblock, grid, grid]
+        if step < STEPS - 1:
+            outs += [block, pblock]
+        eta, u, v, peta, pu, pv, street, outbox, *more = call(f"send{step}", with_step, outs, args, scratch=scratch)
         inbox = lax.all_to_all(outbox, "tile", split_axis=0, concat_axis=0, tiled=True)
-        shared = [scal, inbox, eta, street, row_t2, index_a, gain, lower]
+        shared = [inbox, eta, street, row_t2, index_a, gain, lower]
         if step == STEPS - 1:
             return tuple(
                 call(
@@ -585,22 +608,21 @@
                     final_kernel,
                     [sds(3, PX, LANES), rooms, rooms],
                     shared + [u, v, peta, pu, pv, room, face, door_t2],
-                    scalars=1,
+                    scratch=(CX, CX, pltpu.SemaphoreType.DMA((9,))),
+                    writes=HBM,
                 )
             )
-        eta, up, dn, windows = call(
-            f"street{step}", street_kernel, [block, tile8, tile8, tile8], shared + [peta], scalars=1
-        )
-        above, below = shifts(up, dn, "district")
+        v_h, pv_h = more
+        eta, up, dn, windows = call(f"street{step}", street_kernel, [block, tile8, tile8, tile8], shared + [peta])
+        below = to_previous(up, "district")
+        above = to_next(dn, "district")
         with_step = lambda *refs, step=step: room_kernel(step + 1, *refs)
         room, face, reply, eta_h, peta_h = call(
             f"room{step}",
             with_step,
             [rooms, grid, grid, block, pblock],
-            [scal, inbox, windows, room, interior_wet, face, door2, door_t2, fixed, *near],
-            scalars=1,
+            [inbox, windows, room, interior_wet, face, door2, door_t2, fixed, *near],
             scratch=(CX + 16, CX + 16),
-            us=3,
         )
 
 

time: 88.4 us -> 82.8 us (0.937)
  Pallas kernels: 16 us -> 9.67 us
  local copies, waits for them, and re-layouts: 2.56 us -> 0.07 us
  waiting for transfers between devices: 0.03 us -> 1.37 us
  blocking collectives: 40 us -> 41.3 us
    pallas_call x14, Pallas kernels: 16 us -> 9.67 us  [call(): pl.pallas_call(kernel, out_shape=outs, in_specs=[reads] * len(args), out_...]
    ppermute x10, waiting for transfers between devices: 0.03 us -> 1.37 us  [the longest x5 0.79 us: to_next(): lax.ppermute(cells, axis, [(i, (i + 1) % count) for i in range(count)])]
    all_to_all x4, blocking collectives: 40 us -> 41.3 us  [body(): lax.all_to_all(outbox, 'tile', split_axis=0, concat_axis=0, tiled=True)]
    another operation x1 -> x0, local copies, waits for them, and re-layouts: 1.28 us -> none  [body(): jnp.stack([my_tile, parent_anchor[0, 0, 0], parent_anchor[0, 0, 1], my_di...]
  transfers between devices with their start and end apart: 10 -> 10, of which waited for: 0 -> 2; matrix products, arithmetic and copies ran while one was open for 2% -> 0% of each run, Pallas kernels for 7% -> 5%
where the time goes in v3:
time: 82.8 us; the launch traced here: 82.6 us
  blocking collectives  41.3 us (50%)
  starting transfers between devices  29.3 us (35%)
  Pallas kernels  9.67 us (12%)
  waiting for transfers between devices  1.37 us (2%)
  between operations  0.94 us (1%)
    all_to_all x4, blocking collectives, body(): lax.all_to_all(outbox, 'tile', split_axis=0, concat_axis=0, tiled=True)  41.3 us
    ppermute x5, starting transfers between devices, to_previous(): lax.ppermute(cells, axis, [((i + 1) % count, i) for i in range(count)])  23.5 us
    pallas_call x14, Pallas kernels, call(): pl.pallas_call(kernel, out_shape=outs, in_specs=[reads] * len(args), out_...  9.67 us
    ppermute x5, starting transfers between devices, to_next(): lax.ppermute(cells, axis, [(i, (i + 1) % count) for i in range(count)])  5.77 us
  transfers between devices with their start and end apart: 10, of which 2 were waited for; matrix products, arithmetic and copies ran while one was open for 0% of the time, Pallas kernels for 5%

profile of v3, /device:TPU:1, one launch (start us, length us, event | category | flops | bytes accessed | tf_op | source)
XLA Modules:
  0.0 82.6 jit_solution(4164749532844687947)
XLA Ops:
  0.6 0.0 copy-start.6
  0.6 0.0 copy-start.7
  0.7 0.0 copy-start.8
  0.7 0.0 copy-start.9
  0.7 1.8 %edges.1 = (f32[16,128]{1,0:T(8,128)}, f32[16,128]{1,0:T(8,128)}, f32[16,128]{1,0:T(8,128)}) custom-call(f32[3,16,128]{2,1,0:T(8,128)} %refs_1_.4, f32[16,128]{1,0:T(8,128)} %refs_1_.7, f32[3,64,128]{2,1,0:T(8,128)} %refs_3_.7, f32[64,128]{1,0:T(8,128)} %refs_2_.7, s32[4,64,128]{2,1,0:T(8,128)} %refs_3_.13, s32[1,64]{1,0:T(1,128)} %bitcast.27, ...), custom_call_target="tpu_custom_call" | custom-call | flops 1000000 | bytes 1000000 | tf_op jit(solution)/shard_map/edges/pallas_call | solution.py:503
  2.6 0.0 copy-start
  2.6 3.9 %collective-permute-start = (f32[16,128]{1,0:T(8,128)}, f32[16,128]{1,0:T(8,128)S(1)}, u32[]{:S(2)}, u32[]{:S(2)}) collective-permute-start(f32[16,128]{1,0:T(8,128)} %get-tuple-element.89), channel_id=1, source_target_pairs={{0,16},{16,32},{32,48},{48,64},{64,80},{80,96},{96,112},{112,128},... | collective-permute-start | bytes 24584 | tf_op jit(solution)/shard_map/ppermute | solution.py:517
  6.5 5.3 %collective-permute-start.1 = (f32[16,128]{1,0:T(8,128)}, f32[16,128]{1,0:T(8,128)S(1)}, u32[]{:S(2)}, u32[]{:S(2)}) collective-permute-start(f32[16,128]{1,0:T(8,128)} %get-tuple-element.90), channel_id=1, source_target_pairs={{16,0},{32,16},{48,32},{64,48},{80,64},{96,80},{112,96},{128,112},... | collective-permute-start | bytes 24584 | tf_op jit(solution)/shard_map/ppermute | solution.py:522
  11.8 1.0 %collective-permute-start.3 = (f32[16,128]{1,0:T(8,128)}, f32[16,128]{1,0:T(8,128)S(1)}, u32[]{:S(2)}, u32[]{:S(2)}) collective-permute-start(f32[16,128]{1,0:T(8,128)} %get-tuple-element.91), channel_id=1, source_target_pairs={{1,0},{2,1},{3,2},{4,3},{5,4},{6,5},{7,6},{8,7},{9,8},{10,9},{11,1... | collective-permute-start | bytes 24584 | tf_op jit(solution)/shard_map/ppermute | solution.py:522
  12.8 1.2 %collective-permute-start.2 = (f32[16,128]{1,0:T(8,128)}, f32[16,128]{1,0:T(8,128)S(1)}, u32[]{:S(2)}, u32[]{:S(2)}) collective-permute-start(f32[16,128]{1,0:T(8,128)} %get-tuple-element.91), channel_id=1, source_target_pairs={{0,1},{1,2},{2,3},{3,4},{4,5},{5,6},{6,7},{7,8},{8,9},{9,10},{10,1... | collective-permute-start | bytes 24584 | tf_op jit(solution)/shard_map/ppermute | solution.py:517
  14.0 0.0 copy-done.8
  14.0 0.0 copy-start.2
  14.0 0.0 copy-start.4
  14.0 0.0 copy-start.5
  14.1 0.8 %setup.1 = (bf16[128,128]{1,0:T(8,128)(2,1)S(1)}, bf16[64,256]{1,0:T(8,128)(2,1)S(1)}, s32[128,128]{1,0:T(8,128)S(1)}, s32[128,128]{1,0:T(8,128)S(1)}, f32[128,1...) custom-call(s32[1,64]{1,0:T(1,128)S(1)} %bitcast.28, ...), custom_call_target="tpu_custom_call" | custom-call | flops 1000000 | bytes 1000000 | tf_op jit(solution)/shard_map/setup/pallas_call | solution.py:503
  14.9 0.0 collective-permute-done.refs_6_.refs_4_
  14.9 0.0 collective-permute-done.1.refs_7_.refs_5_
  14.9 0.6 collective-permute-done.3.refs_9_.right.refs_7_
  15.5 0.8 collective-permute-done.2.refs_8_.left.refs_6_
  16.3 0.0 copy-done.3
  16.3 0.5 send0.1
  16.8 12.8 %all_to_all.44 = f32[16,8,128]{2,1,0:T(8,128)S(1)} all-to-all(f32[16,8,128]{2,1,0:T(8,128)S(1)} %bitcast.26), channel_id=1, replica_groups=mesh['district'=16,'tile'=16] {'tile'}, dimensions={0} | all-to-all | bytes 131072 | tf_op jit(solution)/shard_map/all_to_all | solution.py:602
  29.6 0.2 street0.1
  29.9 0.0 collective-permute-start.4
  29.9 5.7 %collective-permute-start.5 = (f32[8,128]{1,0:T(8,128)S(1)}, f32[8,128]{1,0:T(8,128)S(1)}, u32[]{:S(2)}, u32[]{:S(2)}) collective-permute-start(f32[8,128]{1,0:T(8,128)S(1)} %get-tuple-element.115), channel_id=1, source_target_pairs={{16,0},{32,16},{48,32},{64,48},{80,64},{96,80},{112,96},{128,112},... | collective-permute-start | bytes 12296 | tf_op jit(solution)/shard_map/ppermute | solution.py:522
  35.6 0.4 near.1
  36.0 1.0 %room0.1 = (f32[3,64,128]{2,1,0:T(8,128)S(1)}, f32[128,128]{1,0:T(8,128)S(1)}, f32[128,128]{1,0:T(8,128)S(1)}, f32[64,128]{1,0:T(8,128)S(1)}, f32[16,128]{1,0:T(8,128)S(1)}) custom-call(f32[128,128]{1,0:T(8,128)S(1)} %bitcast.17, f32[8,128]{1,0:T(8,128)S(1)} %get-tuple-element.103.refs_1_, f32[3,64,128]{2,1,0:T(8,128)S(1)} %get-tuple-element.104.refs_2_, ...), custom_call_target="tpu_custom_call" | custom-call | flops 1000000 | bytes 1000000 | tf_op jit(solution)/shard_map/room0/pallas_call | solution.py:503
  37.0 0.0 collective-permute-done.4.refs_11_
  37.0 0.0 collective-permute-done.5.refs_12_
  37.0 0.4 send1.1
  37.4 9.4 %all_to_all.45 = f32[16,8,128]{2,1,0:T(8,128)S(1)} all-to-all(f32[16,8,128]{2,1,0:T(8,128)S(1)} %bitcast.24), channel_id=1, replica_groups=mesh['district'=16,'tile'=16] {'tile'}, dimensions={0} | all-to-all | bytes 131072 | tf_op jit(solution)/shard_map/all_to_all | solution.py:602
  46.9 0.2 street1.1
  47.1 0.7 collective-permute-start.6
  47.8 5.4 %collective-permute-start.7 = (f32[8,128]{1,0:T(8,128)S(1)}, f32[8,128]{1,0:T(8,128)S(1)}, u32[]{:S(2)}, u32[]{:S(2)}) collective-permute-start(f32[8,128]{1,0:T(8,128)S(1)} %get-tuple-element.134), channel_id=1, source_target_pairs={{16,0},{32,16},{48,32},{64,48},{80,64},{96,80},{112,96},{128,112},... | collective-permute-start | bytes 12296 | tf_op jit(solution)/shard_map/ppermute | solution.py:522
  53.2 1.0 %room1.1 = (f32[3,64,128]{2,1,0:T(8,128)S(1)}, f32[128,128]{1,0:T(8,128)S(1)}, f32[128,128]{1,0:T(8,128)S(1)}, f32[64,128]{1,0:T(8,128)S(1)}, f32[16,128]{1,0:T(8,128)S(1)}) custom-call(f32[128,128]{1,0:T(8,128)S(1)} %bitcast.21, f32[8,128]{1,0:T(8,128)S(1)} %get-tuple-element.129.refs_1_, f32[3,64,128]{2,1,0:T(8,128)S(1)} %get-tuple-element.130.refs_2_, ...), custom_call_target="tpu_custom_call" | custom-call | flops 1000000 | bytes 1000000 | tf_op jit(solution)/shard_map/room1/pallas_call | solution.py:503
  54.2 0.0 collective-permute-done.6.refs_11_
  54.2 0.0 collective-permute-done.7.refs_12_
  54.2 0.4 send2.1
  54.6 9.5 %all_to_all.46 = f32[16,8,128]{2,1,0:T(8,128)S(1)} all-to-all(f32[16,8,128]{2,1,0:T(8,128)S(1)} %bitcast.25), channel_id=1, replica_groups=mesh['district'=16,'tile'=16] {'tile'}, dimensions={0} | all-to-all | bytes 131072 | tf_op jit(solution)/shard_map/all_to_all | solution.py:602
  64.2 0.2 street2.1
  64.4 0.0 collective-permute-start.8
  64.4 6.2 %collective-permute-start.9 = (f32[8,128]{1,0:T(8,128)S(1)}, f32[8,128]{1,0:T(8,128)S(1)}, u32[]{:S(2)}, u32[]{:S(2)}) collective-permute-start(f32[8,128]{1,0:T(8,128)S(1)} %get-tuple-element.153), channel_id=1, source_target_pairs={{16,0},{32,16},{48,32},{64,48},{80,64},{96,80},{112,96},{128,112},... | collective-permute-start | bytes 12296 | tf_op jit(solution)/shard_map/ppermute | solution.py:522
  70.6 1.0 %room2.1 = (f32[3,64,128]{2,1,0:T(8,128)S(1)}, f32[128,128]{1,0:T(8,128)S(1)}, f32[128,128]{1,0:T(8,128)S(1)}, f32[64,128]{1,0:T(8,128)S(1)}, f32[16,128]{1,0:T(8,128)S(1)}) custom-call(f32[128,128]{1,0:T(8,128)S(1)} %bitcast.19, f32[8,128]{1,0:T(8,128)S(1)} %get-tuple-element.148.refs_1_, f32[3,64,128]{2,1,0:T(8,128)S(1)} %get-tuple-element.149.refs_2_, ...), custom_call_target="tpu_custom_call" | custom-call | flops 1000000 | bytes 1000000 | tf_op jit(solution)/shard_map/room2/pallas_call | solution.py:503
  71.5 0.0 collective-permute-done.8.refs_11_
  71.5 0.0 collective-permute-done.9.refs_12_
  71.5 0.4 send3.1
  72.0 9.5 %all_to_all.47 = f32[16,8,128]{2,1,0:T(8,128)S(1)} all-to-all(f32[16,8,128]{2,1,0:T(8,128)S(1)} %bitcast.23), channel_id=1, replica_groups=mesh['district'=16,'tile'=16] {'tile'}, dimensions={0} | all-to-all | bytes 131072 | tf_op jit(solution)/shard_map/all_to_all | solution.py:602
  81.5 1.1 %final.1 = (f32[3,16,128]{2,1,0:T(8,128)}, f32[3,64,128]{2,1,0:T(8,128)}, f32[3,64,128]{2,1,0:T(8,128)}) custom-call(f32[128,128]{1,0:T(8,128)S(1)} %bitcast.22, f32[64,128]{1,0:T(8,128)S(1)} %get-tuple-element.164.eta, f32[128,128]{1,0:T(8,128)S(1)} %get-tuple-element.165.street, bf16[64,256]{1,0:T(8,128)(2,1)S(1)} %get-tuple-element.98.row_t2, ...), custom_call_target="tpu_custom_call" | custom-call | flops 1000000 | bytes 1000000 | tf_op jit(solution)/shard_map/final/pallas_call | solution.py:503
  (18 shorter events, 0.0 us)
Async XLA Ops:
  0.6 13.3 %copy-start.6 = (f32[3,64,128]{2,1,0:T(8,128)S(1)}, f32[3,64,128]{2,1,0:T(8,128)}, u32[]{:S(2)}) copy-start(f32[3,64,128]{2,1,0:T(8,128)} %room.1) | copy-start | bytes 294916
  0.6 13.3 %copy-start.7 = (s32[64]{0:T(128)S(1)}, s32[64]{0:T(128)}, u32[]{:S(2)}) copy-start(s32[64]{0:T(128)} %param.22) | copy-start | bytes 772
  0.7 13.3 %copy-start.8 = (s32[64]{0:T(128)S(1)}, s32[64]{0:T(128)}, u32[]{:S(2)}) copy-start(s32[64]{0:T(128)} %param.23) | copy-start | bytes 772
  0.7 13.3 %copy-start.9 = (s32[64,1]{0,1:T(1,128)S(1)}, s32[64,1]{0,1:T(1,128)}, u32[]{:S(2)}) copy-start(s32[64,1]{0,1:T(1,128)} %param.24) | copy-start | bytes 772
  0.7 13.3 %copy-start.10 = (s32[64]{0:T(128)S(1)}, s32[64]{0:T(128)}, u32[]{:S(2)}) copy-start(s32[64]{0:T(128)} %param.25) | copy-start | bytes 772
  0.7 13.3 %copy-start.11 = (f32[64]{0:T(128)S(1)}, f32[64]{0:T(128)}, u32[]{:S(2)}) copy-start(f32[64]{0:T(128)} %param.26) | copy-start | bytes 772
  0.7 13.3 %copy-start.12 = (s32[1,16,2]{1,2,0:T(2,128)S(1)}, s32[1,16,2]{1,2,0:T(2,128)}, u32[]{:S(2)}) copy-start(s32[1,16,2]{1,2,0:T(2,128)} %param.21) | copy-start | bytes 388
  0.7 13.3 %copy-start.13 = (s32[1,128]{1,0:T(1,128)S(1)}, s32[1,128]{1,0:T(1,128)}, u32[]{:S(2)}) copy-start(s32[1,128]{1,0:T(1,128)} %door.1) | copy-start | bytes 1540
  0.7 13.3 %copy-start.1 = (s32[4,64,128]{2,1,0:T(8,128)S(1)}, s32[4,64,128]{2,1,0:T(8,128)}, u32[]{:S(2)}) copy-start(s32[4,64,128]{2,1,0:T(8,128)} %refs_3_.12) | copy-start | bytes 393220
  0.7 15.6 %copy-start.3 = (f32[3,64,128]{2,1,0:T(8,128)S(1)}, f32[3,64,128]{2,1,0:T(8,128)}, u32[]{:S(2)}) copy-start(f32[3,64,128]{2,1,0:T(8,128)} %refs_3_.7) | copy-start | bytes 294916
  2.6 13.7 %copy-start = (s32[4,64,128]{2,1,0:T(8,128)S(1)}, s32[4,64,128]{2,1,0:T(8,128)}, u32[]{:S(2)}) copy-start(s32[4,64,128]{2,1,0:T(8,128)} %refs_3_.13) | copy-start | bytes 393220
  2.6 12.3 %collective-permute-start = (f32[16,128]{1,0:T(8,128)}, f32[16,128]{1,0:T(8,128)S(1)}, u32[]{:S(2)}, u32[]{:S(2)}) collective-permute-start(f32[16,128]{1,0:T(8,128)} %get-tuple-element.89), channel_id=1, source_target_pairs={{0,16},{16,32},{32,48},{48,64},{64,80},{80,96},{96,112},{112,128},... | collective-permute-start | bytes 24584 | tf_op jit(solution)/shard_map/ppermute | solution.py:517
  6.5 8.4 %collective-permute-start.1 = (f32[16,128]{1,0:T(8,128)}, f32[16,128]{1,0:T(8,128)S(1)}, u32[]{:S(2)}, u32[]{:S(2)}) collective-permute-start(f32[16,128]{1,0:T(8,128)} %get-tuple-element.90), channel_id=1, source_target_pairs={{16,0},{32,16},{48,32},{64,48},{80,64},{96,80},{112,96},{128,112},... | collective-permute-start | bytes 24584 | tf_op jit(solution)/shard_map/ppermute | solution.py:522
  11.8 3.7 %collective-permute-start.3 = (f32[16,128]{1,0:T(8,128)}, f32[16,128]{1,0:T(8,128)S(1)}, u32[]{:S(2)}, u32[]{:S(2)}) collective-permute-start(f32[16,128]{1,0:T(8,128)} %get-tuple-element.91), channel_id=1, source_target_pairs={{1,0},{2,1},{3,2},{4,3},{5,4},{6,5},{7,6},{8,7},{9,8},{10,9},{11,1... | collective-permute-start | bytes 24584 | tf_op jit(solution)/shard_map/ppermute | solution.py:522
  12.8 3.5 %collective-permute-start.2 = (f32[16,128]{1,0:T(8,128)}, f32[16,128]{1,0:T(8,128)S(1)}, u32[]{:S(2)}, u32[]{:S(2)}) collective-permute-start(f32[16,128]{1,0:T(8,128)} %get-tuple-element.91), channel_id=1, source_target_pairs={{0,1},{1,2},{2,3},{3,4},{4,5},{5,6},{6,7},{7,8},{8,9},{9,10},{10,1... | collective-permute-start | bytes 24584 | tf_op jit(solution)/shard_map/ppermute | solution.py:517
  14.0 2.3 %copy-start.2 = (f32[64,128]{1,0:T(8,128)S(1)}, f32[64,128]{1,0:T(8,128)}, u32[]{:S(2)}) copy-start(f32[64,128]{1,0:T(8,128)} %refs_2_.7) | copy-start | bytes 98308
  14.0 2.3 %copy-start.4 = (f32[16,128]{1,0:T(8,128)S(1)}, f32[16,128]{1,0:T(8,128)}, u32[]{:S(2)}) copy-start(f32[16,128]{1,0:T(8,128)} %refs_1_.7) | copy-start | bytes 24580
  14.0 2.3 %copy-start.5 = (f32[3,16,128]{2,1,0:T(8,128)S(1)}, f32[3,16,128]{2,1,0:T(8,128)}, u32[]{:S(2)}) copy-start(f32[3,16,128]{2,1,0:T(8,128)} %refs_1_.4) | copy-start | bytes 73732
  29.9 7.1 %collective-permute-start.4 = (f32[8,128]{1,0:T(8,128)S(1)}, f32[8,128]{1,0:T(8,128)S(1)}, u32[]{:S(2)}, u32[]{:S(2)}) collective-permute-start(f32[8,128]{1,0:T(8,128)S(1)} %get-tuple-element.114), channel_id=1, source_target_pairs={{0,16},{16,32},{32,48},{48,64},{64,80},{80,96},{96,112},{112,128},... | collective-permute-start | bytes 12296 | tf_op jit(solution)/shard_map/ppermute | solution.py:517
  29.9 7.1 %collective-permute-start.5 = (f32[8,128]{1,0:T(8,128)S(1)}, f32[8,128]{1,0:T(8,128)S(1)}, u32[]{:S(2)}, u32[]{:S(2)}) collective-permute-start(f32[8,128]{1,0:T(8,128)S(1)} %get-tuple-element.115), channel_id=1, source_target_pairs={{16,0},{32,16},{48,32},{64,48},{80,64},{96,80},{112,96},{128,112},... | collective-permute-start | bytes 12296 | tf_op jit(solution)/shard_map/ppermute | solution.py:522
  47.1 7.1 %collective-permute-start.6 = (f32[8,128]{1,0:T(8,128)S(1)}, f32[8,128]{1,0:T(8,128)S(1)}, u32[]{:S(2)}, u32[]{:S(2)}) collective-permute-start(f32[8,128]{1,0:T(8,128)S(1)} %get-tuple-element.133), channel_id=1, source_target_pairs={{0,16},{16,32},{32,48},{48,64},{64,80},{80,96},{96,112},{112,128},... | collective-permute-start | bytes 12296 | tf_op jit(solution)/shard_map/ppermute | solution.py:517
  47.8 6.4 %collective-permute-start.7 = (f32[8,128]{1,0:T(8,128)S(1)}, f32[8,128]{1,0:T(8,128)S(1)}, u32[]{:S(2)}, u32[]{:S(2)}) collective-permute-start(f32[8,128]{1,0:T(8,128)S(1)} %get-tuple-element.134), channel_id=1, source_target_pairs={{16,0},{32,16},{48,32},{64,48},{80,64},{96,80},{112,96},{128,112},... | collective-permute-start | bytes 12296 | tf_op jit(solution)/shard_map/ppermute | solution.py:522
  64.4 7.1 %collective-permute-start.8 = (f32[8,128]{1,0:T(8,128)S(1)}, f32[8,128]{1,0:T(8,128)S(1)}, u32[]{:S(2)}, u32[]{:S(2)}) collective-permute-start(f32[8,128]{1,0:T(8,128)S(1)} %get-tuple-element.152), channel_id=1, source_target_pairs={{0,16},{16,32},{32,48},{48,64},{64,80},{80,96},{96,112},{112,128},... | collective-permute-start | bytes 12296 | tf_op jit(solution)/shard_map/ppermute | solution.py:517
  64.4 7.1 %collective-permute-start.9 = (f32[8,128]{1,0:T(8,128)S(1)}, f32[8,128]{1,0:T(8,128)S(1)}, u32[]{:S(2)}, u32[]{:S(2)}) collective-permute-start(f32[8,128]{1,0:T(8,128)S(1)} %get-tuple-element.153), channel_id=1, source_target_pairs={{16,0},{32,16},{48,32},{64,48},{80,64},{96,80},{112,96},{128,112},... | collective-permute-start | bytes 12296 | tf_op jit(solution)/shard_map/ppermute | solution.py:522

commit v4 on v3

--- a/solution.py
+++ b/solution.py
@@ -28,6 +28,8 @@
 L_PCOL = 72
 L_WIN = 80
 L_CCOL = 96
+L_CROW = 64
+L_PROW = 96
 
 
 def lane(shape):
@@ -82,6 +84,36 @@
 def unpack2(left, right, at, groups):
     chosen = jnp.where(lane(left.shape) % 2 == 1, right, left)
     return jnp.concatenate([roll(chosen, -(at + 2 * g + 1)) for g in range(groups)], 0)
+
+
+def pack_rows(packed, rows, at):
+    shape = packed.shape
+    both = jnp.where(sub(shape) < 4, rows[0:1], rows[1:2])
+    inside = (lane(shape) >= at) & (lane(shape) < at + R)
+    for k in range(4):
+        packed = jnp.where(inside & ((sub(shape) & 3) == k), roll(both, at - R * k), packed)
+    return packed
+
+
+def unpack_rows(packed, at):
+    shape = packed.shape
+    spread = jnp.zeros(shape, f32)
+    for k in range(4):
+        spread = jnp.where(((sub(shape) & 3) == k) & (lane(shape) // R == k), roll(packed, R * k - at), spread)
+    return jnp.sum(spread[0:4], axis=0, keepdims=True), jnp.sum(spread[4:8], axis=0, keepdims=True)
+
+
+def odd_tile():
+    return lax.rem(lax.axis_index("tile"), 2) == 1
+
+
+def sibling():
+    tile = lax.axis_index("tile")
+    return tile + 1 - 2 * lax.rem(tile, 2)
+
+
+def for_me(inbox):
+    return inbox[:, 0:CAP].reshape(SLOTS, LANES)
 
 
 def advance(eta_x, u_x, v, v_h, eta_h, q, q_up, q_dn, q_h, flux_x, rows):
@@ -265,13 +297,23 @@
     face[...], reply[...] = room_reply(eta, both, fixed_now)
 
 
-def near_kernel(left, right, row2, row_t2, index, gain):
+def near_kernel(first, second, row2, row_t2, index, gain, sib_index, sib_gain, sib_first, sib_t2):
+    left, right = before_after(first[...], second[...])
     shape = (SLOTS, LANES)
     at_lane = lane(shape)
+    row, col, weight = slots_of(first[...])
+    row = row - jnp.where(odd_tile(), CX - 2, 0)
+    sib_index[...] = (at_lane - col + L_ROOM) & (LANES - 1)
+    touched = (at_lane >= col) & (at_lane < col + R) & (row >= 0) & (row < 2)
+    sib_gain[...] = jnp.where(touched, area_ratio * weight, 0.0)
+    sib_first[...] = jnp.where(jnp.broadcast_to(row, shape) == 0, 1.0, 0.0)
+    chosen = jnp.where((at_lane == row) & (row < 2), 1.0, 0.0)
+    turned_8 = jnp.transpose(chosen)[0:16]
+    sib_t2[...] = jnp.concatenate([turned_8, turned_8], 1).astype(bf16)
     turned = []
     for part, side in enumerate((right, left)):
         rows = slice(part * SLOTS, (part + 1) * SLOTS)
-        row, col, weight = slots_of(side[...])
+        row, col, weight = slots_of(side)
         chosen = jnp.where(at_lane == row, 1.0, 0.0)
         row2[rows] = (chosen + roll(chosen, CX)).astype(bf16)
         turned.append(jnp.transpose(chosen)[0:CX].astype(bf16))
@@ -285,6 +327,11 @@
     row_t2[...] = jnp.concatenate(turned + turned, 1)
 
 
+def before_after(first, second):
+    odd = odd_tile()
+    return jnp.where(odd, first, second), jnp.where(odd, second, first)
+
+
 def gate(there, cells):
     return jnp.where(there, cells, 0.0)
 
@@ -296,7 +343,7 @@
     last = step == STEPS - 1
     if step == 0:
         (
-            place, parent, parent_depth, child, child_depth, child_wet, above0, below0, left0, right0, reply, row2, index_s,
+            place, parent, parent_depth, child, child_depth, child_wet, above0, below0, cols0, cols1, reply, row2, index_s,
             eta_o, u_o, v_o, peta_o, pu_o, pv_o, street_o, out, *more, eta_x, flux_x, u_x, peta_x, pflux_x, pu_x,
         ) = refs
         u_x[8 : 8 + CX] = child[1]
@@ -311,24 +358,28 @@
         eta_x[8 + CX : 10 + CX] = gate(has_below, below0[0:2])
         peta_x[6:8] = gate(has_above, above0[7:9])
         peta_x[8 + PX : 10 + PX] = gate(has_below, below0[7:9])
-        left, right = gate(has_left, left0[0:8]), gate(has_right, right0[0:8])
+        left, right = before_after(cols0[0:8], cols1[0:8])
+        left, right = gate(has_left, left), gate(has_right, right)
         v, v_h = child[2], unpack2(left, right, 32, 8)
         eta_h = unpack4(left, right, 0, 8)
         pv, pv_h = parent[2], unpack2(left, right, 120, 2)
         peta_h = unpack4(left, right, 112, 2)
     else:
         (
-            place, parent_depth, child_depth, child_wet, above0, below0, left0, right0, reply, row2, index_s,
-            above, below, eta_i, u_x, v_i, vh_i, etah_i, peta_i, pu_x, pv_i, pvh_i, petah_i,
+            place, parent_depth, child_depth, child_wet, above0, below0, cols0, cols1, reply, row2, index_s,
+            moved, swapped, eta_i, u_x, v_i, vh_i, etah_i, peta_i, pu_x, pv_i, pvh_i, petah_i,
             eta_o, u_o, v_o, peta_o, pu_o, pv_o, street_o, out, *more, eta_x, flux_x, peta_x, pflux_x,
         ) = refs
+        mine, other = moved[0:4], swapped[4:8]
+        above, below = jnp.where(odd_tile(), mine, other), jnp.where(odd_tile(), other, mine)
         eta_x[8 : 8 + CX] = eta_i[...]
         peta_x[8 : 8 + PX] = peta_i[...]
         eta_x[6:8] = gate(has_above, above[0:2])
         eta_x[8 + CX : 10 + CX] = gate(has_below, below[0:2])
         peta_x[6:8] = gate(has_above, above[2:4])
         peta_x[8 + PX : 10 + PX] = gate(has_below, below[2:4])
-        left, right = gate(has_left, left0[0:8]), gate(has_right, right0[0:8])
+        left, right = before_after(cols0[0:8], cols1[0:8])
+        left, right = gate(has_left, left), gate(has_right, right)
         v, v_h, eta_h = v_i[...], vh_i[...], etah_i[...]
         pv, pv_h, peta_h = pv_i[...], pvh_i[...], petah_i[...]
     wet = child_wet[step].astype(f32)
@@ -372,9 +423,16 @@
     window = jnp.where((index >= 0) & (index < LANES), window, 0.0)
     common = jnp.where((at_lane >= L_WIN) & (at_lane < L_CCOL), window, common)
     street = along(street, index_s[...])
+    if not last:
+        odd = odd_tile()
+        rest = pack_rows(jnp.zeros(shape, f32), jnp.where(odd, eta[0:2], eta[CX - 2 : CX]), L_CROW)
+        rest = pack_rows(rest, jnp.where(odd, peta[0:2], peta[PX - 2 : PX]), L_PROW)
     for t in range(TILES):
         rows = slice(t * CAP, (t + 1) * CAP)
-        out[rows] = jnp.where(at_lane < R, street[rows], jnp.where(at_lane < L_PCOL, reply[rows], common))
+        out[t, 0:CAP] = jnp.where(at_lane < R, street[rows], jnp.where(at_lane < L_PCOL, reply[rows], common))
+        if not last:
+            rows = slice((t ^ 1) * CAP, ((t ^ 1) + 1) * CAP)
+            out[t, CAP : 2 * CAP] = jnp.where(at_lane < L_NEAR, reply[rows], rest)
 
 
 def windows_sum(inbox):
@@ -422,25 +480,39 @@
     return weight * (levels - face)
 
 
-def street_kernel(inbox, eta, street, row_t2, index_a, gain, lower, peta, eta_o, up, dn, windows_o):
-    eta, windows_o[...] = street_update(
-        inbox[...], eta[...], street[...], row_t2[...], index_a[...], gain[...], lower[...]
+def street_kernel(
+    inbox, eta, street, row_t2, index_a, gain, lower, peta, sib_index, sib_gain, sib_first, sib_t2, eta_o, message, windows_o
+):
+    eta, windows = street_update(
+        for_me(inbox), eta[...], street[...], row_t2[...], index_a[...], gain[...], lower[...]
     )
     eta_o[...] = eta
-    blank = jnp.zeros((4, LANES), f32)
-    up[0:2] = eta[0:2]
-    up[2:4] = peta[0:2]
-    up[4:8] = blank
-    dn[0:2] = eta[CX - 2 : CX]
-    dn[2:4] = peta[PX - 2 : PX]
-    dn[4:8] = blank
+    windows_o[...] = windows
+    odd = odd_tile()
+    shape = (8, LANES)
+    packed = inbox[sibling(), CAP : 2 * CAP]
+    row0, row1 = unpack_rows(packed, L_CROW)
+    prow0, prow1 = unpack_rows(packed, L_PROW)
+    target = along(windows, jnp.full(shape, L_WIN, i32) + sibling())
+    target = jnp.where((sub(shape) & 3) == lane(shape) // R, target, 0.0)
+    target = jnp.sum(jnp.where(odd, target[4:8], target[0:4]), axis=0, keepdims=True)
+    row0, row1 = nudge(row0, target), nudge(row1, target)
+    levels = jnp.where(sib_first[...] > 0, row0, row1)
+    sums = along(inbox[:, CAP : 2 * CAP].reshape(SLOTS, LANES), sib_index[...])
+    lost = pick(sib_t2[...], sib_gain[...] * (4.0 * levels - sums))
+    message[0:2] = jnp.where(odd, eta[CX - 2 : CX], eta[0:2])
+    message[2:4] = jnp.where(odd, peta[PX - 2 : PX], peta[0:2])
+    message[4:5] = row0 - lost[0:1]
+    message[5:6] = row1 - lost[1:2]
+    message[6:7] = prow0
+    message[7:8] = prow1
 
 
 def room_kernel(
     step, inbox, windows, room, room_wet, face, door2, door_t2, fixed, near2, near_t2, near_index, near_gain,
     room_new, face_o, reply, etah_o, petah_o, eta_x, flux_x,
 ):
-    received = inbox[...]
+    received = for_me(inbox)
     flow = room_flow(received, windows[...], face[...])
     eta = room[0] + pick(door_t2[...], flow)
     eta, u, v = room_advance(eta, room[1], room[2], room_wet[step].astype(f32), eta_x, flux_x)
@@ -449,8 +521,8 @@
     room_new[2] = v
     face_o[...], reply[...] = room_reply(eta, door2[...], fixed[...])
     tile = lax.axis_index("tile")
-    left = inbox[pl.ds(pl.multiple_of(8 * lax.rem(tile + TILES - 1, TILES), 8), 8)]
-    right = inbox[pl.ds(pl.multiple_of(8 * lax.rem(tile + 1, TILES), 8), 8)]
+    left = inbox[lax.rem(tile + TILES - 1, TILES), 0:CAP]
+    right = inbox[lax.rem(tile + 1, TILES), 0:CAP]
     at_lane = lane((8, LANES))
 
     def kept(cells):
@@ -480,7 +552,7 @@
     copies = [pltpu.make_async_copy(src, dst, done.at[k]) for k, (src, dst) in enumerate(pairs)]
     for copy in copies[:-2]:
         copy.start()
-    received = inbox[...]
+    received = for_me(inbox)
     child_eta[...], windows = street_update(
         received, eta[...], street[...], row_t2[...], index_a[...], gain[...], lower[...]
     )
@@ -520,6 +592,23 @@
 def to_previous(cells, axis):
     count = lax.axis_size(axis)
     return lax.ppermute(cells, axis, [((i + 1) % count, i) for i in range(count)])
+
+
+def snake(cells):
+    districts, tiles = lax.axis_size("district"), lax.axis_size("tile")
+    pairs = []
+    for d in range(districts):
+        for t in range(tiles):
+            to = d + 1 if t % 2 else d - 1
+            target = (to, t) if 0 <= to < districts else (d, t ^ 1)
+            pairs.append((d * tiles + t, target[0] * tiles + target[1]))
+    return lax.ppermute(cells, ("district", "tile"), pairs)
+
+
+def swap(cells, axis, which):
+    count = lax.axis_size(axis)
+    partner = [i + 1 if i % 2 == which else i - 1 for i in range(count)]
+    return lax.ppermute(cells, axis, [(i, p if 0 <= p < count else i) for i, p in enumerate(partner)])
 
 
 def body(
@@ -557,8 +646,7 @@
         reads=HBM,
         limit=60,
     )
-    left0 = to_next(side, "tile")
-    right0 = to_previous(side, "tile")
+    cols0, cols1 = swap(side, "tile", 0), swap(side, "tile", 1)
     row2, row_t2, index_s, index_a, gain, lower, fixed, door2, door_t2, room, face, reply, place = call(
         "setup",
         setup_kernel,
@@ -577,25 +665,26 @@
         near_kernel,
         [
             sds(2 * SLOTS, LANES, dtype=bf16), sds(CX, 4 * SLOTS, dtype=bf16), sds(2 * SLOTS, LANES, dtype=i32),
-            sds(2 * SLOTS, LANES),
+            sds(2 * SLOTS, LANES), sds(SLOTS, LANES, dtype=i32), grid, grid, sds(16, 2 * SLOTS, dtype=bf16),
         ],
-        [left0, right0],
-    )
+        [cols0, cols1],
+    )
+    near, siblings = near[:4], near[4:]
     for step in range(STEPS):
         with_step = lambda *refs, step=step: send_kernel(step, *refs)
         if step == 0:
             args = [
-                place, parent_state, parent_depth, child_state, child_depth, child_wet, above0, below0, left0, right0,
+                place, parent_state, parent_depth, child_state, child_depth, child_wet, above0, below0, cols0, cols1,
                 reply, row2, index_s,
             ]
             scratch = (CX + 16,) * 3 + (PX + 16,) * 3
         else:
             args = [
-                place, parent_depth, child_depth, child_wet, above0, below0, left0, right0, reply, row2, index_s,
-                above, below, eta, u, v, v_h, eta_h, peta, pu, pv, pv_h, peta_h,
+                place, parent_depth, child_depth, child_wet, above0, below0, cols0, cols1, reply, row2, index_s,
+                moved, swapped, eta, u, v, v_h, eta_h, peta, pu, pv, pv_h, peta_h,
             ]
             scratch = (CX + 16,) * 2 + (PX + 16,) * 2
-        outs = [block, tall, block, pblock, ptall, pblock, grid, grid]
+        outs = [block, tall, block, pblock, ptall, pblock, grid, sds(TILES, CAP if step == STEPS - 1 else 2 * CAP, LANES)]
         if step < STEPS - 1:
             outs += [block, pblock]
         eta, u, v, peta, pu, pv, street, outbox, *more = call(f"send{step}", with_step, outs, args, scratch=scratch)
@@ -613,9 +702,10 @@
                 )
             )
         v_h, pv_h = more
-        eta, up, dn, windows = call(f"street{step}", street_kernel, [block, tile8, tile8, tile8], shared + [peta])
-        below = to_previous(up, "district")
-        above = to_next(dn, "district")
+        eta, message, windows = call(
+            f"street{step}", street_kernel, [block, tile8, tile8], [*shared, peta, *siblings]
+        )
+        moved = snake(message)
         with_step = lambda *refs, step=step: room_kernel(step + 1, *refs)
         room, face, reply, eta_h, peta_h = call(
             f"room{step}",
@@ -624,6 +714,8 @@
             [inbox, windows, room, interior_wet, face, door2, door_t2, fixed, *near],
             scratch=(CX + 16, CX + 16),
         )
+        moved, reply = lax.optimization_barrier((moved, reply))
+        swapped = swap(moved, "tile", 0)
 
 
 def solution(mesh):

time: 82.8 us -> 80.1 us (0.967); the launches traced: 82.6 us -> 78.9 us
  blocking collectives: 41.3 us -> 26.6 us
  waiting for transfers between devices: 1.37 us -> 8.86 us
  starting transfers between devices: 29.3 us -> 31.9 us
  Pallas kernels: 9.67 us -> 10.6 us
    ppermute x5 -> x1, starting transfers between devices: 23.5 us -> 5.31 us  [to_previous(): lax.ppermute(cells, axis, [((i + 1) % count, i) for i in range(count)])]
    ppermute x0 -> x8, starting transfers between devices: none -> 16.5 us  [the longest x5 14.6 us: swap(): lax.ppermute(cells, axis, [(i, p if 0 <= p < count else i) for i, p in en...]
    all_to_all x4 -> x3, blocking collectives: 41.3 us -> 26.6 us  [body(): lax.all_to_all(outbox, 'tile', split_axis=0, concat_axis=0, tiled=True)]
    all_to_all x0 -> x1, starting transfers between devices: none -> 6.12 us  [body(): lax.all_to_all(outbox, 'tile', split_axis=0, concat_axis=0, tiled=True)]
    all_to_all x0 -> x1, waiting for transfers between devices: none -> 5.53 us  [body(): lax.all_to_all(outbox, 'tile', split_axis=0, concat_axis=0, tiled=True)]
    ppermute x0 -> x8, waiting for transfers between devices: none -> 3.32 us  [the longest x5 2.9 us: swap(): lax.ppermute(cells, axis, [(i, p if 0 <= p < count else i) for i, p in en...]
    ppermute x5 -> x1, starting transfers between devices: 5.77 us -> 3.9 us  [to_next(): lax.ppermute(cells, axis, [(i, (i + 1) % count) for i in range(count)])]
    pallas_call x14, Pallas kernels: 9.67 us -> 10.6 us  [call(): pl.pallas_call(kernel, out_shape=outs, in_specs=[reads] * len(args), out_...]
  transfers between devices with their start and end apart: 10 -> 11, of which waited for: 2 -> 7; matrix products, arithmetic and copies ran while one was open for 0% -> 0% of each run, Pallas kernels for 5% -> 6%
where the time goes in v4:
time: 80.1 us; the launch traced here: 78.9 us
  starting transfers between devices  31.9 us (40%)
  blocking collectives  26.6 us (33%)
  Pallas kernels  10.6 us (13%)
  waiting for transfers between devices  8.86 us (11%)
  between operations  0.95 us (1%)
    all_to_all x3, blocking collectives, body(): lax.all_to_all(outbox, 'tile', split_axis=0, concat_axis=0, tiled=True)  26.6 us
    ppermute x5, starting transfers between devices, swap(): lax.ppermute(cells, axis, [(i, p if 0 <= p < count else i) for i, p in en...  14.6 us
    pallas_call x14, Pallas kernels, call(): pl.pallas_call(kernel, out_shape=outs, in_specs=[reads] * len(args), out_...  10.6 us
    all_to_all x1, starting transfers between devices, body(): lax.all_to_all(outbox, 'tile', split_axis=0, concat_axis=0, tiled=True)  6.12 us
    all_to_all x1, waiting for transfers between devices, body(): lax.all_to_all(outbox, 'tile', split_axis=0, concat_axis=0, tiled=True)  5.53 us
    ppermute x1, starting transfers between devices, to_previous(): lax.ppermute(cells, axis, [((i + 1) % count, i) for i in range(count)])  5.31 us
    ppermute x1, starting transfers between devices, to_next(): lax.ppermute(cells, axis, [(i, (i + 1) % count) for i in range(count)])  3.9 us
    ppermute x5, waiting for transfers between devices, swap(): lax.ppermute(cells, axis, [(i, p if 0 <= p < count else i) for i, p in en...  2.9 us
  transfers between devices with their start and end apart: 11, of which 7 were waited for; matrix products, arithmetic and copies ran while one was open for 0% of the time, Pallas kernels for 6%

profile of v4, /device:TPU:1, one launch (start us, length us, event | category | flops | bytes accessed | tf_op | source)
XLA Modules:
  0.0 78.9 jit_solution(6702471979761012695)
XLA Ops:
  0.7 1.8 %edges.1 = (f32[16,128]{1,0:T(8,128)}, f32[16,128]{1,0:T(8,128)}, f32[16,128]{1,0:T(8,128)}) custom-call(f32[3,16,128]{2,1,0:T(8,128)} %refs_1_.4, f32[16,128]{1,0:T(8,128)} %refs_1_.7, f32[3,64,128]{2,1,0:T(8,128)} %refs_3_.7, f32[64,128]{1,0:T(8,128)} %refs_2_.7, s32[4,64,128]{2,1,0:T(8,128)} %refs_3_.13, s32[1,64]{1,0:T(1,128)} %bitcast.8, ...), custom_call_target="tpu_custom_call" | custom-call | flops 1000000 | bytes 1000000 | tf_op jit(solution)/shard_map/edges/pallas_call | solution.py:575
  2.6 0.0 copy-start
  2.6 3.9 %collective-permute-start = (f32[16,128]{1,0:T(8,128)}, f32[16,128]{1,0:T(8,128)S(1)}, u32[]{:S(2)}, u32[]{:S(2)}) collective-permute-start(f32[16,128]{1,0:T(8,128)} %get-tuple-element.96), channel_id=1, source_target_pairs={{0,16},{16,32},{32,48},{48,64},{64,80},{80,96},{96,112},{112,128},... | collective-permute-start | bytes 24584 | tf_op jit(solution)/shard_map/ppermute | solution.py:589
  6.5 5.3 %collective-permute-start.1 = (f32[16,128]{1,0:T(8,128)}, f32[16,128]{1,0:T(8,128)S(1)}, u32[]{:S(2)}, u32[]{:S(2)}) collective-permute-start(f32[16,128]{1,0:T(8,128)} %get-tuple-element.97), channel_id=1, source_target_pairs={{16,0},{32,16},{48,32},{64,48},{80,64},{96,80},{112,96},{128,112},... | collective-permute-start | bytes 24584 | tf_op jit(solution)/shard_map/ppermute | solution.py:594
  11.8 4.0 %collective-permute-start.3 = (f32[16,128]{1,0:T(8,128)}, f32[16,128]{1,0:T(8,128)S(1)}, u32[]{:S(2)}, u32[]{:S(2)}) collective-permute-start(f32[16,128]{1,0:T(8,128)} %get-tuple-element.98), channel_id=1, source_target_pairs={{0,0},{1,2},{2,1},{3,4},{4,3},{5,6},{6,5},{7,8},{8,7},{9,10},{10,9... | collective-permute-start | bytes 24584 | tf_op jit(solution)/shard_map/ppermute | solution.py:611
  15.9 0.1 collective-permute-start.2
  16.0 0.0 copy-done.6
  16.0 0.0 copy-done.7
  16.0 0.0 copy-done.8
  16.0 0.0 copy-done.9
  16.0 0.0 copy-done.10
  16.0 0.0 copy-start.2
  16.1 0.0 copy-start.4
  16.1 0.0 copy-start.5
  16.1 0.8 %setup.1 = (bf16[128,128]{1,0:T(8,128)(2,1)S(1)}, bf16[64,256]{1,0:T(8,128)(2,1)S(1)}, s32[128,128]{1,0:T(8,128)S(1)}, s32[128,128]{1,0:T(8,128)S(1)}, f32[128,1...) custom-call(s32[1,64]{1,0:T(1,128)S(1)} %bitcast.9, ...), custom_call_target="tpu_custom_call" | custom-call | flops 1000000 | bytes 1000000 | tf_op jit(solution)/shard_map/setup/pallas_call | solution.py:575
  16.9 0.0 collective-permute-done.refs_6_.refs_4_
  16.9 0.0 collective-permute-done.1.refs_7_.refs_5_
  17.0 0.4 collective-permute-done.3.refs_9_.second.refs_7_
  17.4 0.0 collective-permute-done.2.refs_8_.first.refs_6_
  17.4 1.2 %send0.1 = (f32[64,128]{1,0:T(8,128)S(1)}, f32[80,128]{1,0:T(8,128)S(1)}, f32[64,128]{1,0:T(8,128)S(1)}, f32[16,128]{1,0:T(8,128)S(1)}, f32[32,128]{1,0:T(8,128)...) custom-call(s32[16,128]{1,0:T(8,128)S(1)} %get-tuple-element.95.refs, ...), custom_call_target="tpu_custom_call" | custom-call | flops 1000000 | bytes 1000000 | tf_op jit(solution)/shard_map/send0/pallas_call | solution.py:575
  18.6 6.1 %all-to-all-start = ((f32[16,16,128]{2,1,0:T(8,128)}), f32[16,16,128]{2,1,0:T(8,128)S(1)}, u32[]{:S(2)}, u32[]{:S(2)}) async-start(f32[16,16,128]{2,1,0:T(8,128)} %get-tuple-element.102), calls=%async_computation | async-start | bytes 262144 | tf_op jit(solution)/shard_map/all_to_all | solution.py:691
  24.7 0.6 near.1
  25.4 5.5 %all-to-all-done.inbox.refs_0_ = f32[16,16,128]{2,1,0:T(8,128)S(1)} async-done(((f32[16,16,128]{2,1,0:T(8,128)}), f32[16,16,128]{2,1,0:T(8,128)S(1)}, u32[]{:S(2)}, u32[]{:S(2)}) %all-to-all-start) | async-done | bytes 131104 | tf_op jit(solution)/shard_map/all_to_all | solution.py:691
  30.9 0.3 street0.1
  31.2 0.1 collective-permute-start.4
  31.3 1.0 %room0.1 = (f32[3,64,128]{2,1,0:T(8,128)S(1)}, f32[128,128]{1,0:T(8,128)S(1)}, f32[128,128]{1,0:T(8,128)S(1)}, f32[64,128]{1,0:T(8,128)S(1)}, f32[16,128]{1,0:T(8,128)S(1)}) custom-call(f32[16,16,128]{2,1,0:T(8,128)S(1)} %all-to-all-done.inbox.refs_0_, f32[8,128]{1,0:T(8,128)S(1)} %get-tuple-element.115.refs_1_, ...), custom_call_target="tpu_custom_call" | custom-call | flops 1000000 | bytes 1000000 | tf_op jit(solution)/shard_map/room0/pallas_call | solution.py:575
  32.2 0.3 collective-permute-done.4.refs_11_
  32.6 3.9 %collective-permute-start.5 = (f32[8,128]{1,0:T(8,128)S(1)}, f32[8,128]{1,0:T(8,128)S(1)}, u32[]{:S(2)}, u32[]{:S(2)}) collective-permute-start(f32[8,128]{1,0:T(8,128)S(1)} %collective-permute-done.4.refs_11_), channel_id=1, source_target_pairs={{0,1},{1,0},{2,3},{3,2},{4,5},{5,4},{6,7},{7,6},{8,9},{9,8},{10,11... | collective-permute-start | bytes 12296 | tf_op jit(solution)/shard_map/ppermute | solution.py:611
  36.4 0.8 %collective-permute-done.5.refs_12_ = f32[8,128]{1,0:T(8,128)S(1)} collective-permute-done((f32[8,128]{1,0:T(8,128)S(1)}, f32[8,128]{1,0:T(8,128)S(1)}, u32[]{:S(2)}, u32[]{:S(2)}) %collective-permute-start.5) | collective-permute-done | bytes 4128 | tf_op jit(solution)/shard_map/ppermute | solution.py:611
  37.3 0.4 send1.1
  37.7 9.0 %all_to_all.20.inbox.refs_0_ = f32[16,16,128]{2,1,0:T(8,128)S(1)} all-to-all(f32[16,16,128]{2,1,0:T(8,128)S(1)} %get-tuple-element.137), channel_id=1, replica_groups=mesh['district'=16,'tile'=16] {'tile'}, dimensions={0} | all-to-all | bytes 262144 | tf_op jit(solution)/shard_map/all_to_all | solution.py:691
  46.7 0.3 street1.1
  47.0 0.3 collective-permute-start.6
  47.3 1.0 %room1.1 = (f32[3,64,128]{2,1,0:T(8,128)S(1)}, f32[128,128]{1,0:T(8,128)S(1)}, f32[128,128]{1,0:T(8,128)S(1)}, f32[64,128]{1,0:T(8,128)S(1)}, f32[16,128]{1,0:T(8,128)S(1)}) custom-call(f32[16,16,128]{2,1,0:T(8,128)S(1)} %all_to_all.20.inbox.refs_0_, f32[8,128]{1,0:T(8,128)S(1)} %get-tuple-element.142.refs_1_, f32[3,64,128]{2,1,0:T(8,128)S(1)} %get-tuple-element.143.refs_2_, ...), custom_call_target="tpu_custom_call" | custom-call | flops 1000000 | bytes 1000000 | tf_op jit(solution)/shard_map/room1/pallas_call | solution.py:575
  48.3 0.1 collective-permute-done.6.refs_11_
  48.4 3.8 %collective-permute-start.7 = (f32[8,128]{1,0:T(8,128)S(1)}, f32[8,128]{1,0:T(8,128)S(1)}, u32[]{:S(2)}, u32[]{:S(2)}) collective-permute-start(f32[8,128]{1,0:T(8,128)S(1)} %collective-permute-done.6.refs_11_), channel_id=1, source_target_pairs={{0,1},{1,0},{2,3},{3,2},{4,5},{5,4},{6,7},{7,6},{8,9},{9,8},{10,11... | collective-permute-start | bytes 12296 | tf_op jit(solution)/shard_map/ppermute | solution.py:611
  52.2 0.8 %collective-permute-done.7.refs_12_ = f32[8,128]{1,0:T(8,128)S(1)} collective-permute-done((f32[8,128]{1,0:T(8,128)S(1)}, f32[8,128]{1,0:T(8,128)S(1)}, u32[]{:S(2)}, u32[]{:S(2)}) %collective-permute-start.7) | collective-permute-done | bytes 4128 | tf_op jit(solution)/shard_map/ppermute | solution.py:611
  53.0 0.4 send2.1
  53.5 9.0 %all_to_all.21.inbox.refs_0_ = f32[16,16,128]{2,1,0:T(8,128)S(1)} all-to-all(f32[16,16,128]{2,1,0:T(8,128)S(1)} %get-tuple-element.157), channel_id=1, replica_groups=mesh['district'=16,'tile'=16] {'tile'}, dimensions={0} | all-to-all | bytes 262144 | tf_op jit(solution)/shard_map/all_to_all | solution.py:691
  62.4 0.3 street2.1
  62.7 1.5 %collective-permute-start.8 = (f32[8,128]{1,0:T(8,128)S(1)}, f32[8,128]{1,0:T(8,128)S(1)}, u32[]{:S(2)}, u32[]{:S(2)}) collective-permute-start(f32[8,128]{1,0:T(8,128)S(1)} %get-tuple-element.161), channel_id=1, source_target_pairs={{0,1},{1,17},{2,3},{3,19},{4,5},{5,21},{6,7},{7,23},{8,9},{9,25},{... | collective-permute-start | bytes 12296 | tf_op jit(solution)/shard_map/ppermute | solution.py:605
  64.3 1.0 %room2.1 = (f32[3,64,128]{2,1,0:T(8,128)S(1)}, f32[128,128]{1,0:T(8,128)S(1)}, f32[128,128]{1,0:T(8,128)S(1)}, f32[64,128]{1,0:T(8,128)S(1)}, f32[16,128]{1,0:T(8,128)S(1)}) custom-call(f32[16,16,128]{2,1,0:T(8,128)S(1)} %all_to_all.21.inbox.refs_0_, f32[8,128]{1,0:T(8,128)S(1)} %get-tuple-element.162.refs_1_, f32[3,64,128]{2,1,0:T(8,128)S(1)} %get-tuple-element.163.refs_2_, ...), custom_call_target="tpu_custom_call" | custom-call | flops 1000000 | bytes 1000000 | tf_op jit(solution)/shard_map/room2/pallas_call | solution.py:575
  65.2 0.0 collective-permute-done.8.refs_11_
  65.2 2.7 %collective-permute-start.9 = (f32[8,128]{1,0:T(8,128)S(1)}, f32[8,128]{1,0:T(8,128)S(1)}, u32[]{:S(2)}, u32[]{:S(2)}) collective-permute-start(f32[8,128]{1,0:T(8,128)S(1)} %collective-permute-done.8.refs_11_), channel_id=1, source_target_pairs={{0,1},{1,0},{2,3},{3,2},{4,5},{5,4},{6,7},{7,6},{8,9},{9,8},{10,11... | collective-permute-start | bytes 12296 | tf_op jit(solution)/shard_map/ppermute | solution.py:611
  68.0 0.8 %collective-permute-done.9.refs_12_ = f32[8,128]{1,0:T(8,128)S(1)} collective-permute-done((f32[8,128]{1,0:T(8,128)S(1)}, f32[8,128]{1,0:T(8,128)S(1)}, u32[]{:S(2)}, u32[]{:S(2)}) %collective-permute-start.9) | collective-permute-done | bytes 4128 | tf_op jit(solution)/shard_map/ppermute | solution.py:611
  68.8 0.4 send3.1
  69.2 8.6 %all_to_all.22.inbox = f32[16,8,128]{2,1,0:T(8,128)S(1)} all-to-all(f32[16,8,128]{2,1,0:T(8,128)S(1)} %get-tuple-element.177), channel_id=1, replica_groups=mesh['district'=16,'tile'=16] {'tile'}, dimensions={0} | all-to-all | bytes 131072 | tf_op jit(solution)/shard_map/all_to_all | solution.py:691
  77.8 1.1 %final.1 = (f32[3,16,128]{2,1,0:T(8,128)}, f32[3,64,128]{2,1,0:T(8,128)}, f32[3,64,128]{2,1,0:T(8,128)}) custom-call(f32[16,8,128]{2,1,0:T(8,128)S(1)} %all_to_all.22.inbox, f32[64,128]{1,0:T(8,128)S(1)} %get-tuple-element.178.eta, f32[128,128]{1,0:T(8,128)S(1)} %get-tuple-element.179.street, bf16[64,256]{1,0:T(8,128)(2,1)S(1)} %get-tuple-element.105.row_t2, ...), custom_call_target="tpu_custom_call" | custom-call | flops 1000000 | bytes 1000000 | tf_op jit(solution)/shard_map/final/pallas_call | solution.py:575
  (19 shorter events, 0.0 us)
Async XLA Ops:
  0.6 15.3 %copy-start.6 = (f32[3,64,128]{2,1,0:T(8,128)S(1)}, f32[3,64,128]{2,1,0:T(8,128)}, u32[]{:S(2)}) copy-start(f32[3,64,128]{2,1,0:T(8,128)} %room.1) | copy-start | bytes 294916
  0.6 15.3 %copy-start.7 = (s32[64]{0:T(128)S(1)}, s32[64]{0:T(128)}, u32[]{:S(2)}) copy-start(s32[64]{0:T(128)} %param.22) | copy-start | bytes 772
  0.7 15.3 %copy-start.8 = (s32[64]{0:T(128)S(1)}, s32[64]{0:T(128)}, u32[]{:S(2)}) copy-start(s32[64]{0:T(128)} %param.23) | copy-start | bytes 772
  0.7 15.3 %copy-start.9 = (s32[64,1]{0,1:T(1,128)S(1)}, s32[64,1]{0,1:T(1,128)}, u32[]{:S(2)}) copy-start(s32[64,1]{0,1:T(1,128)} %param.24) | copy-start | bytes 772
  0.7 15.3 %copy-start.10 = (s32[64]{0:T(128)S(1)}, s32[64]{0:T(128)}, u32[]{:S(2)}) copy-start(s32[64]{0:T(128)} %param.25) | copy-start | bytes 772
  0.7 15.3 %copy-start.11 = (f32[64]{0:T(128)S(1)}, f32[64]{0:T(128)}, u32[]{:S(2)}) copy-start(f32[64]{0:T(128)} %param.26) | copy-start | bytes 772
  0.7 15.3 %copy-start.12 = (s32[1,16,2]{1,2,0:T(2,128)S(1)}, s32[1,16,2]{1,2,0:T(2,128)}, u32[]{:S(2)}) copy-start(s32[1,16,2]{1,2,0:T(2,128)} %param.21) | copy-start | bytes 388
  0.7 15.3 %copy-start.13 = (s32[1,128]{1,0:T(1,128)S(1)}, s32[1,128]{1,0:T(1,128)}, u32[]{:S(2)}) copy-start(s32[1,128]{1,0:T(1,128)} %door.1) | copy-start | bytes 1540
  0.7 15.3 %copy-start.1 = (s32[4,64,128]{2,1,0:T(8,128)S(1)}, s32[4,64,128]{2,1,0:T(8,128)}, u32[]{:S(2)}) copy-start(s32[4,64,128]{2,1,0:T(8,128)} %refs_3_.12) | copy-start | bytes 393220
  0.7 16.7 %copy-start.3 = (f32[3,64,128]{2,1,0:T(8,128)S(1)}, f32[3,64,128]{2,1,0:T(8,128)}, u32[]{:S(2)}) copy-start(f32[3,64,128]{2,1,0:T(8,128)} %refs_3_.7) | copy-start | bytes 294916
  2.6 14.8 %copy-start = (s32[4,64,128]{2,1,0:T(8,128)S(1)}, s32[4,64,128]{2,1,0:T(8,128)}, u32[]{:S(2)}) copy-start(s32[4,64,128]{2,1,0:T(8,128)} %refs_3_.13) | copy-start | bytes 393220
  2.6 14.3 %collective-permute-start = (f32[16,128]{1,0:T(8,128)}, f32[16,128]{1,0:T(8,128)S(1)}, u32[]{:S(2)}, u32[]{:S(2)}) collective-permute-start(f32[16,128]{1,0:T(8,128)} %get-tuple-element.96), channel_id=1, source_target_pairs={{0,16},{16,32},{32,48},{48,64},{64,80},{80,96},{96,112},{112,128},... | collective-permute-start | bytes 24584 | tf_op jit(solution)/shard_map/ppermute | solution.py:589
  6.5 10.4 %collective-permute-start.1 = (f32[16,128]{1,0:T(8,128)}, f32[16,128]{1,0:T(8,128)S(1)}, u32[]{:S(2)}, u32[]{:S(2)}) collective-permute-start(f32[16,128]{1,0:T(8,128)} %get-tuple-element.97), channel_id=1, source_target_pairs={{16,0},{32,16},{48,32},{64,48},{80,64},{96,80},{112,96},{128,112},... | collective-permute-start | bytes 24584 | tf_op jit(solution)/shard_map/ppermute | solution.py:594
  11.8 5.6 %collective-permute-start.3 = (f32[16,128]{1,0:T(8,128)}, f32[16,128]{1,0:T(8,128)S(1)}, u32[]{:S(2)}, u32[]{:S(2)}) collective-permute-start(f32[16,128]{1,0:T(8,128)} %get-tuple-element.98), channel_id=1, source_target_pairs={{0,0},{1,2},{2,1},{3,4},{4,3},{5,6},{6,5},{7,8},{8,7},{9,10},{10,9... | collective-permute-start | bytes 24584 | tf_op jit(solution)/shard_map/ppermute | solution.py:611
  15.9 1.5 %collective-permute-start.2 = (f32[16,128]{1,0:T(8,128)}, f32[16,128]{1,0:T(8,128)S(1)}, u32[]{:S(2)}, u32[]{:S(2)}) collective-permute-start(f32[16,128]{1,0:T(8,128)} %get-tuple-element.98), channel_id=1, source_target_pairs={{0,1},{1,0},{2,3},{3,2},{4,5},{5,4},{6,7},{7,6},{8,9},{9,8},{10,11... | collective-permute-start | bytes 24584 | tf_op jit(solution)/shard_map/ppermute | solution.py:611
  16.0 1.4 %copy-start.2 = (f32[64,128]{1,0:T(8,128)S(1)}, f32[64,128]{1,0:T(8,128)}, u32[]{:S(2)}) copy-start(f32[64,128]{1,0:T(8,128)} %refs_2_.7) | copy-start | bytes 98308
  16.1 1.4 %copy-start.4 = (f32[16,128]{1,0:T(8,128)S(1)}, f32[16,128]{1,0:T(8,128)}, u32[]{:S(2)}) copy-start(f32[16,128]{1,0:T(8,128)} %refs_1_.7) | copy-start | bytes 24580
  16.1 1.4 %copy-start.5 = (f32[3,16,128]{2,1,0:T(8,128)S(1)}, f32[3,16,128]{2,1,0:T(8,128)}, u32[]{:S(2)}) copy-start(f32[3,16,128]{2,1,0:T(8,128)} %refs_1_.4) | copy-start | bytes 73732
  18.6 12.3 %all-to-all-start = ((f32[16,16,128]{2,1,0:T(8,128)}), f32[16,16,128]{2,1,0:T(8,128)S(1)}, u32[]{:S(2)}, u32[]{:S(2)}) async-start(f32[16,16,128]{2,1,0:T(8,128)} %get-tuple-element.102), calls=%async_computation | async-start | bytes 262144 | tf_op jit(solution)/shard_map/all_to_all | solution.py:691
  31.2 1.4 %collective-permute-start.4 = (f32[8,128]{1,0:T(8,128)S(1)}, f32[8,128]{1,0:T(8,128)S(1)}, u32[]{:S(2)}, u32[]{:S(2)}) collective-permute-start(f32[8,128]{1,0:T(8,128)S(1)} %get-tuple-element.114), channel_id=1, source_target_pairs={{0,1},{1,17},{2,3},{3,19},{4,5},{5,21},{6,7},{7,23},{8,9},{9,25},{... | collective-permute-start | bytes 12296 | tf_op jit(solution)/shard_map/ppermute | solution.py:605
  32.6 4.7 %collective-permute-start.5 = (f32[8,128]{1,0:T(8,128)S(1)}, f32[8,128]{1,0:T(8,128)S(1)}, u32[]{:S(2)}, u32[]{:S(2)}) collective-permute-start(f32[8,128]{1,0:T(8,128)S(1)} %collective-permute-done.4.refs_11_), channel_id=1, source_target_pairs={{0,1},{1,0},{2,3},{3,2},{4,5},{5,4},{6,7},{7,6},{8,9},{9,8},{10,11... | collective-permute-start | bytes 12296 | tf_op jit(solution)/shard_map/ppermute | solution.py:611
  47.0 1.4 %collective-permute-start.6 = (f32[8,128]{1,0:T(8,128)S(1)}, f32[8,128]{1,0:T(8,128)S(1)}, u32[]{:S(2)}, u32[]{:S(2)}) collective-permute-start(f32[8,128]{1,0:T(8,128)S(1)} %get-tuple-element.141), channel_id=1, source_target_pairs={{0,1},{1,17},{2,3},{3,19},{4,5},{5,21},{6,7},{7,23},{8,9},{9,25},{... | collective-permute-start | bytes 12296 | tf_op jit(solution)/shard_map/ppermute | solution.py:605
  48.4 4.7 %collective-permute-start.7 = (f32[8,128]{1,0:T(8,128)S(1)}, f32[8,128]{1,0:T(8,128)S(1)}, u32[]{:S(2)}, u32[]{:S(2)}) collective-permute-start(f32[8,128]{1,0:T(8,128)S(1)} %collective-permute-done.6.refs_11_), channel_id=1, source_target_pairs={{0,1},{1,0},{2,3},{3,2},{4,5},{5,4},{6,7},{7,6},{8,9},{9,8},{10,11... | collective-permute-start | bytes 12296 | tf_op jit(solution)/shard_map/ppermute | solution.py:611
  62.7 2.5 %collective-permute-start.8 = (f32[8,128]{1,0:T(8,128)S(1)}, f32[8,128]{1,0:T(8,128)S(1)}, u32[]{:S(2)}, u32[]{:S(2)}) collective-permute-start(f32[8,128]{1,0:T(8,128)S(1)} %get-tuple-element.161), channel_id=1, source_target_pairs={{0,1},{1,17},{2,3},{3,19},{4,5},{5,21},{6,7},{7,23},{8,9},{9,25},{... | collective-permute-start | bytes 12296 | tf_op jit(solution)/shard_map/ppermute | solution.py:605
  65.2 3.5 %collective-permute-start.9 = (f32[8,128]{1,0:T(8,128)S(1)}, f32[8,128]{1,0:T(8,128)S(1)}, u32[]{:S(2)}, u32[]{:S(2)}) collective-permute-start(f32[8,128]{1,0:T(8,128)S(1)} %collective-permute-done.8.refs_11_), channel_id=1, source_target_pairs={{0,1},{1,0},{2,3},{3,2},{4,5},{5,4},{6,7},{7,6},{8,9},{9,8},{10,11... | collective-permute-start | bytes 12296 | tf_op jit(solution)/shard_map/ppermute | solution.py:611

commit v5 on v4

--- a/solution.py
+++ b/solution.py
@@ -578,7 +578,7 @@
         in_specs=[reads] * len(args),
         out_specs=[writes] * len(outs),
         scratch_shapes=[pltpu.VMEM((rows, LANES), f32) if isinstance(rows, int) else rows for rows in scratch],
-        compiler_params=pltpu.CompilerParams(vmem_limit_bytes=limit * 2**20),
+        compiler_params=pltpu.CompilerParams(vmem_limit_bytes=int(limit * 2**20)),
         cost_estimate=pl.CostEstimate(flops=1000000 * us, bytes_accessed=1000000 * us, transcendentals=0),
         name=name,
     )(*args)
@@ -644,7 +644,7 @@
         inputs,
         scratch=[pltpu.VMEM(a.shape, a.dtype) for a in inputs] + [pltpu.SemaphoreType.DMA((16,))],
         reads=HBM,
-        limit=60,
+        limit=53.89,
     )
     cols0, cols1 = swap(side, "tile", 0), swap(side, "tile", 1)
     row2, row_t2, index_s, index_a, gain, lower, fixed, door2, door_t2, room, face, reply, place = call(

time: 80.1 us -> 79.9 us (level)
  no operation moved by 1% of the time
where the time goes in v5:
time: 79.9 us; the launch traced here: 78.7 us
  starting transfers between devices  31.9 us (40%)
  blocking collectives  26.6 us (33%)
  Pallas kernels  9.96 us (12%)
  waiting for transfers between devices  8.7 us (11%)
  between operations  0.9 us (1%)
    all_to_all x3, blocking collectives, body(): lax.all_to_all(outbox, 'tile', split_axis=0, concat_axis=0, tiled=True)  26.6 us
    ppermute x5, starting transfers between devices, swap(): lax.ppermute(cells, axis, [(i, p if 0 <= p < count else i) for i, p in en...  14.6 us
    pallas_call x14, Pallas kernels, call(): pl.pallas_call(kernel, out_shape=outs, in_specs=[reads] * len(args), out_...  9.96 us
    all_to_all x1, starting transfers between devices, body(): lax.all_to_all(outbox, 'tile', split_axis=0, concat_axis=0, tiled=True)  6.12 us
    all_to_all x1, waiting for transfers between devices, body(): lax.all_to_all(outbox, 'tile', split_axis=0, concat_axis=0, tiled=True)  5.53 us
    ppermute x1, starting transfers between devices, to_previous(): lax.ppermute(cells, axis, [((i + 1) % count, i) for i in range(count)])  5.31 us
    ppermute x1, starting transfers between devices, to_next(): lax.ppermute(cells, axis, [(i, (i + 1) % count) for i in range(count)])  3.9 us
    ppermute x5, waiting for transfers between devices, swap(): lax.ppermute(cells, axis, [(i, p if 0 <= p < count else i) for i, p in en...  2.74 us
  transfers between devices with their start and end apart: 11, of which 7 were waited for; matrix products, arithmetic and copies ran while one was open for 0% of the time, Pallas kernels for 6%

profile of v5, /device:TPU:1, one launch (start us, length us, event | category | flops | bytes accessed | tf_op | source)
XLA Modules:
  0.0 78.7 jit_solution(7639936019299337126)
XLA Ops:
  0.7 0.6 copy-done.7
  1.3 0.0 copy-done.8
  1.3 0.0 copy-done.9
  1.3 0.0 copy-done.10
  1.3 0.0 copy-done.11
  1.4 1.2 %edges.1 = (f32[16,128]{1,0:T(8,128)S(1)}, f32[16,128]{1,0:T(8,128)S(1)}, f32[16,128]{1,0:T(8,128)S(1)}) custom-call(f32[3,16,128]{2,1,0:T(8,128)} %refs_1_.4, f32[16,128]{1,0:T(8,128)} %refs_1_.7, f32[3,64,128]{2,1,0:T(8,128)} %refs_3_.7, f32[64,128]{1,0:T(8,128)} %refs_2_.7, s32[4,64,128]{2,1,0:T(8,128)} %refs_3_.13, s32[1,64]{1,0:T(1,128)S(1)} %bitcast.8, ...), custom_call_target="tpu_custom_call" | custom-call | flops 1000000 | bytes 1000000 | tf_op jit(solution)/shard_map/edges/pallas_call | solution.py:575
  2.6 0.0 copy-start
  2.6 3.9 %collective-permute-start = (f32[16,128]{1,0:T(8,128)S(1)}, f32[16,128]{1,0:T(8,128)S(1)}, u32[]{:S(2)}, u32[]{:S(2)}) collective-permute-start(f32[16,128]{1,0:T(8,128)S(1)} %get-tuple-element.96), channel_id=1, source_target_pairs={{0,16},{16,32},{32,48},{48,64},{64,80},{80,96},{96,112},{112,128},... | collective-permute-start | bytes 24584 | tf_op jit(solution)/shard_map/ppermute | solution.py:589
  6.5 5.3 %collective-permute-start.1 = (f32[16,128]{1,0:T(8,128)S(1)}, f32[16,128]{1,0:T(8,128)S(1)}, u32[]{:S(2)}, u32[]{:S(2)}) collective-permute-start(f32[16,128]{1,0:T(8,128)S(1)} %get-tuple-element.97), channel_id=1, source_target_pairs={{16,0},{32,16},{48,32},{64,48},{80,64},{96,80},{112,96},{128,112},... | collective-permute-start | bytes 24584 | tf_op jit(solution)/shard_map/ppermute | solution.py:594
  11.8 4.0 %collective-permute-start.3 = (f32[16,128]{1,0:T(8,128)S(1)}, f32[16,128]{1,0:T(8,128)S(1)}, u32[]{:S(2)}, u32[]{:S(2)}) collective-permute-start(f32[16,128]{1,0:T(8,128)S(1)} %get-tuple-element.98), channel_id=1, source_target_pairs={{0,0},{1,2},{2,1},{3,4},{4,3},{5,6},{6,5},{7,8},{8,7},{9,10},{10,9... | collective-permute-start | bytes 24584 | tf_op jit(solution)/shard_map/ppermute | solution.py:611
  15.8 0.1 collective-permute-start.2
  16.0 0.0 copy-start.2
  16.0 0.0 copy-start.4
  16.0 0.0 copy-start.5
  16.0 0.8 %setup.1 = (bf16[128,128]{1,0:T(8,128)(2,1)S(1)}, bf16[64,256]{1,0:T(8,128)(2,1)S(1)}, s32[128,128]{1,0:T(8,128)S(1)}, s32[128,128]{1,0:T(8,128)S(1)}, f32[128,1...) custom-call(s32[1,64]{1,0:T(1,128)S(1)} %bitcast.9, ...), custom_call_target="tpu_custom_call" | custom-call | flops 1000000 | bytes 1000000 | tf_op jit(solution)/shard_map/setup/pallas_call | solution.py:575
  16.8 0.0 collective-permute-done.refs_6_.refs_4_
  16.9 0.0 collective-permute-done.1.refs_7_.refs_5_
  16.9 0.3 collective-permute-done.3.refs_9_.second.refs_7_
  17.1 0.0 collective-permute-done.2.refs_8_.first.refs_6_
  17.2 1.2 %send0.1 = (f32[64,128]{1,0:T(8,128)S(1)}, f32[80,128]{1,0:T(8,128)S(1)}, f32[64,128]{1,0:T(8,128)S(1)}, f32[16,128]{1,0:T(8,128)S(1)}, f32[32,128]{1,0:T(8,128)...) custom-call(s32[16,128]{1,0:T(8,128)S(1)} %get-tuple-element.95.refs, ...), custom_call_target="tpu_custom_call" | custom-call | flops 1000000 | bytes 1000000 | tf_op jit(solution)/shard_map/send0/pallas_call | solution.py:575
  18.4 6.1 %all-to-all-start = ((f32[16,16,128]{2,1,0:T(8,128)}), f32[16,16,128]{2,1,0:T(8,128)S(1)}, u32[]{:S(2)}, u32[]{:S(2)}) async-start(f32[16,16,128]{2,1,0:T(8,128)} %get-tuple-element.102), calls=%async_computation | async-start | bytes 262144 | tf_op jit(solution)/shard_map/all_to_all | solution.py:691
  24.5 0.6 near.1
  25.1 5.5 %all-to-all-done.inbox.refs_0_ = f32[16,16,128]{2,1,0:T(8,128)S(1)} async-done(((f32[16,16,128]{2,1,0:T(8,128)}), f32[16,16,128]{2,1,0:T(8,128)S(1)}, u32[]{:S(2)}, u32[]{:S(2)}) %all-to-all-start) | async-done | bytes 131104 | tf_op jit(solution)/shard_map/all_to_all | solution.py:691
  30.6 0.3 street0.1
  30.9 0.1 collective-permute-start.4
  31.0 1.0 %room0.1 = (f32[3,64,128]{2,1,0:T(8,128)S(1)}, f32[128,128]{1,0:T(8,128)S(1)}, f32[128,128]{1,0:T(8,128)S(1)}, f32[64,128]{1,0:T(8,128)S(1)}, f32[16,128]{1,0:T(8,128)S(1)}) custom-call(f32[16,16,128]{2,1,0:T(8,128)S(1)} %all-to-all-done.inbox.refs_0_, f32[8,128]{1,0:T(8,128)S(1)} %get-tuple-element.115.refs_1_, ...), custom_call_target="tpu_custom_call" | custom-call | flops 1000000 | bytes 1000000 | tf_op jit(solution)/shard_map/room0/pallas_call | solution.py:575
  32.0 0.3 collective-permute-done.4.refs_11_
  32.3 3.9 %collective-permute-start.5 = (f32[8,128]{1,0:T(8,128)S(1)}, f32[8,128]{1,0:T(8,128)S(1)}, u32[]{:S(2)}, u32[]{:S(2)}) collective-permute-start(f32[8,128]{1,0:T(8,128)S(1)} %collective-permute-done.4.refs_11_), channel_id=1, source_target_pairs={{0,1},{1,0},{2,3},{3,2},{4,5},{5,4},{6,7},{7,6},{8,9},{9,8},{10,11... | collective-permute-start | bytes 12296 | tf_op jit(solution)/shard_map/ppermute | solution.py:611
  36.2 0.8 %collective-permute-done.5.refs_12_ = f32[8,128]{1,0:T(8,128)S(1)} collective-permute-done((f32[8,128]{1,0:T(8,128)S(1)}, f32[8,128]{1,0:T(8,128)S(1)}, u32[]{:S(2)}, u32[]{:S(2)}) %collective-permute-start.5) | collective-permute-done | bytes 4128 | tf_op jit(solution)/shard_map/ppermute | solution.py:611
  37.0 0.4 send1.1
  37.5 9.0 %all_to_all.20.inbox.refs_0_ = f32[16,16,128]{2,1,0:T(8,128)S(1)} all-to-all(f32[16,16,128]{2,1,0:T(8,128)S(1)} %get-tuple-element.137), channel_id=1, replica_groups=mesh['district'=16,'tile'=16] {'tile'}, dimensions={0} | all-to-all | bytes 262144 | tf_op jit(solution)/shard_map/all_to_all | solution.py:691
  46.4 0.3 street1.1
  46.7 0.3 collective-permute-start.6
  47.1 1.0 %room1.1 = (f32[3,64,128]{2,1,0:T(8,128)S(1)}, f32[128,128]{1,0:T(8,128)S(1)}, f32[128,128]{1,0:T(8,128)S(1)}, f32[64,128]{1,0:T(8,128)S(1)}, f32[16,128]{1,0:T(8,128)S(1)}) custom-call(f32[16,16,128]{2,1,0:T(8,128)S(1)} %all_to_all.20.inbox.refs_0_, f32[8,128]{1,0:T(8,128)S(1)} %get-tuple-element.142.refs_1_, f32[3,64,128]{2,1,0:T(8,128)S(1)} %get-tuple-element.143.refs_2_, ...), custom_call_target="tpu_custom_call" | custom-call | flops 1000000 | bytes 1000000 | tf_op jit(solution)/shard_map/room1/pallas_call | solution.py:575
  48.0 0.1 collective-permute-done.6.refs_11_
  48.1 3.8 %collective-permute-start.7 = (f32[8,128]{1,0:T(8,128)S(1)}, f32[8,128]{1,0:T(8,128)S(1)}, u32[]{:S(2)}, u32[]{:S(2)}) collective-permute-start(f32[8,128]{1,0:T(8,128)S(1)} %collective-permute-done.6.refs_11_), channel_id=1, source_target_pairs={{0,1},{1,0},{2,3},{3,2},{4,5},{5,4},{6,7},{7,6},{8,9},{9,8},{10,11... | collective-permute-start | bytes 12296 | tf_op jit(solution)/shard_map/ppermute | solution.py:611
  52.0 0.8 %collective-permute-done.7.refs_12_ = f32[8,128]{1,0:T(8,128)S(1)} collective-permute-done((f32[8,128]{1,0:T(8,128)S(1)}, f32[8,128]{1,0:T(8,128)S(1)}, u32[]{:S(2)}, u32[]{:S(2)}) %collective-permute-start.7) | collective-permute-done | bytes 4128 | tf_op jit(solution)/shard_map/ppermute | solution.py:611
  52.8 0.4 send2.1
  53.2 9.0 %all_to_all.21.inbox.refs_0_ = f32[16,16,128]{2,1,0:T(8,128)S(1)} all-to-all(f32[16,16,128]{2,1,0:T(8,128)S(1)} %get-tuple-element.157), channel_id=1, replica_groups=mesh['district'=16,'tile'=16] {'tile'}, dimensions={0} | all-to-all | bytes 262144 | tf_op jit(solution)/shard_map/all_to_all | solution.py:691
  62.2 0.3 street2.1
  62.5 1.5 %collective-permute-start.8 = (f32[8,128]{1,0:T(8,128)S(1)}, f32[8,128]{1,0:T(8,128)S(1)}, u32[]{:S(2)}, u32[]{:S(2)}) collective-permute-start(f32[8,128]{1,0:T(8,128)S(1)} %get-tuple-element.161), channel_id=1, source_target_pairs={{0,1},{1,17},{2,3},{3,19},{4,5},{5,21},{6,7},{7,23},{8,9},{9,25},{... | collective-permute-start | bytes 12296 | tf_op jit(solution)/shard_map/ppermute | solution.py:605
  64.0 1.0 %room2.1 = (f32[3,64,128]{2,1,0:T(8,128)S(1)}, f32[128,128]{1,0:T(8,128)S(1)}, f32[128,128]{1,0:T(8,128)S(1)}, f32[64,128]{1,0:T(8,128)S(1)}, f32[16,128]{1,0:T(8,128)S(1)}) custom-call(f32[16,16,128]{2,1,0:T(8,128)S(1)} %all_to_all.21.inbox.refs_0_, f32[8,128]{1,0:T(8,128)S(1)} %get-tuple-element.162.refs_1_, f32[3,64,128]{2,1,0:T(8,128)S(1)} %get-tuple-element.163.refs_2_, ...), custom_call_target="tpu_custom_call" | custom-call | flops 1000000 | bytes 1000000 | tf_op jit(solution)/shard_map/room2/pallas_call | solution.py:575
  65.0 0.0 collective-permute-done.8.refs_11_
  65.0 2.7 %collective-permute-start.9 = (f32[8,128]{1,0:T(8,128)S(1)}, f32[8,128]{1,0:T(8,128)S(1)}, u32[]{:S(2)}, u32[]{:S(2)}) collective-permute-start(f32[8,128]{1,0:T(8,128)S(1)} %collective-permute-done.8.refs_11_), channel_id=1, source_target_pairs={{0,1},{1,0},{2,3},{3,2},{4,5},{5,4},{6,7},{7,6},{8,9},{9,8},{10,11... | collective-permute-start | bytes 12296 | tf_op jit(solution)/shard_map/ppermute | solution.py:611
  67.7 0.8 %collective-permute-done.9.refs_12_ = f32[8,128]{1,0:T(8,128)S(1)} collective-permute-done((f32[8,128]{1,0:T(8,128)S(1)}, f32[8,128]{1,0:T(8,128)S(1)}, u32[]{:S(2)}, u32[]{:S(2)}) %collective-permute-start.9) | collective-permute-done | bytes 4128 | tf_op jit(solution)/shard_map/ppermute | solution.py:611
  68.5 0.4 send3.1
  69.0 8.6 %all_to_all.22.inbox = f32[16,8,128]{2,1,0:T(8,128)S(1)} all-to-all(f32[16,8,128]{2,1,0:T(8,128)S(1)} %get-tuple-element.177), channel_id=1, replica_groups=mesh['district'=16,'tile'=16] {'tile'}, dimensions={0} | all-to-all | bytes 131072 | tf_op jit(solution)/shard_map/all_to_all | solution.py:691
  77.6 1.1 %final.1 = (f32[3,16,128]{2,1,0:T(8,128)}, f32[3,64,128]{2,1,0:T(8,128)}, f32[3,64,128]{2,1,0:T(8,128)}) custom-call(f32[16,8,128]{2,1,0:T(8,128)S(1)} %all_to_all.22.inbox, f32[64,128]{1,0:T(8,128)S(1)} %get-tuple-element.178.eta, f32[128,128]{1,0:T(8,128)S(1)} %get-tuple-element.179.street, bf16[64,256]{1,0:T(8,128)(2,1)S(1)} %get-tuple-element.105.row_t2, ...), custom_call_target="tpu_custom_call" | custom-call | flops 1000000 | bytes 1000000 | tf_op jit(solution)/shard_map/final/pallas_call | solution.py:575
  (19 shorter events, 0.0 us)
Async XLA Ops:
  0.6 0.7 copy-start.7
  0.6 0.7 copy-start.8
  0.7 0.7 copy-start.9
  0.7 0.7 copy-start.10
  0.7 0.7 copy-start.11
  0.7 15.2 %copy-start.6 = (f32[3,64,128]{2,1,0:T(8,128)S(1)}, f32[3,64,128]{2,1,0:T(8,128)}, u32[]{:S(2)}) copy-start(f32[3,64,128]{2,1,0:T(8,128)} %room.1) | copy-start | bytes 294916
  0.7 15.2 %copy-start.12 = (s32[1,16,2]{1,2,0:T(2,128)S(1)}, s32[1,16,2]{1,2,0:T(2,128)}, u32[]{:S(2)}) copy-start(s32[1,16,2]{1,2,0:T(2,128)} %param.21) | copy-start | bytes 388
  0.7 15.2 %copy-start.13 = (s32[1,128]{1,0:T(1,128)S(1)}, s32[1,128]{1,0:T(1,128)}, u32[]{:S(2)}) copy-start(s32[1,128]{1,0:T(1,128)} %door.1) | copy-start | bytes 1540
  1.4 14.6 %copy-start.1 = (s32[4,64,128]{2,1,0:T(8,128)S(1)}, s32[4,64,128]{2,1,0:T(8,128)}, u32[]{:S(2)}) copy-start(s32[4,64,128]{2,1,0:T(8,128)} %refs_3_.12) | copy-start | bytes 393220
  1.4 15.8 %copy-start.3 = (f32[3,64,128]{2,1,0:T(8,128)S(1)}, f32[3,64,128]{2,1,0:T(8,128)}, u32[]{:S(2)}) copy-start(f32[3,64,128]{2,1,0:T(8,128)} %refs_3_.7) | copy-start | bytes 294916
  2.6 14.6 %copy-start = (s32[4,64,128]{2,1,0:T(8,128)S(1)}, s32[4,64,128]{2,1,0:T(8,128)}, u32[]{:S(2)}) copy-start(s32[4,64,128]{2,1,0:T(8,128)} %refs_3_.13) | copy-start | bytes 393220
  2.6 14.3 %collective-permute-start = (f32[16,128]{1,0:T(8,128)S(1)}, f32[16,128]{1,0:T(8,128)S(1)}, u32[]{:S(2)}, u32[]{:S(2)}) collective-permute-start(f32[16,128]{1,0:T(8,128)S(1)} %get-tuple-element.96), channel_id=1, source_target_pairs={{0,16},{16,32},{32,48},{48,64},{64,80},{80,96},{96,112},{112,128},... | collective-permute-start | bytes 24584 | tf_op jit(solution)/shard_map/ppermute | solution.py:589
  6.5 10.4 %collective-permute-start.1 = (f32[16,128]{1,0:T(8,128)S(1)}, f32[16,128]{1,0:T(8,128)S(1)}, u32[]{:S(2)}, u32[]{:S(2)}) collective-permute-start(f32[16,128]{1,0:T(8,128)S(1)} %get-tuple-element.97), channel_id=1, source_target_pairs={{16,0},{32,16},{48,32},{64,48},{80,64},{96,80},{112,96},{128,112},... | collective-permute-start | bytes 24584 | tf_op jit(solution)/shard_map/ppermute | solution.py:594
  11.8 5.4 %collective-permute-start.3 = (f32[16,128]{1,0:T(8,128)S(1)}, f32[16,128]{1,0:T(8,128)S(1)}, u32[]{:S(2)}, u32[]{:S(2)}) collective-permute-start(f32[16,128]{1,0:T(8,128)S(1)} %get-tuple-element.98), channel_id=1, source_target_pairs={{0,0},{1,2},{2,1},{3,4},{4,3},{5,6},{6,5},{7,8},{8,7},{9,10},{10,9... | collective-permute-start | bytes 24584 | tf_op jit(solution)/shard_map/ppermute | solution.py:611
  15.8 1.3 %collective-permute-start.2 = (f32[16,128]{1,0:T(8,128)S(1)}, f32[16,128]{1,0:T(8,128)S(1)}, u32[]{:S(2)}, u32[]{:S(2)}) collective-permute-start(f32[16,128]{1,0:T(8,128)S(1)} %get-tuple-element.98), channel_id=1, source_target_pairs={{0,1},{1,0},{2,3},{3,2},{4,5},{5,4},{6,7},{7,6},{8,9},{9,8},{10,11... | collective-permute-start | bytes 24584 | tf_op jit(solution)/shard_map/ppermute | solution.py:611
  16.0 1.2 %copy-start.2 = (f32[64,128]{1,0:T(8,128)S(1)}, f32[64,128]{1,0:T(8,128)}, u32[]{:S(2)}) copy-start(f32[64,128]{1,0:T(8,128)} %refs_2_.7) | copy-start | bytes 98308
  16.0 1.2 %copy-start.4 = (f32[16,128]{1,0:T(8,128)S(1)}, f32[16,128]{1,0:T(8,128)}, u32[]{:S(2)}) copy-start(f32[16,128]{1,0:T(8,128)} %refs_1_.7) | copy-start | bytes 24580
  16.0 1.2 %copy-start.5 = (f32[3,16,128]{2,1,0:T(8,128)S(1)}, f32[3,16,128]{2,1,0:T(8,128)}, u32[]{:S(2)}) copy-start(f32[3,16,128]{2,1,0:T(8,128)} %refs_1_.4) | copy-start | bytes 73732
  18.4 12.3 %all-to-all-start = ((f32[16,16,128]{2,1,0:T(8,128)}), f32[16,16,128]{2,1,0:T(8,128)S(1)}, u32[]{:S(2)}, u32[]{:S(2)}) async-start(f32[16,16,128]{2,1,0:T(8,128)} %get-tuple-element.102), calls=%async_computation | async-start | bytes 262144 | tf_op jit(solution)/shard_map/all_to_all | solution.py:691
  30.9 1.4 %collective-permute-start.4 = (f32[8,128]{1,0:T(8,128)S(1)}, f32[8,128]{1,0:T(8,128)S(1)}, u32[]{:S(2)}, u32[]{:S(2)}) collective-permute-start(f32[8,128]{1,0:T(8,128)S(1)} %get-tuple-element.114), channel_id=1, source_target_pairs={{0,1},{1,17},{2,3},{3,19},{4,5},{5,21},{6,7},{7,23},{8,9},{9,25},{... | collective-permute-start | bytes 12296 | tf_op jit(solution)/shard_map/ppermute | solution.py:605
  32.3 4.7 %collective-permute-start.5 = (f32[8,128]{1,0:T(8,128)S(1)}, f32[8,128]{1,0:T(8,128)S(1)}, u32[]{:S(2)}, u32[]{:S(2)}) collective-permute-start(f32[8,128]{1,0:T(8,128)S(1)} %collective-permute-done.4.refs_11_), channel_id=1, source_target_pairs={{0,1},{1,0},{2,3},{3,2},{4,5},{5,4},{6,7},{7,6},{8,9},{9,8},{10,11... | collective-permute-start | bytes 12296 | tf_op jit(solution)/shard_map/ppermute | solution.py:611
  46.7 1.4 %collective-permute-start.6 = (f32[8,128]{1,0:T(8,128)S(1)}, f32[8,128]{1,0:T(8,128)S(1)}, u32[]{:S(2)}, u32[]{:S(2)}) collective-permute-start(f32[8,128]{1,0:T(8,128)S(1)} %get-tuple-element.141), channel_id=1, source_target_pairs={{0,1},{1,17},{2,3},{3,19},{4,5},{5,21},{6,7},{7,23},{8,9},{9,25},{... | collective-permute-start | bytes 12296 | tf_op jit(solution)/shard_map/ppermute | solution.py:605
  48.1 4.7 %collective-permute-start.7 = (f32[8,128]{1,0:T(8,128)S(1)}, f32[8,128]{1,0:T(8,128)S(1)}, u32[]{:S(2)}, u32[]{:S(2)}) collective-permute-start(f32[8,128]{1,0:T(8,128)S(1)} %collective-permute-done.6.refs_11_), channel_id=1, source_target_pairs={{0,1},{1,0},{2,3},{3,2},{4,5},{5,4},{6,7},{7,6},{8,9},{9,8},{10,11... | collective-permute-start | bytes 12296 | tf_op jit(solution)/shard_map/ppermute | solution.py:611
  62.5 2.5 %collective-permute-start.8 = (f32[8,128]{1,0:T(8,128)S(1)}, f32[8,128]{1,0:T(8,128)S(1)}, u32[]{:S(2)}, u32[]{:S(2)}) collective-permute-start(f32[8,128]{1,0:T(8,128)S(1)} %get-tuple-element.161), channel_id=1, source_target_pairs={{0,1},{1,17},{2,3},{3,19},{4,5},{5,21},{6,7},{7,23},{8,9},{9,25},{... | collective-permute-start | bytes 12296 | tf_op jit(solution)/shard_map/ppermute | solution.py:605
  65.0 3.5 %collective-permute-start.9 = (f32[8,128]{1,0:T(8,128)S(1)}, f32[8,128]{1,0:T(8,128)S(1)}, u32[]{:S(2)}, u32[]{:S(2)}) collective-permute-start(f32[8,128]{1,0:T(8,128)S(1)} %collective-permute-done.8.refs_11_), channel_id=1, source_target_pairs={{0,1},{1,0},{2,3},{3,2},{4,5},{5,4},{6,7},{7,6},{8,9},{9,8},{10,11... | collective-permute-start | bytes 12296 | tf_op jit(solution)/shard_map/ppermute | solution.py:611
